TPU v7x, 32 devices: a whole 2x2x4 slice. The times are simulated.
32 devices in a mesh: ctx: 16 (over z, y, x), head: 2 (over core).
Axes of the slice: x: 2, y: 2, z: 4, core: 2. Of those that a mesh axis runs over, the one named last changes fastest.
Arguments:
- queries: float32 [8192, 1024], P('ctx', 'head'), may hold values from -5 to 5
- keys: float32 [8192, 1024], P('ctx', 'head'), may hold values from -5 to 5
- values: float32 [8192, 1024], P('ctx', 'head'), may hold values from -6 to 6
- transitions: float32 [8192, 1024], P('ctx', 'head'), may hold values from -6 to 6
- betas: float32 [8, 8192], P('head', 'ctx'), may hold values from 0 to 2
- documents: int32 [8192], P('ctx'), may hold values from 0 to 7, never falling along the last dimension, each value on 1 to 2048 neighbouring positions
- out_weight: float32 [1024, 2048], P('head'), may hold values from -1.5 to 1.5
Outputs:
- output: float32 [8192, 2048], P(('ctx', 'head'))
Inputs may be any that keep to these rules, and one draw needn't show every extreme that they name: `documents`: document ids never fall along the tokens; every document holds at most 2048 tokens.
All inputs are finite; a program needn't handle non-finite values.
Results may differ from a plain program's by a relative error of at most 0.0003.
Values sent between devices are 32-bit elements; how exact they have to be, the bound alone decides.
No kernel may reach another device: no remote copies, remote signals or barrier semaphores. Data moves between devices by JAX's collectives and lax.ppermute only.
A program may use at most 320 MiB of HBM per device.

v0:
```python
import math

import jax
import jax.numpy as jnp
from jax import lax
from jax.sharding import PartitionSpec as P

BLOCK_TOKENS = 512


HIGHEST = lax.Precision.HIGHEST


def passed_along(value, axis, steps):
    count = lax.axis_size(axis)
    leading, last = (max(0, -steps), min(count, count - steps))
    return lax.ppermute(value, axis, [(source, source + steps) for source in range(leading, last)])


def contract(pattern, left_operand, right_operand):
    return jnp.einsum(pattern, left_operand, right_operand, precision=HIGHEST)


def piece_length():
    return 128


def unit_lower_inverse(lower_mat):
    lead = lower_mat.shape[:-2]
    order = lower_mat.shape[-1]
    depth = len(lead)
    inverse_blocks = jnp.ones(lead + (order, 1, 1), jnp.float32)
    size = 1
    while size < order:
        count = order // (2 * size)
        tiled = lower_mat.reshape(lead + (count, 2, size, count, 2, size))
        diagonal_tiles = jnp.diagonal(tiled, axis1=depth, axis2=depth + 3)
        lower_left = jnp.moveaxis(diagonal_tiles[..., 1, :, 0, :, :], -1, depth)
        paired = inverse_blocks.reshape(lead + (count, 2, size, size))
        upper_inverse = paired[..., 0, :, :]
        lower_inverse = paired[..., 1, :, :]
        off_block = -contract(
            "...ij,...jk->...ik",
            lower_inverse,
            contract("...ij,...jk->...ik", lower_left, upper_inverse),
        )
        top_half = jnp.concatenate([upper_inverse, jnp.zeros_like(upper_inverse)], axis=-1)
        bottom_half = jnp.concatenate([off_block, lower_inverse], axis=-1)
        inverse_blocks = jnp.concatenate([top_half, bottom_half], axis=-2)
        size = size * 2
    return inverse_blocks.reshape(lead + (order, order))


def local_parts(queries, keys, transitions, betas):
    batches, length, groups, head_size = queries.shape
    piece_size = piece_length()
    pieces = length // piece_size
    sub_shape = (batches, pieces, piece_size, groups, head_size)
    unit_dirs = transitions * lax.rsqrt(
        jnp.sum(transitions * transitions, axis=-1, keepdims=True) + 1e-06
    )
    query_sub = queries.reshape(sub_shape)
    key_sub = keys.reshape(sub_shape)
    trans_sub = unit_dirs.reshape(sub_shape)
    beta_sub = jnp.transpose(betas.reshape(batches, pieces, piece_size, groups), (0, 1, 3, 2))
    row_ids = lax.broadcasted_iota(jnp.int32, (piece_size, piece_size), 0)
    col_ids = lax.broadcasted_iota(jnp.int32, (piece_size, piece_size), 1)
    strictly = row_ids > col_ids
    within = row_ids >= col_ids
    gram_matrix = contract("bnihd,bnjhd->bnhij", trans_sub, trans_sub)
    lower_mat = jnp.eye(piece_size, dtype=jnp.float32) + jnp.where(
        strictly, beta_sub[..., :, None] * gram_matrix, 0.0
    )
    beta_keys = jnp.where(
        strictly, beta_sub[..., :, None] * contract("bnihd,bnjhd->bnhij", trans_sub, key_sub), 0.0
    )
    beta_rows = beta_sub[..., None] * jnp.transpose(trans_sub, (0, 1, 3, 2, 4))
    inverse = unit_lower_inverse(lower_mat)
    solved = contract(
        "bnhij,bnhjk->bnhik", inverse, jnp.concatenate([beta_keys, beta_rows], axis=-1)
    )
    carried = solved[..., :piece_size]
    applied = solved[..., piece_size:]
    query_dirs = jnp.where(within, contract("bnihd,bnshd->bnhis", query_sub, trans_sub), 0.0)
    own_scores = contract("bnihd,bnjhd->bnhij", query_sub, key_sub) - contract(
        "bnhis,bnhsj->bnhij", query_dirs, carried
    )
    query_hat = jnp.transpose(query_sub, (0, 1, 3, 2, 4)) - contract(
        "bnhis,bnhsd->bnhid", query_dirs, applied
    )
    key_hat = jnp.transpose(key_sub, (0, 1, 3, 2, 4)) - contract(
        "bnhsj,bnshd->bnhjd", carried, trans_sub
    )
    sub_steps = jnp.eye(head_size, dtype=jnp.float32) - contract(
        "bnshe,bnhsf->bnhef", trans_sub, applied
    )
    return (query_hat, key_hat, own_scores, sub_steps)


def block_form(query_hat, key_hat, own_scores, sub_steps):
    batches, pieces, groups, piece_size, head_size = query_hat.shape
    rows_out = []
    queries_out = []
    for query_index in range(pieces):
        current = query_hat[:, query_index]
        tile_list = [own_scores[:, query_index]]
        for key_index in range(query_index - 1, -1, -1):
            tile_list.insert(0, contract("bhid,bhjd->bhij", current, key_hat[:, key_index]))
            current = contract("bhie,bhef->bhif", current, sub_steps[:, key_index])
        if query_index < pieces - 1:
            tile_list.append(
                jnp.zeros(
                    (batches, groups, piece_size, (pieces - 1 - query_index) * piece_size),
                    jnp.float32,
                )
            )
        rows_out.append(jnp.concatenate(tile_list, axis=-1))
        queries_out.append(current)
    intra_scores = jnp.concatenate(rows_out, axis=2)
    block_queries = jnp.stack(queries_out, axis=2).reshape(
        batches, groups, pieces * piece_size, head_size
    )
    suffix = jnp.broadcast_to(
        jnp.eye(head_size, dtype=jnp.float32), (batches, groups, head_size, head_size)
    )
    keys_out = [None] * pieces
    for key_index in range(pieces - 1, -1, -1):
        keys_out[key_index] = contract("bhef,bhjf->bhje", suffix, key_hat[:, key_index])
        suffix = contract("bhef,bhfg->bheg", suffix, sub_steps[:, key_index])
    block_keys = jnp.stack(keys_out, axis=2).reshape(
        batches, groups, pieces * piece_size, head_size
    )
    return (block_queries, block_keys, intra_scores, suffix)


def absorb(softmax_state, raw_scores, allowed, value_part):
    row_peak, row_total, summed = softmax_state
    masked = jnp.where(allowed, raw_scores, -jnp.inf)
    new_peak = jnp.maximum(row_peak, jnp.max(masked, axis=-1, keepdims=True))
    factor = jnp.exp(row_peak - new_peak)
    weights = jnp.where(allowed, jnp.exp(masked - new_peak), 0.0)
    row_total = row_total * factor + jnp.sum(weights, axis=-1, keepdims=True)
    summed = summed * factor + contract("...ij,...jd->...id", weights, value_part)
    return (new_peak, row_total, summed)


def shards(queries, keys, values, transitions, betas, documents, out_weight):
    groups = betas.shape[0]
    token_rows = queries.shape[0]
    head_size = queries.shape[1] // groups
    length = BLOCK_TOKENS
    blocks = token_rows // length
    block_shape = (blocks, length, groups, head_size)
    beta_blocks = jnp.transpose(betas.reshape(groups, blocks, length), (1, 2, 0))
    parts = local_parts(
        queries.reshape(block_shape),
        keys.reshape(block_shape),
        transitions.reshape(block_shape),
        beta_blocks,
    )
    block_queries, block_keys, intra_scores, block_steps = block_form(*parts)
    value_blocks = jnp.transpose(values.reshape(block_shape), (0, 2, 1, 3))
    document_blocks = documents.reshape(blocks, length)
    doc_float = document_blocks.astype(jnp.float32)
    identity = jnp.eye(head_size, dtype=jnp.float32)
    hop_total = (blocks + 2) // blocks
    received = []
    suffixes = [None] * blocks
    running = jnp.broadcast_to(identity, (groups, head_size, head_size))
    suffixes[0] = running
    running = contract("hef,hfg->heg", running, block_steps[0])
    carry_keys = jnp.stack([contract("hef,hjf->hje", suffixes[0], block_keys[0])], axis=0)
    carry_values = value_blocks
    carry_docs = doc_float
    for hop_index in range(1, hop_total + 1):
        key_count = min(blocks, 3 - (hop_index - 1) * blocks)
        arrived = passed_along((carry_keys, carry_values, carry_docs), "ctx", 1)
        received.insert(
            0,
            (
                arrived[0],
                arrived[1],
                arrived[2],
                jnp.broadcast_to(identity, (key_count, groups, head_size, head_size)),
            ),
        )
        if hop_index < hop_total:
            carry_keys = contract("hef,bhjf->bhje", running, arrived[0])
            carry_values = arrived[1]
            carry_docs = arrived[2]
    ext_keys = jnp.concatenate([item[0] for item in received] + [block_keys], axis=0)
    ext_values = jnp.concatenate([item[1] for item in received] + [value_blocks], axis=0)
    ext_docs = jnp.concatenate([item[2] for item in received] + [doc_float], axis=0)
    ext_steps = jnp.concatenate([item[3] for item in received] + [block_steps], axis=0)
    score_scale = 1.0 / math.sqrt(head_size)
    causal = lax.broadcasted_iota(jnp.int32, (length, length), 0) >= lax.broadcasted_iota(
        jnp.int32, (length, length), 1
    )
    own_allowed = (document_blocks[:, None, :, None] == document_blocks[:, None, None, :]) & causal
    softmax_state = (
        jnp.full((blocks, groups, length, 1), -jnp.inf, jnp.float32),
        jnp.zeros((blocks, groups, length, 1), jnp.float32),
        jnp.zeros((blocks, groups, length, head_size), jnp.float32),
    )
    softmax_state = absorb(softmax_state, intra_scores * score_scale, own_allowed, value_blocks)
    current = block_queries
    anchor = lax.axis_index("ctx") * blocks
    block_ids = lax.iota(jnp.int32, blocks)
    for distance in range(1, 4):
        lowest = 3 - distance
        if distance > 1:
            current = contract(
                "bhie,bhef->bhif", current, ext_steps[lowest + 1 : lowest + 1 + blocks]
            )
        valid_block = anchor + block_ids - distance >= 0
        allowed = (
            doc_float[:, None, :, None] == ext_docs[lowest : lowest + blocks][:, None, None, :]
        ) & valid_block[:, None, None, None]
        raw_scores = (
            contract("bhid,bhjd->bhij", current, ext_keys[lowest : lowest + blocks]) * score_scale
        )
        softmax_state = absorb(
            softmax_state, raw_scores, allowed, ext_values[lowest : lowest + blocks]
        )
    attended = softmax_state[2] / softmax_state[1]
    flattened = jnp.transpose(attended, (0, 2, 1, 3)).reshape(token_rows, groups * head_size)
    share_rows = token_rows // lax.axis_size("head")
    partial_out = jnp.dot(
        flattened, out_weight, precision=HIGHEST, preferred_element_type=jnp.float32
    )
    full_sum = lax.psum(partial_out, "head")
    return lax.dynamic_slice_in_dim(full_sum, lax.axis_index("head") * share_rows, share_rows, 0)


def solution(mesh):
    return jax.shard_map(
        shards,
        mesh=mesh,
        in_specs=(
            P("ctx", "head"),
            P("ctx", "head"),
            P("ctx", "head"),
            P("ctx", "head"),
            P("head", "ctx"),
            P("ctx"),
            P("head", None),
        ),
        out_specs=P(("ctx", "head"), None),
        check_vma=False,
    )
```

profile of v0, /device:TPU:0, one launch (start us, length us, event | category | flops | bytes accessed | tf_op | source)
XLA Modules:
  0.0 659.3 jit_solution(8311878118716486122)
XLA Ops:
  13.3 26.3 %copy.387 = f32[4,4,128,128]{1,3,2,0:T(8,128)} copy(f32[4,4,128,128]{2,3,1,0:T(8,128)S(1)} %fusion.52) | data formatting | bytes 2097152 | tf_op jit(solution)/shard_map/add | solution.py:71
  39.6 53.1 %reshape.1069 = f32[1,4,4,16,2,4,16,2,4]{5,4,3,8,7,6,2,1,0:T(2,128)} reshape(f32[4,4,128,128]{2,3,1,0:T(8,128)S(1)} %fusion.52) | data formatting | bytes 2097152 | tf_op jit(solution)/shard_map/reshape | solution.py:36
  92.7 26.6 %reshape.966 = f32[1,4,4,8,2,8,8,2,8]{5,4,3,8,7,6,2,1,0:T(2,128)} reshape(f32[4,4,128,128]{2,3,1,0:T(8,128)S(1)} %fusion.52) | data formatting | bytes 2097152 | tf_op jit(solution)/shard_map/reshape | solution.py:36
  119.3 12.1 %reshape.971 = f32[1,4,4,4,2,16,4,2,16]{5,4,3,8,7,6,2,1,0:T(2,128)} reshape(f32[4,4,128,128]{2,3,1,0:T(8,128)S(1)} %fusion.52) | data formatting | bytes 2097152 | tf_op jit(solution)/shard_map/reshape | solution.py:36
  131.4 4.6 reshape.976
  136.1 2.5 reshape.1011
  139.9 2.5 reshape.949
  143.8 38.3 %copy.514 = f32[1,4,4,64,2,1,64,2,1]{2,1,6,3,7,4,8,5,0:T(4,128)} copy(f32[1,4,4,64,2,1,64,2,1]{2,7,6,4,3,1,8,5,0:T(2,128)} %bitcast.451) | data formatting | bytes 2097152 | tf_op jit(solution)/shard_map/reshape | solution.py:36
  182.1 1.9 gather_fusion
  185.1 2.1 copy.474
  187.3 38.3 %copy.513 = f32[1,4,4,32,2,2,32,2,2]{2,1,6,3,8,7,5,4,0:T(4,128)} copy(f32[1,4,4,32,2,2,32,2,2]{2,8,7,6,5,4,3,1,0:T(2,128)} %bitcast.452) | data formatting | bytes 2097152 | tf_op jit(solution)/shard_map/reshape | solution.py:36
  225.6 2.3 gather_fusion.1
  227.9 8.4 %copy.395 = f32[32,4,4,2,2,2,2]{6,4,0,2,1,5,3:T(2,128)} copy(f32[32,4,4,2,2,2,2]{2,1,6,5,4,3,0:T(4,128)S(1)} %gather_fusion.1) | data formatting | bytes 65536 | tf_op jit(solution)/shard_map/jit(diagonal)/gather | solution.py:37
  236.4 2.5 copy.475
  238.9 4.5 fusion.121
  243.4 3.5 fusion.71
  249.1 104.7 %copy.400 = f32[1,4,4,16,2,4,16,2,4]{8,5,6,3,7,4,2,1,0:T(4,128)} copy(f32[1,4,4,16,2,4,16,2,4]{5,4,3,8,7,6,2,1,0:T(2,128)} %reshape.1069) | data formatting | bytes 2097152 | tf_op jit(solution)/shard_map/reshape | solution.py:36
  353.8 4.5 gather_fusion.2
  358.3 2.2 copy.518
  361.5 1.9 fusion.109
  364.4 2.7 fusion.70
  367.1 25.7 %copy.404 = f32[1,4,4,8,2,8,8,2,8]{8,5,6,3,7,4,2,1,0:T(8,128)} copy(f32[1,4,4,8,2,8,8,2,8]{5,4,3,8,7,6,2,1,0:T(2,128)} %reshape.966) | data formatting | bytes 2097152 | tf_op jit(solution)/shard_map/reshape | solution.py:36
  392.8 6.6 %gather_fusion.3 = f32[8,4,4,2,8,2,8]{6,4,5,3,2,1,0:T(8,128)S(1)} fusion(f32[4,4,2,8,2,8,8,8]{5,3,7,6,4,2,1,0:T(8,128)} %bitcast.457, s32[8]{0:T(128)S(1)} %or_bitcast_fusion.2), kind=kCustom, calls=%fused_computation.3 | custom fusion | bytes 262208 | tf_op jit(solution)/shard_map/jit(diagonal)/gather | solution.py:37
  405.1 13.2 %copy.408 = f32[1,4,4,4,2,16,4,2,16]{8,5,6,3,7,4,2,1,0:T(8,128)} copy(f32[1,4,4,4,2,16,4,2,16]{5,4,3,8,7,6,2,1,0:T(2,128)} %reshape.971) | data formatting | bytes 2097152 | tf_op jit(solution)/shard_map/reshape | solution.py:36
  418.3 4.1 gather_fusion.4
  427.2 7.6 %copy.412 = f32[1,4,4,2,2,32,2,2,32]{8,5,6,3,7,4,2,1,0:T(8,128)} copy(f32[1,4,4,2,2,32,2,2,32]{5,4,3,8,7,6,2,1,0:T(2,128)} %reshape.976) | data formatting | bytes 2097152 | tf_op jit(solution)/shard_map/reshape | solution.py:36
  434.8 2.9 gather_fusion.5
  446.4 2.1 fusion.49
  449.1 3.8 fusion.45
  452.8 1.8 fusion.46
  454.7 2.0 fusion.57
  461.6 2.0 convolution_bitcast_fusion.2
  463.7 5.8 collective-permute-start.1
  469.5 2.5 collective-permute-start
  471.9 2.5 copy.431
  474.5 4.4 collective-permute-start.2
  478.9 2.6 reshape.948
  481.4 2.5 reshape_reshape.6
  483.9 3.2 fusion.51
  487.2 3.3 fusion.56
  495.2 2.3 fusion.92
  501.8 2.3 fusion.47
  505.8 3.5 fusion.173
  509.3 2.3 convolution_bitcast_fusion.1
  511.6 2.5 collective-permute-start.4
  518.0 3.3 collective-permute-start.3
  521.4 4.4 collective-permute-start.5
  526.8 10.9 %collective-permute-done.3 = f32[1,512]{1,0:T(1,128)S(1)} collective-permute-done((f32[1,512]{1,0:T(1,128)S(1)}, f32[1,512]{1,0:T(1,128)S(1)}, u32[]{:S(2)}, u32[]{:S(2)}) %collective-permute-start.3) | collective-permute-done | bytes 2080 | tf_op jit(solution)/shard_map/ppermute | solution.py:17
  537.7 4.4 collective-permute-start.6
  543.1 2.1 convolution_bitcast_fusion
  545.2 5.3 collective-permute-start.7
  551.6 8.7 %collective-permute-done.6 = f32[1,512]{1,0:T(1,128)S(1)} collective-permute-done((f32[1,512]{1,0:T(1,128)S(1)}, f32[1,512]{1,0:T(1,128)S(1)}, u32[]{:S(2)}, u32[]{:S(2)}) %collective-permute-start.6) | collective-permute-done | bytes 2080 | tf_op jit(solution)/shard_map/ppermute | solution.py:17
  560.9 5.1 fusion.13
  566.0 4.6 collective-permute-start.8
  570.7 3.9 fusion.14
  574.6 8.2 %collective-permute-done.7 = f32[1,4,512,128]{3,2,1,0:T(8,128)} collective-permute-done((f32[1,4,512,128]{3,2,1,0:T(8,128)}, f32[1,4,512,128]{3,2,1,0:T(8,128)}, u32[]{:S(2)}, u32[]{:S(2)}) %collective-permute-start.7) | collective-permute-done | bytes 1048608 | tf_op jit(solution)/shard_map/ppermute | solution.py:17
  582.8 5.1 fusion.15
  591.6 5.1 fusion.61
  596.6 4.7 fusion.64
  601.4 4.7 fusion.65
  606.1 3.6 fusion.96
  609.7 8.6 %fusion.178 = f32[512,2048]{1,0:T(8,128)} fusion(f32[512,512]{0,1:T(8,128)S(1)} %bitcast.475, f32[512,2048]{1,0:T(8,128)S(1)} %copy-done.8), kind=kOutput, calls=%fused_computation.295 | convolution fusion | flops 6442450944 | bytes 9437184 | tf_op jit(solution)/shard_map/dot_general | solution.py:228
  618.3 30.7 %all-reduce.10.cloned.1.call-done = f32[512,2048]{1,0:T(8,128)} async-done(((f32[512,2048]{1,0:T(8,128)}), f32[512,2048]{1,0:T(8,128)}) %all-reduce.10.cloned.1.call-update) | async-done | bytes 4194320 | tf_op jit(solution)/shard_map/psum | solution.py:231
  649.1 3.1 constant_dynamic-slice_fusion
  (169 shorter events, 60.8 us)
Async XLA Ops:
  6.5 642.5 %all-reduce.10.cloned.1.call-start = ((), (), s32[]{:S(2)}) async-start(), calls=%async_computation | async-start | bytes 8388608 | tf_op jit(solution)/shard_map/psum | solution.py:231
  8.3 3.1 copy-start.30
  131.4 7.2 %copy-start = (f32[512,512]{1,0:T(8,128)S(1)}, f32[512,512]{1,0:T(8,128)}, u32[]{:S(2)}) copy-start(f32[512,512]{1,0:T(8,128)} %param.10) | copy-start | bytes 3145732
  138.6 3.8 copy-start.11
  143.8 40.5 %copy-start.32 = (f32[1,4,4,64,1,2]{3,2,1,5,4,0:T(4,128)S(1)}, f32[1,4,4,64,1,2]{3,2,1,5,4,0:T(4,128)}, u32[]{:S(2)}) copy-start(f32[1,4,4,64,1,2]{3,2,1,5,4,0:T(4,128)} %constant.40.clone.1) | copy-start | bytes 24580
  399.4 1.0 copy-start.18
  399.4 1.2 copy-start.19
  399.4 1.3 copy-start.20
  422.4 1.0 copy-start.16
  422.4 1.2 copy-start.21
  422.4 1.3 copy-start.22
  437.7 1.0 copy-start.17
  437.7 1.2 copy-start.23
  437.7 1.3 copy-start.24
  442.5 3.9 copy-start.5
  442.8 5.7 copy-start.12
  449.0 5.6 copy-start.13
  454.7 6.1 copy-start.1
  456.7 4.9 copy-start.3
  459.4 10.0 %copy-start.31 = (s32[512]{0:T(512)S(1)}, s32[512]{0:T(512)}, u32[]{:S(2)}) copy-start(s32[512]{0:T(512)} %param.12) | copy-start | bytes 6148
  463.7 45.7 %collective-permute-start.1 = (f32[1,4,512,128]{3,2,1,0:T(8,128)}, f32[1,4,512,128]{3,2,1,0:T(8,128)}, u32[]{:S(2)}, u32[]{:S(2)}) collective-permute-start(f32[1,4,512,128]{3,2,1,0:T(8,128)} %convolution_bitcast_fusion.2), channel_id=1, source_target_pairs={{0,2},{2,4},{4,6},{6,8},{8,10},{10,12},{12,14},{14,16},{16,18},{18... | collective-permute-start | bytes 3145736 | tf_op jit(solution)/shard_map/ppermute | solution.py:17
  469.5 48.6 %collective-permute-start = (f32[1,512]{1,0:T(1,128)S(1)}, f32[1,512]{1,0:T(1,128)S(1)}, u32[]{:S(2)}, u32[]{:S(2)}) collective-permute-start(f32[1,512]{1,0:T(1,128)S(1)} %bitcast.495), channel_id=1, source_target_pairs={{0,2},{2,4},{4,6},{6,8},{8,10},{10,12},{12,14},{14,16},{16,18},{18... | collective-permute-start | bytes 6152 | tf_op jit(solution)/shard_map/ppermute | solution.py:17
  474.5 46.9 %collective-permute-start.2 = (f32[1,4,512,128]{2,3,1,0:T(8,128)}, f32[1,4,512,128]{2,3,1,0:T(8,128)}, u32[]{:S(2)}, u32[]{:S(2)}) collective-permute-start(f32[1,4,512,128]{2,3,1,0:T(8,128)} %bitcast.483), channel_id=1, source_target_pairs={{0,2},{2,4},{4,6},{6,8},{8,10},{10,12},{12,14},{14,16},{16,18},{18... | collective-permute-start | bytes 3145736 | tf_op jit(solution)/shard_map/ppermute | solution.py:17
  483.9 6.5 copy-start.4
  483.9 7.2 %copy-start.2 = (f32[1,4,4,128,128]{3,4,2,1,0:T(8,128)S(1)}, f32[1,4,4,128,128]{3,4,2,1,0:T(8,128)}, u32[]{:S(2)}) copy-start(f32[1,4,4,128,128]{3,4,2,1,0:T(8,128)} %copy-done.1) | copy-start | bytes 3145732
  487.2 8.0 %copy-start.6 = (f32[4,128,4,128]{3,2,1,0:T(4,128)S(1)}, f32[4,128,4,128]{3,2,1,0:T(4,128)}, u32[]{:S(2)}) copy-start(f32[4,128,4,128]{3,2,1,0:T(4,128)} %reshape.949) | copy-start | bytes 3145732
  487.2 8.0 %copy-start.7 = (f32[4,128,4,128]{3,2,1,0:T(4,128)S(1)}, f32[4,128,4,128]{3,2,1,0:T(4,128)}, u32[]{:S(2)}) copy-start(f32[4,128,4,128]{3,2,1,0:T(4,128)} %reshape.948) | copy-start | bytes 3145732
  497.7 18.4 %copy-start.14 = (pred[512,512]{0,1:T(8,128)(4,1)}, pred[512,512]{0,1:T(8,128)(4,1)S(1)}, u32[]{:S(2)}) copy-start(pred[512,512]{0,1:T(8,128)(4,1)S(1)} %fusion.90) | copy-start | bytes 786436
  511.6 30.5 %collective-permute-start.4 = (f32[1,4,512,128]{3,2,1,0:T(8,128)S(1)}, f32[1,4,512,128]{3,2,1,0:T(8,128)S(1)}, u32[]{:S(2)}, u32[]{:S(2)}) collective-permute-start(f32[1,4,512,128]{3,2,1,0:T(8,128)S(1)} %convolution_bitcast_fusion.1), channel_id=1, source_target_pairs={{0,2},{2,4},{4,6},{6,8},{8,10},{10,12},{12,14},{14,16},{16,18},{18... | collective-permute-start | bytes 3145736 | tf_op jit(solution)/shard_map/ppermute | solution.py:17
  518.0 19.7 %collective-permute-start.3 = (f32[1,512]{1,0:T(1,128)S(1)}, f32[1,512]{1,0:T(1,128)S(1)}, u32[]{:S(2)}, u32[]{:S(2)}) collective-permute-start(f32[1,512]{1,0:T(1,128)S(1)} %collective-permute-done), channel_id=1, source_target_pairs={{0,2},{2,4},{4,6},{6,8},{8,10},{10,12},{12,14},{14,16},{16,18},{18... | collective-permute-start | bytes 6152 | tf_op jit(solution)/shard_map/ppermute | solution.py:17
  521.4 44.6 %collective-permute-start.5 = (f32[1,4,512,128]{2,3,1,0:T(8,128)}, f32[1,4,512,128]{2,3,1,0:T(8,128)}, u32[]{:S(2)}, u32[]{:S(2)}) collective-permute-start(f32[1,4,512,128]{2,3,1,0:T(8,128)} %collective-permute-done.2), channel_id=1, source_target_pairs={{0,2},{2,4},{4,6},{6,8},{8,10},{10,12},{12,14},{14,16},{16,18},{18... | collective-permute-start | bytes 3145736 | tf_op jit(solution)/shard_map/ppermute | solution.py:17
  537.7 22.6 %collective-permute-start.6 = (f32[1,512]{1,0:T(1,128)S(1)}, f32[1,512]{1,0:T(1,128)S(1)}, u32[]{:S(2)}, u32[]{:S(2)}) collective-permute-start(f32[1,512]{1,0:T(1,128)S(1)} %collective-permute-done.3), channel_id=1, source_target_pairs={{0,2},{2,4},{4,6},{6,8},{8,10},{10,12},{12,14},{14,16},{16,18},{18... | collective-permute-start | bytes 6152 | tf_op jit(solution)/shard_map/ppermute | solution.py:17
  542.1 1.0 copy-start.9
  545.2 37.6 %collective-permute-start.7 = (f32[1,4,512,128]{3,2,1,0:T(8,128)}, f32[1,4,512,128]{3,2,1,0:T(8,128)}, u32[]{:S(2)}, u32[]{:S(2)}) collective-permute-start(f32[1,4,512,128]{3,2,1,0:T(8,128)} %convolution_bitcast_fusion), channel_id=1, source_target_pairs={{0,2},{2,4},{4,6},{6,8},{8,10},{10,12},{12,14},{14,16},{16,18},{18... | collective-permute-start | bytes 3145736 | tf_op jit(solution)/shard_map/ppermute | solution.py:17
  551.6 19.1 %copy-start.10 = (f32[1,4,512,128]{3,2,1,0:T(8,128)S(1)}, f32[1,4,512,128]{3,2,1,0:T(8,128)}, u32[]{:S(2)}) copy-start(f32[1,4,512,128]{3,2,1,0:T(8,128)} %copy-done.9) | copy-start | bytes 3145732
  566.0 40.1 %collective-permute-start.8 = (f32[1,4,512,128]{2,3,1,0:T(8,128)}, f32[1,4,512,128]{2,3,1,0:T(8,128)S(1)}, u32[]{:S(2)}, u32[]{:S(2)}) collective-permute-start(f32[1,4,512,128]{2,3,1,0:T(8,128)} %collective-permute-done.5), channel_id=1, source_target_pairs={{0,2},{2,4},{4,6},{6,8},{8,10},{10,12},{12,14},{14,16},{16,18},{18... | collective-permute-start | bytes 3145736 | tf_op jit(solution)/shard_map/ppermute | solution.py:17
  589.0 2.2 copy-start.15
  589.0 2.2 copy-start.25
  589.0 2.2 copy-start.26
  589.0 2.2 copy-start.27
  589.0 2.2 copy-start.28
  589.0 2.5 copy-start.29
  606.1 3.6 copy-start.8
Sparse Core Ops, SparseCore 0:
  618.4 30.5 all-reduce.9
where the time goes:
time: 665 us; the launch traced here: 659 us
  local copies, waits for them, and re-layouts  426 us (64%)
  matrix products  107 us (16%)
  waiting for transfers between devices  58.5 us (9%)
  starting transfers between devices  37.2 us (6%)
  other arithmetic  16.4 us (2%)
  between operations  14.8 us (2%)
    reshape x10, local copies, waits for them, and re-layouts, unit_lower_inverse(): tiled = lower_mat.reshape(lead + (count, 2, size, count, 2, size))  324 us
    dot_general x54, matrix products, contract(): return jnp.einsum(pattern, left_operand, right_operand, precision=HIGHEST)  98 us
    ppermute x9, starting transfers between devices, passed_along(): lax.ppermute(value, axis, [(source, source + steps) for source in range(l...  37.2 us
    gather x13, local copies, waits for them, and re-layouts, unit_lower_inverse(): diagonal_tiles = jnp.diagonal(tiled, axis1=depth, axis2=depth + 3)  36.4 us
    psum x1, waiting for transfers between devices, shards(): full_sum = lax.psum(partial_out, 'head')  30.7 us
    ppermute x9, waiting for transfers between devices, passed_along(): lax.ppermute(value, axis, [(source, source + steps) for source in range(l...  27.8 us
    add x1, local copies, waits for them, and re-layouts, local_parts(): jnp.eye(piece_size, dtype=jnp.float32)  26.3 us
    unnamed x72, local copies, waits for them, and re-layouts  14.1 us
  transfers between devices with their start and end apart: 10, of which 4 were waited for; matrix products, arithmetic and copies ran while one was open for 11% of the time, Pallas kernels for 0%

commit v1 on v0

v1 whole, which is shorter than its diff:
```python
import functools
import math

import jax
import jax.numpy as jnp
from jax import lax
from jax.experimental import pallas as pl
from jax.experimental.pallas import tpu as pltpu
from jax.sharding import PartitionSpec as P

BLOCK_TOKENS = 512
PIECE = 128
SEED = 16
BATCH = 2
ROWS = 256
GROUPS = 2
FAR = -1e30
VMEM_BYTES = 56 * 2**20
COST = 1.15e9


def lasting(microseconds):
    return pl.CostEstimate(flops=int(microseconds * COST), bytes_accessed=1000, transcendentals=0)


def split(value):
    high = value.astype(jnp.bfloat16)
    return high, (value - high.astype(jnp.float32)).astype(jnp.bfloat16)


def product(left, right, left_dim, right_dim):
    left_high, left_low = split(left)
    right_high, right_low = split(right)
    return lax.dot_general(
        jnp.concatenate([left_high, left_low, left_high], axis=left_dim),
        jnp.concatenate([right_high, right_high, right_low], axis=right_dim),
        (((left_dim,), (right_dim,)), ((), ())),
        preferred_element_type=jnp.float32,
    )


def mm(left, right):
    return product(left, right, 1, 0)


def mm_nt(left, right):
    return product(left, right, 1, 1)


def mm_tn(left, right):
    return product(left, right, 0, 0)


def columns_of(row):
    parts = [
        jnp.broadcast_to(row[:, i : i + PIECE], (PIECE, PIECE)).T
        for i in range(0, row.shape[1], PIECE)
    ]
    return jnp.concatenate(parts, axis=0) if len(parts) > 1 else parts[0]


def unit_lower_inverses(stricts):
    order = stricts[0].shape[0]
    blocks = order // SEED
    rows = lax.broadcasted_iota(jnp.int32, (order, order), 0)
    cols = lax.broadcasted_iota(jnp.int32, (order, order), 1)
    diagonal = rows // SEED == cols // SEED
    packed = []
    for strict in stricts:
        kept = jnp.where(diagonal, strict, 0.0)
        total = kept[:SEED]
        for block in range(1, blocks):
            total = total + kept[block * SEED : (block + 1) * SEED]
        packed.append(total)
    packed = jnp.concatenate(packed, axis=0)
    lane = lax.broadcasted_iota(jnp.int32, packed.shape, 1)
    row = lax.broadcasted_iota(jnp.int32, packed.shape, 0)
    shape = (len(stricts), SEED, order)
    inverse = jnp.where(lane % SEED == row % SEED, 1.0, 0.0).reshape(shape)
    first = lane - lane % SEED
    for k in range(SEED - 1):
        column = jnp.take_along_axis(packed, first + k, axis=1, mode="promise_in_bounds")
        inverse = inverse - column.reshape(shape) * inverse[:, k : k + 1, :]
    inverses = [
        jnp.where(diagonal, jnp.concatenate([inverse[i]] * blocks, axis=0), 0.0)
        for i in range(len(stricts))
    ]
    size = SEED
    while size < order:
        below = (rows // size == cols // size + 1) & (rows // (2 * size) == cols // (2 * size))
        right = [mm(jnp.where(below, s, 0.0), x) for s, x in zip(stricts, inverses)]
        inverses = [x - mm(x, r) for x, r in zip(inverses, right)]
        size *= 2
    return inverses


def stacked_values(values):
    return jnp.concatenate(split(values), axis=1)


def softmax_part(scores, stacked):
    rows, dh = scores.shape[0], stacked.shape[1] // 2
    peak = jnp.max(scores, axis=-1, keepdims=True)
    weights = jnp.exp2(scores - peak)
    total = jnp.sum(weights, axis=-1, keepdims=True)
    summed = lax.dot_general(
        jnp.concatenate(split(weights), axis=0), stacked, (((1,), (0,)), ((), ())),
        preferred_element_type=jnp.float32,
    )
    summed = summed[:rows] + summed[rows:]
    return (summed[:, :dh] + summed[:, dh:]) / total, peak + jnp.log2(total)


def stacked_keys(keys):
    high, low = split(keys)
    return jnp.concatenate([high, high, low], axis=1).T


def stacked_queries(queries):
    high, low = split(queries)
    return jnp.concatenate([high, low, high], axis=1)


def scored(queries, keys):
    return lax.dot_general(queries, keys, (((1,), (0,)), ((), ())), preferred_element_type=jnp.float32)


def prepare_kernel(q_ref, k_ref, v_ref, w_ref, beta_ref, doc_ref, qo_ref, ko_ref, st_ref, o_ref, lse_ref, *, scale):
    batch, dh, _ = st_ref.shape
    length = q_ref.shape[0]
    pieces = length // PIECE
    rows = lax.broadcasted_iota(jnp.int32, (PIECE, PIECE), 0)
    cols = lax.broadcasted_iota(jnp.int32, (PIECE, PIECE), 1)
    identity = jnp.where(rows == cols, 1.0, 0.0)
    spans = [slice(i * PIECE, (i + 1) * PIECE) for i in range(pieces)]
    heads = [slice(h * dh, (h + 1) * dh) for h in range(batch)]
    where = [(head, span) for head in heads for span in spans]
    directions = [w_ref[span, head] for head, span in where]
    units = [w * lax.rsqrt(jnp.sum(w * w, axis=-1, keepdims=True) + 1e-06) for w in directions]
    first = pl.program_id(0) * batch
    beta_rows = [beta_ref[pl.ds(first + h, 1), :] for h in range(batch)]
    betas = [columns_of(row[:, span]) for row in beta_rows for span in spans]
    grams = [
        mm_nt(jnp.concatenate([t, q_ref[span, head]], axis=0), jnp.concatenate([t, k_ref[span, head]], axis=0))
        for t, (head, span) in zip(units, where)
    ]
    inverses = unit_lower_inverses(
        [jnp.where(rows > cols, beta * g[:PIECE, :PIECE], 0.0) for beta, g in zip(betas, grams)]
    )
    solved = [
        mm(x, jnp.concatenate([jnp.where(rows > cols, beta * g[:PIECE, PIECE:], 0.0), beta * t], axis=1))
        for x, beta, g, t in zip(inverses, betas, grams, units)
    ]
    change = [mm(jnp.where(rows >= cols, g[PIECE:, :PIECE], 0.0), s) for g, s in zip(grams, solved)]
    carried = [mm_tn(s, t) for s, t in zip(solved, units)]

    def by_head(flat):
        return [flat[h * pieces : (h + 1) * pieces] for h in range(batch)]

    own = by_head([g[PIECE:, PIECE:] - c[:, :PIECE] for g, c in zip(grams, change)])
    q_hat = by_head([q_ref[span, head] - c[:, PIECE:] for (head, span), c in zip(where, change)])
    k_hat = by_head([k_ref[span, head] - c[:PIECE] for (head, span), c in zip(where, carried)])
    st = by_head([identity - c[PIECE:] for c in carried])
    tiles = [[[None] * pieces for _ in range(pieces)] for _ in range(batch)]
    for h in range(batch):
        for i in range(pieces):
            tiles[h][i][i] = own[h][i]
    current = [list(q) for q in q_hat]
    suffix = [[None] * pieces for _ in range(batch)]
    for back in range(1, pieces):
        for h in range(batch):
            for i in range(back, pieces):
                tiles[h][i][i - back] = mm_nt(current[h][i], k_hat[h][i - back])
                current[h][i] = mm_nt(current[h][i], st[h][i - back])
            j = pieces - back
            suffix[h][j - 1] = st[h][j] if back == 1 else mm(st[h][j], suffix[h][j])
    for h in range(batch):
        for i in range(pieces):
            qo_ref[h, spans[i], :] = current[h][i]
            ko_ref[h, spans[i], :] = k_hat[h][i] if i == pieces - 1 else mm(k_hat[h][i], suffix[h][i])
        st_ref[h] = mm(st[h][0], suffix[h][0]) if pieces > 1 else st[h][0]
    doc_row = (doc_ref[...].reshape(1, length) + 1).astype(jnp.float32)
    doc_col = columns_of(doc_row)
    doc_lines = [doc_row[:, span] for span in spans]
    doc_lines.append(jnp.zeros((qo_ref.shape[1] - length - pieces, dh), jnp.float32))
    doc_lines = jnp.concatenate(doc_lines, axis=0)
    for h in range(batch):
        qo_ref[h, length:, :] = doc_lines
        ko_ref[h, length:, :] = doc_lines
    stacked = [stacked_values(v_ref[:, head]) for head in heads]
    for i in range(pieces):
        for h in range(batch):
            masked = []
            for j in range(i + 1):
                same = doc_col[spans[i]] == doc_row[:, spans[j]]
                if i == j:
                    same = same & (rows >= cols)
                masked.append(jnp.where(same, tiles[h][i][j] * scale, FAR))
            out, lse = softmax_part(
                jnp.concatenate(masked, axis=1) if i else masked[0], stacked[h][: (i + 1) * PIECE]
            )
            o_ref[h, spans[i], :] = out
            lse_ref[h, spans[i], :] = jnp.broadcast_to(lse, (PIECE, PIECE))


def message_rows(length):
    return length + (length // PIECE + 7) // 8 * 8


def prepare(queries, keys, values, transitions, betas, documents, scale):
    length = queries.shape[0]
    heads = betas.shape[0]
    dh = queries.shape[1] // heads
    rows = message_rows(length)
    column = pl.BlockSpec((length, BATCH * dh), lambda h: (0, h))
    head = pl.BlockSpec((BATCH, length, dh), lambda h: (h, 0, 0))
    message = pl.BlockSpec((BATCH, rows, dh), lambda h: (h, 0, 0))
    f32 = jnp.float32
    return pl.pallas_call(
        functools.partial(prepare_kernel, scale=scale),
        grid=(heads // BATCH,),
        in_specs=[column] * 4
        + [
            pl.BlockSpec((heads, length), lambda h: (0, 0)),
            pl.BlockSpec((length,), lambda h: (0,)),
        ],
        out_specs=[message, message, pl.BlockSpec((BATCH, dh, dh), lambda h: (h, 0, 0)), head, head],
        out_shape=[
            jax.ShapeDtypeStruct((heads, rows, dh), f32),
            jax.ShapeDtypeStruct((heads, rows, dh), f32),
            jax.ShapeDtypeStruct((heads, dh, dh), f32),
            jax.ShapeDtypeStruct((heads, length, dh), f32),
            jax.ShapeDtypeStruct((heads, length, dh), f32),
        ],
        compiler_params=pltpu.CompilerParams(vmem_limit_bytes=VMEM_BYTES),
        name="prepare",
        cost_estimate=lasting(13),
    )(queries, keys, values, transitions, betas, documents)


def steps_kernel(place_ref, own_ref, near_ref, out_ref):
    even = lax.rem(place_ref[0], 2) == 0
    for h in range(own_ref.shape[0]):
        near = near_ref[h]
        out_ref[h] = jnp.where(even, near, mm(near, own_ref[h]))


def joined_steps(place, own, near):
    whole = pl.BlockSpec(own.shape, lambda i, p: (0, 0, 0))
    return pl.pallas_call(
        steps_kernel,
        grid_spec=pltpu.PrefetchScalarGridSpec(
            num_scalar_prefetch=1, grid=(1,), in_specs=[whole, whole], out_specs=whole
        ),
        out_shape=jax.ShapeDtypeStruct(own.shape, jnp.float32),
        compiler_params=pltpu.CompilerParams(vmem_limit_bytes=VMEM_BYTES),
        name="joined_steps",
        cost_estimate=lasting(2),
    )(place, own, near)


def doc_line(ref, length, valid):
    line = jnp.concatenate([ref[0, length + i : length + i + 1, :] for i in range(length // PIECE)], axis=1)
    return jnp.where(valid, line, 0.0)


def masked(scores, col, row):
    wide = jnp.concatenate([col] * (scores.shape[1] // PIECE), axis=1)
    return jnp.where(wide == row, scores, FAR)


def partner_kernel(
    place_ref, qp_ref, ko_ref, vo_ref, k1_ref, v1a_ref, v1b_ref, k2_ref, v2a_ref, v2b_ref, s_ref, u_ref, msg_ref, *, scale
):
    length = vo_ref.shape[0]
    place = place_ref[0]
    even = lax.rem(place, 2) == 0
    pick = lambda a, b: jnp.where(even, a, b)
    k1 = k1_ref[0, :length, :]
    v1 = jnp.concatenate([v1a_ref[...], v1b_ref[...]], axis=0)
    v2 = jnp.concatenate([v2a_ref[...], v2b_ref[...]], axis=0)
    near, far = place >= 2, place >= 4
    doc_1 = doc_line(k1_ref, length, near)
    docs = jnp.concatenate(
        [pick(doc_line(ko_ref, length, True), doc_1), pick(doc_1, doc_line(k2_ref, length, far))], axis=1
    )
    keys_a = stacked_keys(pick(ko_ref[0, :length, :], k1))
    keys_b = stacked_keys(mm(pick(k1, k2_ref[0, :length, :]), u_ref[0]))
    values = jnp.concatenate(
        [stacked_values(pick(vo_ref[...], v1)), stacked_values(pick(v1, v2))], axis=0
    )
    query = qp_ref[0, :length, :] * scale
    query_a = stacked_queries(query)
    query_b = stacked_queries(pick(mm_nt(query, s_ref[0]), query))
    col = columns_of(doc_line(qp_ref, length, True))
    for start in range(0, length, ROWS):
        span = slice(start, start + ROWS)
        scores = jnp.concatenate([scored(query_a[span], keys_a), scored(query_b[span], keys_b)], axis=1)
        out, lse = softmax_part(masked(scores, col[span], docs), values)
        msg_ref[0, span, :] = out
        for i in range(0, ROWS, PIECE):
            line = length + (start + i) // PIECE
            msg_ref[0, line : line + 1, :] = jnp.broadcast_to(lse[i : i + PIECE], (PIECE, PIECE)).T[:1]
    first = length + length // PIECE
    msg_ref[0, first:, :] = jnp.zeros((msg_ref.shape[1] - first, msg_ref.shape[2]), jnp.float32)


def own_kernel(place_ref, qo_ref, k1_ref, v1a_ref, v1b_ref, s_ref, u_ref, od_ref, ld_ref, out_ref, lse_ref, *, scale):
    length = od_ref.shape[1]
    place = place_ref[0]
    even = lax.rem(place, 2) == 0
    pick = lambda a, b: jnp.where(even, a, b)
    docs = doc_line(k1_ref, length, place >= 2)
    k1 = k1_ref[0, :length, :]
    keys = stacked_keys(pick(mm(k1, u_ref[0]), k1))
    values = stacked_values(jnp.concatenate([v1a_ref[...], v1b_ref[...]], axis=0))
    query = qo_ref[0, :length, :] * scale
    query = stacked_queries(pick(query, mm_nt(query, s_ref[0])))
    col = columns_of(doc_line(qo_ref, length, True))
    for start in range(0, length, ROWS):
        span = slice(start, start + ROWS)
        out, lse = softmax_part(masked(scored(query[span], keys), col[span], docs), values)
        lse_d = ld_ref[0, span, :]
        peak = jnp.maximum(lse, lse_d)
        w, w_d = jnp.exp2(lse - peak), jnp.exp2(lse_d - peak)
        total = w + w_d
        out_ref[0, span, :] = (out * w + od_ref[0, span, :] * w_d) / total
        lse_ref[0, span, :] = peak + jnp.log2(total)


def cross_specs(group, per_group, length, rows, dh):
    return {
        "all": pl.BlockSpec((1, rows, dh), lambda h, p: (group * per_group + h, 0, 0)),
        "part": pl.BlockSpec((1, rows, dh), lambda h, p: (h, 0, 0)),
        "all_values": pl.BlockSpec((length, dh), lambda h, p: (0, group * per_group + h)),
        "half_values": pl.BlockSpec((length // 2, dh), lambda h, p: (0, group * per_group + h)),
        "step": pl.BlockSpec((1, dh, dh), lambda h, p: (group * per_group + h, 0, 0)),
        "all_plain": pl.BlockSpec((1, length, dh), lambda h, p: (group * per_group + h, 0, 0)),
        "plain": pl.BlockSpec((1, length, dh), lambda h, p: (h, 0, 0)),
    }


def partner_part(group, per_group, place, q_near, k_own, values, k1, v1, k2, v2, steps, joined, scale):
    length = values.shape[0]
    _, rows, dh = q_near.shape
    spec = cross_specs(group, per_group, length, rows, dh)
    names = ["all", "all", "all_values", "part"] + ["half_values"] * 2 + ["part"] + ["half_values"] * 2 + ["step"] * 2
    return pl.pallas_call(
        functools.partial(partner_kernel, scale=scale),
        grid_spec=pltpu.PrefetchScalarGridSpec(
            num_scalar_prefetch=1,
            grid=(per_group,),
            in_specs=[spec[name] for name in names],
            out_specs=spec["part"],
        ),
        out_shape=jax.ShapeDtypeStruct((per_group, rows, dh), jnp.float32),
        compiler_params=pltpu.CompilerParams(vmem_limit_bytes=VMEM_BYTES),
        name="partner",
        cost_estimate=lasting(6),
    )(place, q_near, k_own, values, k1, *v1, k2, *v2, steps, joined)


def own_part(group, per_group, place, q_own, k1, v1, near_steps, joined, od, ld, scale):
    length = od.shape[1]
    _, rows, dh = q_own.shape
    spec = cross_specs(group, per_group, length, rows, dh)
    names = ["all", "part", "half_values", "half_values", "step", "step", "all_plain", "all_plain"]
    shape = jax.ShapeDtypeStruct((per_group, length, dh), jnp.float32)
    return pl.pallas_call(
        functools.partial(own_kernel, scale=scale),
        grid_spec=pltpu.PrefetchScalarGridSpec(
            num_scalar_prefetch=1,
            grid=(per_group,),
            in_specs=[spec[name] for name in names],
            out_specs=[spec["plain"], spec["plain"]],
        ),
        out_shape=[shape, shape],
        compiler_params=pltpu.CompilerParams(vmem_limit_bytes=VMEM_BYTES),
        name="own",
        cost_estimate=lasting(4.5),
    )(place, q_own, k1, *v1, near_steps, joined, od, ld)


def merge_kernel(core_ref, o_ref, lse_ref, msg_ref, keep_ref, send_ref):
    length, dh = o_ref.shape[1:]
    share = keep_ref.shape[0]
    parts = []
    for i in range(length // PIECE):
        span = slice(i * PIECE, (i + 1) * PIECE)
        lse = lse_ref[0, span, :]
        lse_p = columns_of(msg_ref[0, length + i : length + i + 1, :])
        peak = jnp.maximum(lse, lse_p)
        w, w_p = jnp.exp2(lse - peak), jnp.exp2(lse_p - peak)
        parts.append((o_ref[0, span, :] * w + msg_ref[0, span, :] * w_p) / (w + w_p))
    whole = jnp.concatenate(parts, axis=0)
    first = core_ref[0] == 0
    low, high = whole[:share], whole[share:]
    keep_ref[...] = jnp.where(first, low, high)
    send_ref[...] = jnp.where(first, high, low)


def merge(core, o, lse, msg):
    per_group, length, dh = o.shape
    share = length // 2
    head = pl.BlockSpec((1, length, dh), lambda h, c: (h, 0, 0))
    out = pl.BlockSpec((share, dh), lambda h, c: (0, h))
    shape = jax.ShapeDtypeStruct((share, per_group * dh), jnp.float32)
    return pl.pallas_call(
        merge_kernel,
        grid_spec=pltpu.PrefetchScalarGridSpec(
            num_scalar_prefetch=1,
            grid=(per_group,),
            in_specs=[head, head, pl.BlockSpec((1,) + msg.shape[1:], lambda h, c: (h, 0, 0))],
            out_specs=[out, out],
        ),
        out_shape=[shape, shape],
        compiler_params=pltpu.CompilerParams(vmem_limit_bytes=VMEM_BYTES),
        name="merge",
        cost_estimate=lasting(2.2),
    )(core, o, lse, msg)


def halves_kernel(own_ref, other_ref, *out_refs):
    for ref, (high, low) in zip((own_ref, other_ref), (out_refs[:2], out_refs[2:])):
        high[...], low[...] = split(ref[...])


def weight_halves(w_own, w_other):
    depth, width = w_own.shape
    tile = depth // 4
    spec = pl.BlockSpec((tile, width), lambda n: (n, 0))
    return pl.pallas_call(
        halves_kernel,
        grid=(depth // tile,),
        in_specs=[spec] * 2,
        out_specs=[spec] * 4,
        out_shape=[jax.ShapeDtypeStruct((depth, width), jnp.bfloat16)] * 4,
        compiler_params=pltpu.CompilerParams(vmem_limit_bytes=VMEM_BYTES),
        name="weight_halves",
        cost_estimate=lasting(7),
    )(w_own, w_other)


def project_kernel(*refs):
    *a_refs, own_high, own_low, other_high, other_low, out_ref = refs
    half = len(a_refs) // 2
    parts = []
    for part, high, low in ((a_refs[:half], own_high, own_low), (a_refs[half:], other_high, other_low)):
        a_high, a_low = split(jnp.concatenate([r[...] for r in part], axis=1))
        stacked = scored(jnp.concatenate([a_high, a_low], axis=0), high[...])
        rows = a_high.shape[0]
        parts.append(stacked[:rows] + (stacked[rows:] + scored(a_high, low[...])))
    out_ref[...] = parts[0] + parts[1]


def project(kept, received, weights):
    share = kept[0].shape[0]
    depth, width = weights[0].shape
    tile = min(width, 512)
    a_spec = [pl.BlockSpec(a.shape, lambda n: (0, 0)) for a in kept + received]
    w_spec = pl.BlockSpec((depth, tile), lambda n: (0, n))
    return pl.pallas_call(
        project_kernel,
        grid=(width // tile,),
        in_specs=a_spec + [w_spec] * 4,
        out_specs=pl.BlockSpec((share, tile), lambda n: (0, n)),
        out_shape=jax.ShapeDtypeStruct((share, width), jnp.float32),
        compiler_params=pltpu.CompilerParams(vmem_limit_bytes=VMEM_BYTES),
        name="project",
        cost_estimate=lasting(7.5),
    )(*kept, *received, *weights)


def onward(value, steps):
    count = lax.axis_size("ctx")
    return lax.ppermute(value, "ctx", [(i, (i + steps) % count) for i in range(count)])


def exchanged(value, axis, bit):
    return lax.ppermute(value, axis, [(i, i ^ bit) for i in range(lax.axis_size(axis))])


def after(value, *others):
    return lax.optimization_barrier((value,) + others)[0]


def shards(queries, keys, values, transitions, betas, documents, out_weight):
    heads, length = betas.shape
    dh = queries.shape[1] // heads
    assert length == BLOCK_TOKENS and lax.axis_size("ctx") % 4 == 0 and lax.axis_size("head") == 2
    per_group = heads // GROUPS
    groups = range(GROUPS)
    scale = math.log2(math.e) / math.sqrt(dh)
    index = lax.axis_index("ctx").astype(jnp.int32)
    place = index.reshape(1)
    core = lax.axis_index("head").astype(jnp.int32).reshape(1)
    far_side = lax.rem(index, 4) >= 2
    v_first, v_last = values[: length // 2], values[length // 2 :]

    def chosen(block, behind):
        return jnp.where(far_side, behind, block)

    v1_last = onward(v_last, 2)
    v2_first = onward(v_first, 4)
    w_other = exchanged(out_weight, "head", 1)
    prepared = prepare(queries, keys, values, transitions, betas, documents, scale)
    q_msg, k_msg, steps, od, ld, v2_first, w_other = lax.optimization_barrier((*prepared, v2_first, w_other))
    own_k = [k_msg[g * per_group : (g + 1) * per_group] for g in groups]
    near_steps = exchanged(steps, "ctx", 1)
    v1_first = exchanged(chosen(v_first, v2_first), "ctx", 2)
    v2_last = onward(after(v_last, steps), 4)
    k2 = [onward(own_k[0], 4)]
    q_near = exchanged(after(q_msg, near_steps), "ctx", 1)
    joined = onward(joined_steps(place, steps, near_steps), 2)
    w_other, v1_first, v1_last, v2_last = lax.optimization_barrier((w_other, v1_first, v1_last, v2_last))
    k2 += [onward(after(own_k[g], v2_last), 4) for g in groups[1:]]
    weights = weight_halves(out_weight, w_other)
    sources = [chosen(after(own_k[g], *weights), k2[g]) for g in groups]
    k1 = [exchanged(source, "ctx", 2) for source in sources]
    place = after(place, *sources)
    v1, v2 = (v1_first, v1_last), (v2_first, v2_last)
    kept, received = [], []
    for g in groups:
        msg = partner_part(g, per_group, place, q_near, k_msg, values, k1[g], v1, k2[g], v2, steps, joined, scale)
        out, lse = own_part(g, per_group, place, q_msg, k1[g], v1, near_steps, joined, od, ld, scale)
        keep, send = merge(core, out, lse, exchanged(msg, "ctx", 1))
        kept.append(keep)
        received.append(exchanged(send, "head", 1))
    return project(kept, received, weights)


def solution(mesh):
    return jax.shard_map(
        shards,
        mesh=mesh,
        in_specs=(
            P("ctx", "head"),
            P("ctx", "head"),
            P("ctx", "head"),
            P("ctx", "head"),
            P("head", "ctx"),
            P("ctx"),
            P("head", None),
        ),
        out_specs=P(("ctx", "head"), None),
        check_vma=False,
    )
```

time: 665 us -> 126 us (0.19)
  local copies, waits for them, and re-layouts: 426 us -> 5.78 us
  matrix products: 107 us -> 0 us
  Pallas kernels: 0 us -> 56.6 us
  waiting for transfers between devices: 58.5 us -> 33.8 us
  other arithmetic: 16.4 us -> 0.26 us
  between operations: 14.8 us -> 0.16 us
  starting transfers between devices: 37.2 us -> 29 us
    reshape x14 -> x0, local copies, waits for them, and re-layouts: 328 us -> none  [the longest x10 324 us: unit_lower_inverse(): tiled = lower_mat.reshape(lead + (count, 2, size, count, 2, size))]
    dot_general x55 -> x0, matrix products: 107 us -> none  [the longest x54 98 us: contract(): return jnp.einsum(pattern, left_operand, right_operand, precision=HIGHEST)]
    pallas_call x0 -> x10, Pallas kernels: none -> 56.6 us  [the longest x1 12.9 us: prepare(): pl.pallas_call(functools.partial(prepare_kernel, scale=scale), grid=(head...]
    gather x13 -> x0, local copies, waits for them, and re-layouts: 36.4 us -> none  [unit_lower_inverse(): diagonal_tiles = jnp.diagonal(tiled, axis1=depth, axis2=depth + 3)]
    psum x1 -> x0, waiting for transfers between devices: 30.7 us -> none  [shards(): full_sum = lax.psum(partial_out, 'head')]
    add x1 -> x0, local copies, waits for them, and re-layouts: 26.3 us -> none  [local_parts(): jnp.eye(piece_size, dtype=jnp.float32)]
    unnamed x72 -> x34, local copies, waits for them, and re-layouts: 14.1 us -> 4.63 us
    another operation x7 -> x0, local copies, waits for them, and re-layouts: 9.08 us -> none
  transfers between devices with their start and end apart: 10 -> 16, of which waited for: 4 -> 7; matrix products, arithmetic and copies ran while one was open for 11% -> 1% of each run, Pallas kernels for 0% -> 39%
where the time goes in v1:
time: 126 us
  Pallas kernels  56.6 us (45%)
  waiting for transfers between devices  33.8 us (27%)
  starting transfers between devices  29 us (23%)
  local copies, waits for them, and re-layouts  5.78 us (5%)
    ppermute x10, starting transfers between devices, exchanged(): lax.ppermute(value, axis, [(i, i ^ bit) for i in range(lax.axis_size(axis...  23.3 us
    ppermute x10, waiting for transfers between devices, exchanged(): lax.ppermute(value, axis, [(i, i ^ bit) for i in range(lax.axis_size(axis...  19.1 us
    ppermute x6, waiting for transfers between devices, onward(): lax.ppermute(value, 'ctx', [(i, (i + steps) % count) for i in range(count)])  14.6 us
    pallas_call x1, Pallas kernels, prepare(): pl.pallas_call(functools.partial(prepare_kernel, scale=scale), grid=(head...  12.9 us
    pallas_call x2, Pallas kernels, partner_part(): pl.pallas_call(functools.partial(partner_kernel, scale=scale), grid_spec=...  12.6 us
    pallas_call x2, Pallas kernels, own_part(): pl.pallas_call(functools.partial(own_kernel, scale=scale), grid_spec=pltp...  9.42 us
    pallas_call x1, Pallas kernels, project(): pl.pallas_call(project_kernel, grid=(width // tile,), in_specs=a_spec + [...  7.65 us
    pallas_call x1, Pallas kernels, weight_halves(): pl.pallas_call(halves_kernel, grid=(depth // tile,), in_specs=[spec] * 2,...  7.43 us
  transfers between devices with their start and end apart: 16, of which 7 were waited for; matrix products, arithmetic and copies ran while one was open for 1% of the time, Pallas kernels for 39%

profile of v1, /device:TPU:0, one launch (start us, length us, event | category | flops | bytes accessed | tf_op | source)
XLA Modules:
  0.0 125.6 jit_solution(7936449070953644118)
XLA Ops:
  0.0 0.5 collective-permute-start.1
  0.5 1.1 slice.12
  1.5 0.0 copy-start
  1.5 2.6 %collective-permute-start = (f32[256,512]{1,0:T(8,128)S(1)}, f32[256,512]{1,0:T(8,128)S(1)}, u32[]{:S(2)}, u32[]{:S(2)}) collective-permute-start(f32[256,512]{1,0:T(8,128)S(1)} %slice.12), channel_id=1, source_target_pairs={{0,8},{2,10},{4,12},{6,14},{8,16},{10,18},{12,20},{14,22},{16,24},... | collective-permute-start | bytes 1572872 | tf_op jit(solution)/shard_map/ppermute | solution.py:476
  4.2 12.9 %prepare.1 = (f32[4,520,128]{2,1,0:T(8,128)}, f32[4,520,128]{2,1,0:T(8,128)}, f32[4,128,128]{2,1,0:T(8,128)}, f32[4,512,128]{2,1,0:T(8,128)}, f32[4,512,128]{2,1,0:T(8,128)}) custom-call(f32[512,512]{1,0:T(8,128)} %q_ref.1, f32[512,512]{1,0:T(8,128)} %k_ref.1, f32[512,512]{1,0:T(8,128)} %vo_ref.3, f32[512,512]{1,0:T(8,128)} %w_ref.1, f32[4,512]{1,0:T(4,128)} %beta_ref.1, ...), custom_call_target="tpu_custom_call" | custom-call | flops 14949999616 | bytes 1000 | tf_op jit(solution)/shard_map/prepare/pallas_call | solution.py:219
  17.1 0.0 copy-start.1
  17.1 1.7 %collective-permute-done.v2a_ref = f32[256,512]{1,0:T(8,128)S(1)} collective-permute-done((f32[256,512]{1,0:T(8,128)S(1)}, f32[256,512]{1,0:T(8,128)S(1)}, u32[]{:S(2)}, u32[]{:S(2)}) %collective-permute-start) | collective-permute-done | bytes 524320 | tf_op jit(solution)/shard_map/ppermute | solution.py:476
  18.8 0.0 collective-permute-done.1.other_ref
  18.8 0.0 copy-done
  18.8 0.1 fusion.1
  18.9 1.6 %collective-permute-start.4 = (f32[256,512]{1,0:T(8,128)S(1)}, f32[256,512]{1,0:T(8,128)S(1)}, u32[]{:S(2)}, u32[]{:S(2)}) collective-permute-start(f32[256,512]{1,0:T(8,128)S(1)} %get-tuple-element.48), channel_id=1, source_target_pairs={{0,4},{2,6},{4,8},{6,10},{8,12},{10,14},{12,16},{14,18},{16,20},{1... | collective-permute-start | bytes 1572872 | tf_op jit(solution)/shard_map/ppermute | solution.py:476
  20.5 0.0 collective-permute-start.5
  20.5 1.5 %collective-permute-start.3 = (f32[256,512]{1,0:T(8,128)S(1)}, f32[256,512]{1,0:T(8,128)S(1)}, u32[]{:S(2)}, u32[]{:S(2)}) collective-permute-start(f32[256,512]{1,0:T(8,128)S(1)} %get-tuple-element.76), channel_id=1, source_target_pairs={{0,4},{2,6},{4,0},{6,2},{8,12},{10,14},{12,8},{14,10},{16,20},{18,... | collective-permute-start | bytes 1572872 | tf_op jit(solution)/shard_map/ppermute | solution.py:480
  22.0 0.0 copy-done.12
  22.0 1.5 %collective-permute-start.8 = (f32[4,128,128]{2,1,0:T(8,128)S(1)}, f32[4,128,128]{2,1,0:T(8,128)S(1)}, u32[]{:S(2)}, u32[]{:S(2)}) collective-permute-start(f32[4,128,128]{2,1,0:T(8,128)S(1)} %copy-done.12), channel_id=1, source_target_pairs={{0,2},{2,0},{4,6},{6,4},{8,10},{10,8},{12,14},{14,12},{16,18},{18,... | collective-permute-start | bytes 786440 | tf_op jit(solution)/shard_map/ppermute | solution.py:480
  23.5 0.0 copy-done.1
  23.5 0.1 fusion
  23.5 0.0 copy-done.4
  23.6 1.4 %collective-permute-start.2 = (f32[2,520,128]{2,1,0:T(8,128)S(1)}, f32[2,520,128]{2,1,0:T(8,128)S(1)}, u32[]{:S(2)}, u32[]{:S(2)}) collective-permute-start(f32[2,520,128]{2,1,0:T(8,128)S(1)} %get-tuple-element.54), channel_id=1, source_target_pairs={{0,8},{2,10},{4,12},{6,14},{8,16},{10,18},{12,20},{14,22},{16,24},... | collective-permute-start | bytes 1597448 | tf_op jit(solution)/shard_map/ppermute | solution.py:476
  25.0 4.6 %collective-permute-done.8.near_ref.s_ref = f32[4,128,128]{2,1,0:T(8,128)S(1)} collective-permute-done((f32[4,128,128]{2,1,0:T(8,128)S(1)}, f32[4,128,128]{2,1,0:T(8,128)S(1)}, u32[]{:S(2)}, u32[]{:S(2)}) %collective-permute-start.8) | collective-permute-done | bytes 262176 | tf_op jit(solution)/shard_map/ppermute | solution.py:480
  29.6 1.5 %collective-permute-start.10 = (f32[4,520,128]{2,1,0:T(8,128)}, f32[4,520,128]{2,1,0:T(8,128)}, u32[]{:S(2)}, u32[]{:S(2)}) collective-permute-start(f32[4,520,128]{2,1,0:T(8,128)} %get-tuple-element.66.qo_ref), channel_id=1, source_target_pairs={{0,2},{2,0},{4,6},{6,4},{8,10},{10,8},{12,14},{14,12},{16,18},{18,... | collective-permute-start | bytes 3194888 | tf_op jit(solution)/shard_map/ppermute | solution.py:480
  31.1 6.1 %collective-permute-done.5.v2b_ref = f32[256,512]{1,0:T(8,128)S(1)} collective-permute-done((f32[256,512]{1,0:T(8,128)S(1)}, f32[256,512]{1,0:T(8,128)S(1)}, u32[]{:S(2)}, u32[]{:S(2)}) %collective-permute-start.5) | collective-permute-done | bytes 524320 | tf_op jit(solution)/shard_map/ppermute | solution.py:476
  37.2 0.0 collective-permute-done.4.v1b_ref
  37.2 8.0 %collective-permute-done.3.v1a_ref = f32[256,512]{1,0:T(8,128)S(1)} collective-permute-done((f32[256,512]{1,0:T(8,128)S(1)}, f32[256,512]{1,0:T(8,128)S(1)}, u32[]{:S(2)}, u32[]{:S(2)}) %collective-permute-start.3) | collective-permute-done | bytes 524320 | tf_op jit(solution)/shard_map/ppermute | solution.py:480
  45.2 0.0 collective-permute-start.6
  45.2 7.4 %weight_halves.1 = (bf16[512,2048]{1,0:T(8,128)(2,1)}, bf16[512,2048]{1,0:T(8,128)(2,1)}, bf16[512,2048]{1,0:T(8,128)(2,1)}, bf16[512,2048]{1,0:T(8,128)(2,1)}) custom-call(f32[512,2048]{1,0:T(8,128)} %own_ref.1, f32[512,2048]{1,0:T(8,128)} %collective-permute-done.1.other_ref), custom_call_target="tpu_custom_call" | custom-call | flops 8049999872 | bytes 1000 | tf_op jit(solution)/shard_map/weight_halves/pallas_call | solution.py:432
  52.6 0.0 copy-done.13
  52.6 0.0 copy-done.11
  52.6 0.0 copy-done.9
  52.6 0.0 copy-done.10
  52.6 0.0 collective-permute-done.2.k2_ref
  52.7 0.1 broadcast_select_fusion.1
  52.7 7.1 %collective-permute-start.7 = (f32[2,520,128]{2,1,0:T(8,128)S(1)}, f32[2,520,128]{2,1,0:T(8,128)S(1)}, u32[]{:S(2)}, u32[]{:S(2)}) collective-permute-start(f32[2,520,128]{2,1,0:T(8,128)S(1)} %broadcast_select_fusion.1), channel_id=1, source_target_pairs={{0,4},{2,6},{4,0},{6,2},{8,12},{10,14},{12,8},{14,10},{16,20},{18,... | collective-permute-start | bytes 1597448 | tf_op jit(solution)/shard_map/ppermute | solution.py:480
  59.9 2.0 %joined_steps.1 = f32[4,128,128]{2,1,0:T(8,128)} custom-call(s32[1]{0:T(128)} %bitcast.1.place_ref, f32[4,128,128]{2,1,0:T(8,128)} %get-tuple-element.47.own_ref.s_ref, f32[4,128,128]{2,1,0:T(8,128)} %copy-done.13), custom_call_target="tpu_custom_call" | custom-call | flops 2300000000 | bytes 1000 | tf_op jit(solution)/shard_map/joined_steps/pallas_call | solution.py:250
  61.9 0.1 collective-permute-start.9
  62.0 0.0 collective-permute-done.6.k2_ref
  62.0 0.1 broadcast_select_fusion
  62.0 9.3 %collective-permute-start.12 = (f32[2,520,128]{2,1,0:T(8,128)S(1)}, f32[2,520,128]{2,1,0:T(8,128)S(1)}, u32[]{:S(2)}, u32[]{:S(2)}) collective-permute-start(f32[2,520,128]{2,1,0:T(8,128)S(1)} %broadcast_select_fusion), channel_id=1, source_target_pairs={{0,4},{2,6},{4,0},{6,2},{8,12},{10,14},{12,8},{14,10},{16,20},{18,... | collective-permute-start | bytes 1597448 | tf_op jit(solution)/shard_map/ppermute | solution.py:480
  71.3 6.9 %collective-permute-done.9.u_ref = f32[4,128,128]{2,1,0:T(8,128)S(1)} collective-permute-done((f32[4,128,128]{2,1,0:T(8,128)}, f32[4,128,128]{2,1,0:T(8,128)S(1)}, u32[]{:S(2)}, u32[]{:S(2)}) %collective-permute-start.9) | collective-permute-done | bytes 262176 | tf_op jit(solution)/shard_map/ppermute | solution.py:476
  78.2 0.0 collective-permute-done.7.k1_ref
  78.2 0.7 copy-done.14
  78.9 0.8 copy-done.7
  79.7 4.7 %own.2 = (f32[2,512,128]{2,1,0:T(8,128)}, f32[2,512,128]{2,1,0:T(8,128)}) custom-call(s32[1]{0:T(128)} %bitcast.1.place_ref, f32[4,520,128]{2,1,0:T(8,128)} %get-tuple-element.66.qo_ref, f32[2,520,128]{2,1,0:T(8,128)} %copy-done.7, f32[256,512]{1,0:T(8,128)} %copy-done.10, f32[256,512]{1,0:T(8,128)} %copy-done.9, f32[4,128,128]{2,1,0:T(8,128)} %copy-done.13, ...), custom_call_target="tpu_custom_call" | custom-call | flops 5175000064 | bytes 1000 | tf_op jit(solution)/shard_map/own/pallas_call | solution.py:369
  84.4 0.0 collective-permute-done.10.qp_ref
  84.4 6.3 %partner.2 = f32[2,520,128]{2,1,0:T(8,128)} custom-call(s32[1]{0:T(128)} %bitcast.1.place_ref, f32[4,520,128]{2,1,0:T(8,128)} %collective-permute-done.10.qp_ref, f32[4,520,128]{2,1,0:T(8,128)} %get-tuple-element.44.ko_ref, f32[512,512]{1,0:T(8,128)} %vo_ref.3, f32[2,520,128]{2,1,0:T(8,128)} %copy-done.7, f32[256,512]{1,0:T(8,128)} %copy-done.10, ...), custom_call_target="tpu_custom_call" | custom-call | flops 6899999744 | bytes 1000 | tf_op jit(solution)/shard_map/partner/pallas_call | solution.py:348
  90.7 1.5 %collective-permute-start.11 = (f32[2,520,128]{2,1,0:T(8,128)}, f32[2,520,128]{2,1,0:T(8,128)S(1)}, u32[]{:S(2)}, u32[]{:S(2)}) collective-permute-start(f32[2,520,128]{2,1,0:T(8,128)} %partner.2), channel_id=1, source_target_pairs={{0,2},{2,0},{4,6},{6,4},{8,10},{10,8},{12,14},{14,12},{16,18},{18,... | collective-permute-start | bytes 1597448 | tf_op jit(solution)/shard_map/ppermute | solution.py:480
  92.2 0.0 collective-permute-done.12.k1_ref
  92.2 0.8 copy-done.5
  93.0 6.3 %partner.3 = f32[2,520,128]{2,1,0:T(8,128)} custom-call(s32[1]{0:T(128)} %bitcast.1.place_ref, f32[4,520,128]{2,1,0:T(8,128)} %collective-permute-done.10.qp_ref, f32[4,520,128]{2,1,0:T(8,128)} %get-tuple-element.44.ko_ref, f32[512,512]{1,0:T(8,128)} %vo_ref.3, f32[2,520,128]{2,1,0:T(8,128)} %copy-done.5, f32[256,512]{1,0:T(8,128)} %copy-done.10, ...), custom_call_target="tpu_custom_call" | custom-call | flops 6899999744 | bytes 1000 | tf_op jit(solution)/shard_map/partner/pallas_call | solution.py:348
  99.4 0.5 collective-permute-start.13
  99.9 4.7 %own.3 = (f32[2,512,128]{2,1,0:T(8,128)}, f32[2,512,128]{2,1,0:T(8,128)}) custom-call(s32[1]{0:T(128)} %bitcast.1.place_ref, f32[4,520,128]{2,1,0:T(8,128)} %get-tuple-element.66.qo_ref, f32[2,520,128]{2,1,0:T(8,128)} %copy-done.5, f32[256,512]{1,0:T(8,128)} %copy-done.10, f32[256,512]{1,0:T(8,128)} %copy-done.9, f32[4,128,128]{2,1,0:T(8,128)} %copy-done.13, ...), custom_call_target="tpu_custom_call" | custom-call | flops 5175000064 | bytes 1000 | tf_op jit(solution)/shard_map/own/pallas_call | solution.py:369
  104.5 0.0 collective-permute-done.11.msg_ref
  104.6 0.0 copy-start.6
  104.6 0.8 copy-done.6
  105.4 2.3 %merge.2 = (f32[256,256]{1,0:T(8,128)}, f32[256,256]{1,0:T(8,128)}) custom-call(s32[1]{0:T(128)} %bitcast.core_ref, f32[2,512,128]{2,1,0:T(8,128)} %get-tuple-element.64.o_ref, f32[2,512,128]{2,1,0:T(8,128)} %get-tuple-element.65.lse_ref, f32[2,520,128]{2,1,0:T(8,128)} %copy-done.6), custom_call_target="tpu_custom_call" | custom-call | flops 2529999872 | bytes 1000 | tf_op jit(solution)/shard_map/merge/pallas_call | solution.py:408
  107.6 0.0 collective-permute-start.14
  107.6 4.8 %collective-permute-done.13.msg_ref = f32[2,520,128]{2,1,0:T(8,128)S(1)} collective-permute-done((f32[2,520,128]{2,1,0:T(8,128)}, f32[2,520,128]{2,1,0:T(8,128)S(1)}, u32[]{:S(2)}, u32[]{:S(2)}) %collective-permute-start.13) | collective-permute-done | bytes 532512 | tf_op jit(solution)/shard_map/ppermute | solution.py:480
  112.4 0.8 copy-done.8
  113.2 2.3 %merge.3 = (f32[256,256]{1,0:T(8,128)}, f32[256,256]{1,0:T(8,128)}) custom-call(s32[1]{0:T(128)} %bitcast.core_ref, f32[2,512,128]{2,1,0:T(8,128)} %get-tuple-element.68.o_ref, f32[2,512,128]{2,1,0:T(8,128)} %get-tuple-element.69.lse_ref, f32[2,520,128]{2,1,0:T(8,128)} %copy-done.8), custom_call_target="tpu_custom_call" | custom-call | flops 2529999872 | bytes 1000 | tf_op jit(solution)/shard_map/merge/pallas_call | solution.py:408
  115.4 0.0 collective-permute-start.15
  115.5 0.0 collective-permute-done.14.refs_2_
  115.5 1.7 %collective-permute-done.15.refs_3_ = f32[256,256]{1,0:T(8,128)S(1)} collective-permute-done((f32[256,256]{1,0:T(8,128)}, f32[256,256]{1,0:T(8,128)S(1)}, u32[]{:S(2)}, u32[]{:S(2)}) %collective-permute-start.15) | collective-permute-done | bytes 262176 | tf_op jit(solution)/shard_map/ppermute | solution.py:480
  117.2 0.7 copy-done.16
  117.9 7.7 %project.1 = f32[256,2048]{1,0:T(8,128)} custom-call(f32[256,256]{1,0:T(8,128)} %get-tuple-element.67.refs_0_, f32[256,256]{1,0:T(8,128)} %get-tuple-element.70.refs_1_, f32[256,256]{1,0:T(8,128)} %copy-done.15, f32[256,256]{1,0:T(8,128)} %copy-done.16, bf16[512,2048]{1,0:T(8,128)(2,1)} %get-tuple-element.50.refs_4_, ...), custom_call_target="tpu_custom_call" | custom-call | flops 8625000448 | bytes 1000 | tf_op jit(solution)/shard_map/project/pallas_call | solution.py:462
  (17 shorter events, 0.0 us)
Async XLA Ops:
  0.0 18.8 %collective-permute-start.1 = (f32[512,2048]{1,0:T(8,128)}, f32[512,2048]{1,0:T(8,128)}, u32[]{:S(2)}, u32[]{:S(2)}) collective-permute-start(f32[512,2048]{1,0:T(8,128)} %own_ref.1), channel_id=1, source_target_pairs={{0,1},{1,0},{2,3},{3,2},{4,5},{5,4},{6,7},{7,6},{8,9},{9,8},{10,11... | collective-permute-start | bytes 12582920 | tf_op jit(solution)/shard_map/ppermute | solution.py:480
  1.5 17.3 %copy-start = (f32[512,512]{1,0:T(8,128)S(1)}, f32[512,512]{1,0:T(8,128)}, u32[]{:S(2)}) copy-start(f32[512,512]{1,0:T(8,128)} %vo_ref.3) | copy-start | bytes 3145732
  1.5 17.2 %collective-permute-start = (f32[256,512]{1,0:T(8,128)S(1)}, f32[256,512]{1,0:T(8,128)S(1)}, u32[]{:S(2)}, u32[]{:S(2)}) collective-permute-start(f32[256,512]{1,0:T(8,128)S(1)} %slice.12), channel_id=1, source_target_pairs={{0,8},{2,10},{4,12},{6,14},{8,16},{10,18},{12,20},{14,22},{16,24},... | collective-permute-start | bytes 1572872 | tf_op jit(solution)/shard_map/ppermute | solution.py:476
  17.1 4.9 %copy-start.12 = (f32[4,128,128]{2,1,0:T(8,128)S(1)}, f32[4,128,128]{2,1,0:T(8,128)}, u32[]{:S(2)}) copy-start(f32[4,128,128]{2,1,0:T(8,128)} %get-tuple-element.47.own_ref.s_ref) | copy-start | bytes 786436
  17.1 6.4 %copy-start.1 = (f32[4,520,128]{2,1,0:T(8,128)S(1)}, f32[4,520,128]{2,1,0:T(8,128)}, u32[]{:S(2)}) copy-start(f32[4,520,128]{2,1,0:T(8,128)} %get-tuple-element.44.ko_ref) | copy-start | bytes 3194884
  18.8 4.8 %copy-start.4 = (f32[256,512]{1,0:T(8,128)}, f32[256,512]{1,0:T(8,128)S(1)}, u32[]{:S(2)}) copy-start(f32[256,512]{1,0:T(8,128)S(1)} %collective-permute-done.v2a_ref) | copy-start | bytes 1572868
  18.9 18.2 %collective-permute-start.4 = (f32[256,512]{1,0:T(8,128)S(1)}, f32[256,512]{1,0:T(8,128)S(1)}, u32[]{:S(2)}, u32[]{:S(2)}) collective-permute-start(f32[256,512]{1,0:T(8,128)S(1)} %get-tuple-element.48), channel_id=1, source_target_pairs={{0,4},{2,6},{4,8},{6,10},{8,12},{10,14},{12,16},{14,18},{16,20},{1... | collective-permute-start | bytes 1572872 | tf_op jit(solution)/shard_map/ppermute | solution.py:476
  20.5 16.7 %collective-permute-start.5 = (f32[256,512]{1,0:T(8,128)S(1)}, f32[256,512]{1,0:T(8,128)S(1)}, u32[]{:S(2)}, u32[]{:S(2)}) collective-permute-start(f32[256,512]{1,0:T(8,128)S(1)} %get-tuple-element.48), channel_id=1, source_target_pairs={{0,8},{2,10},{4,12},{6,14},{8,16},{10,18},{12,20},{14,22},{16,24},... | collective-permute-start | bytes 1572872 | tf_op jit(solution)/shard_map/ppermute | solution.py:476
  20.5 24.7 %collective-permute-start.3 = (f32[256,512]{1,0:T(8,128)S(1)}, f32[256,512]{1,0:T(8,128)S(1)}, u32[]{:S(2)}, u32[]{:S(2)}) collective-permute-start(f32[256,512]{1,0:T(8,128)S(1)} %get-tuple-element.76), channel_id=1, source_target_pairs={{0,4},{2,6},{4,0},{6,2},{8,12},{10,14},{12,8},{14,10},{16,20},{18,... | collective-permute-start | bytes 1572872 | tf_op jit(solution)/shard_map/ppermute | solution.py:480
  22.0 7.6 %collective-permute-start.8 = (f32[4,128,128]{2,1,0:T(8,128)S(1)}, f32[4,128,128]{2,1,0:T(8,128)S(1)}, u32[]{:S(2)}, u32[]{:S(2)}) collective-permute-start(f32[4,128,128]{2,1,0:T(8,128)S(1)} %copy-done.12), channel_id=1, source_target_pairs={{0,2},{2,0},{4,6},{6,4},{8,10},{10,8},{12,14},{14,12},{16,18},{18,... | collective-permute-start | bytes 786440 | tf_op jit(solution)/shard_map/ppermute | solution.py:480
  23.6 29.1 %collective-permute-start.2 = (f32[2,520,128]{2,1,0:T(8,128)S(1)}, f32[2,520,128]{2,1,0:T(8,128)S(1)}, u32[]{:S(2)}, u32[]{:S(2)}) collective-permute-start(f32[2,520,128]{2,1,0:T(8,128)S(1)} %get-tuple-element.54), channel_id=1, source_target_pairs={{0,8},{2,10},{4,12},{6,14},{8,16},{10,18},{12,20},{14,22},{16,24},... | collective-permute-start | bytes 1597448 | tf_op jit(solution)/shard_map/ppermute | solution.py:476
  29.6 23.0 %copy-start.13 = (f32[4,128,128]{2,1,0:T(8,128)}, f32[4,128,128]{2,1,0:T(8,128)S(1)}, u32[]{:S(2)}) copy-start(f32[4,128,128]{2,1,0:T(8,128)S(1)} %collective-permute-done.8.near_ref.s_ref) | copy-start | bytes 786436
  29.6 54.8 %collective-permute-start.10 = (f32[4,520,128]{2,1,0:T(8,128)}, f32[4,520,128]{2,1,0:T(8,128)}, u32[]{:S(2)}, u32[]{:S(2)}) collective-permute-start(f32[4,520,128]{2,1,0:T(8,128)} %get-tuple-element.66.qo_ref), channel_id=1, source_target_pairs={{0,2},{2,0},{4,6},{6,4},{8,10},{10,8},{12,14},{14,12},{16,18},{18,... | collective-permute-start | bytes 3194888 | tf_op jit(solution)/shard_map/ppermute | solution.py:480
  37.2 15.5 %copy-start.11 = (f32[256,512]{1,0:T(8,128)}, f32[256,512]{1,0:T(8,128)S(1)}, u32[]{:S(2)}) copy-start(f32[256,512]{1,0:T(8,128)S(1)} %collective-permute-done.5.v2b_ref) | copy-start | bytes 1572868
  37.2 15.5 %copy-start.9 = (f32[256,512]{1,0:T(8,128)}, f32[256,512]{1,0:T(8,128)S(1)}, u32[]{:S(2)}) copy-start(f32[256,512]{1,0:T(8,128)S(1)} %collective-permute-done.4.v1b_ref) | copy-start | bytes 1572868
  45.2 7.5 %copy-start.10 = (f32[256,512]{1,0:T(8,128)}, f32[256,512]{1,0:T(8,128)S(1)}, u32[]{:S(2)}) copy-start(f32[256,512]{1,0:T(8,128)S(1)} %collective-permute-done.3.v1a_ref) | copy-start | bytes 1572868
  45.2 16.8 %collective-permute-start.6 = (f32[2,520,128]{2,1,0:T(8,128)S(1)}, f32[2,520,128]{2,1,0:T(8,128)S(1)}, u32[]{:S(2)}, u32[]{:S(2)}) collective-permute-start(f32[2,520,128]{2,1,0:T(8,128)S(1)} %get-tuple-element.57), channel_id=1, source_target_pairs={{0,8},{2,10},{4,12},{6,14},{8,16},{10,18},{12,20},{14,22},{16,24},... | collective-permute-start | bytes 1597448 | tf_op jit(solution)/shard_map/ppermute | solution.py:476
  52.7 9.2 %copy-start.2 = (f32[2,520,128]{2,1,0:T(8,128)}, f32[2,520,128]{2,1,0:T(8,128)S(1)}, u32[]{:S(2)}) copy-start(f32[2,520,128]{2,1,0:T(8,128)S(1)} %collective-permute-done.2.k2_ref) | copy-start | bytes 1597444
  52.7 25.4 %collective-permute-start.7 = (f32[2,520,128]{2,1,0:T(8,128)S(1)}, f32[2,520,128]{2,1,0:T(8,128)S(1)}, u32[]{:S(2)}, u32[]{:S(2)}) collective-permute-start(f32[2,520,128]{2,1,0:T(8,128)S(1)} %broadcast_select_fusion.1), channel_id=1, source_target_pairs={{0,4},{2,6},{4,0},{6,2},{8,12},{10,14},{12,8},{14,10},{16,20},{18,... | collective-permute-start | bytes 1597448 | tf_op jit(solution)/shard_map/ppermute | solution.py:480
  61.9 16.3 %collective-permute-start.9 = (f32[4,128,128]{2,1,0:T(8,128)}, f32[4,128,128]{2,1,0:T(8,128)S(1)}, u32[]{:S(2)}, u32[]{:S(2)}) collective-permute-start(f32[4,128,128]{2,1,0:T(8,128)} %joined_steps.1), channel_id=1, source_target_pairs={{0,4},{2,6},{4,8},{6,10},{8,12},{10,14},{12,16},{14,18},{16,20},{1... | collective-permute-start | bytes 786440 | tf_op jit(solution)/shard_map/ppermute | solution.py:476
  62.0 22.4 %copy-start.3 = (f32[2,520,128]{2,1,0:T(8,128)}, f32[2,520,128]{2,1,0:T(8,128)S(1)}, u32[]{:S(2)}) copy-start(f32[2,520,128]{2,1,0:T(8,128)S(1)} %collective-permute-done.6.k2_ref) | copy-start | bytes 1597444
  62.0 30.2 %collective-permute-start.12 = (f32[2,520,128]{2,1,0:T(8,128)S(1)}, f32[2,520,128]{2,1,0:T(8,128)S(1)}, u32[]{:S(2)}, u32[]{:S(2)}) collective-permute-start(f32[2,520,128]{2,1,0:T(8,128)S(1)} %broadcast_select_fusion), channel_id=1, source_target_pairs={{0,4},{2,6},{4,0},{6,2},{8,12},{10,14},{12,8},{14,10},{16,20},{18,... | collective-permute-start | bytes 1597448 | tf_op jit(solution)/shard_map/ppermute | solution.py:480
  78.2 0.7 copy-start.14
  78.9 0.8 copy-start.7
  90.7 13.8 %collective-permute-start.11 = (f32[2,520,128]{2,1,0:T(8,128)}, f32[2,520,128]{2,1,0:T(8,128)S(1)}, u32[]{:S(2)}, u32[]{:S(2)}) collective-permute-start(f32[2,520,128]{2,1,0:T(8,128)} %partner.2), channel_id=1, source_target_pairs={{0,2},{2,0},{4,6},{6,4},{8,10},{10,8},{12,14},{14,12},{16,18},{18,... | collective-permute-start | bytes 1597448 | tf_op jit(solution)/shard_map/ppermute | solution.py:480
  92.2 0.8 copy-start.5
  99.4 13.0 %collective-permute-start.13 = (f32[2,520,128]{2,1,0:T(8,128)}, f32[2,520,128]{2,1,0:T(8,128)S(1)}, u32[]{:S(2)}, u32[]{:S(2)}) collective-permute-start(f32[2,520,128]{2,1,0:T(8,128)} %partner.3), channel_id=1, source_target_pairs={{0,2},{2,0},{4,6},{6,4},{8,10},{10,8},{12,14},{14,12},{16,18},{18,... | collective-permute-start | bytes 1597448 | tf_op jit(solution)/shard_map/ppermute | solution.py:480
  104.6 0.8 copy-start.6
  107.6 7.8 %collective-permute-start.14 = (f32[256,256]{1,0:T(8,128)}, f32[256,256]{1,0:T(8,128)S(1)}, u32[]{:S(2)}, u32[]{:S(2)}) collective-permute-start(f32[256,256]{1,0:T(8,128)} %get-tuple-element.71), channel_id=1, source_target_pairs={{0,1},{1,0},{2,3},{3,2},{4,5},{5,4},{6,7},{7,6},{8,9},{9,8},{10,11... | collective-permute-start | bytes 786440 | tf_op jit(solution)/shard_map/ppermute | solution.py:480
  112.4 0.8 copy-start.8
  115.4 1.7 %collective-permute-start.15 = (f32[256,256]{1,0:T(8,128)}, f32[256,256]{1,0:T(8,128)S(1)}, u32[]{:S(2)}, u32[]{:S(2)}) collective-permute-start(f32[256,256]{1,0:T(8,128)} %get-tuple-element.72), channel_id=1, source_target_pairs={{0,1},{1,0},{2,3},{3,2},{4,5},{5,4},{6,7},{7,6},{8,9},{9,8},{10,11... | collective-permute-start | bytes 786440 | tf_op jit(solution)/shard_map/ppermute | solution.py:480
  115.5 1.7 %copy-start.15 = (f32[256,256]{1,0:T(8,128)}, f32[256,256]{1,0:T(8,128)S(1)}, u32[]{:S(2)}) copy-start(f32[256,256]{1,0:T(8,128)S(1)} %collective-permute-done.14.refs_2_) | copy-start | bytes 786436
  117.2 0.7 copy-start.16

commit v2 on v1

--- a/solution.py
+++ b/solution.py
@@ -500,7 +500,6 @@
     def chosen(block, behind):
         return jnp.where(far_side, behind, block)
 
-    v1_last = onward(v_last, 2)
     v2_first = onward(v_first, 4)
     w_other = exchanged(out_weight, "head", 1)
     prepared = prepare(queries, keys, values, transitions, betas, documents, scale)
@@ -509,13 +508,14 @@
     near_steps = exchanged(steps, "ctx", 1)
     v1_first = exchanged(chosen(v_first, v2_first), "ctx", 2)
     v2_last = onward(after(v_last, steps), 4)
-    k2 = [onward(own_k[0], 4)]
     q_near = exchanged(after(q_msg, near_steps), "ctx", 1)
-    joined = onward(joined_steps(place, steps, near_steps), 2)
-    w_other, v1_first, v1_last, v2_last = lax.optimization_barrier((w_other, v1_first, v1_last, v2_last))
-    k2 += [onward(after(own_k[g], v2_last), 4) for g in groups[1:]]
-    weights = weight_halves(out_weight, w_other)
-    sources = [chosen(after(own_k[g], *weights), k2[g]) for g in groups]
+    joined = joined_steps(place, steps, near_steps)
+    joined = onward(joined, 2)
+    source = chosen(v_last, after(v2_last, v1_first))
+    v1_last = exchanged(source, "ctx", 2)
+    k2 = [onward(after(block, joined, source), 4) for block in own_k]
+    weights = weight_halves(out_weight, after(w_other, joined, source))
+    sources = [chosen(after(own_k[g], v1_last, *weights), k2[g]) for g in groups]
     k1 = [exchanged(source, "ctx", 2) for source in sources]
     place = after(place, *sources)
     v1, v2 = (v1_first, v1_last), (v2_first, v2_last)

time: 126 us -> 114 us (0.905)
  starting transfers between devices: 29 us -> 13.9 us
  waiting for transfers between devices: 33.8 us -> 36.4 us
    ppermute x10 -> x11, starting transfers between devices: 23.3 us -> 10.2 us  [exchanged(): lax.ppermute(value, axis, [(i, i ^ bit) for i in range(lax.axis_size(axis...]
    ppermute x6 -> x5, waiting for transfers between devices: 14.6 us -> 21.8 us  [onward(): lax.ppermute(value, 'ctx', [(i, (i + steps) % count) for i in range(count)])]
    ppermute x10 -> x11, waiting for transfers between devices: 19.1 us -> 14.6 us  [exchanged(): lax.ppermute(value, axis, [(i, i ^ bit) for i in range(lax.axis_size(axis...]
    ppermute x6 -> x5, starting transfers between devices: 5.69 us -> 3.72 us  [onward(): lax.ppermute(value, 'ctx', [(i, (i + steps) % count) for i in range(count)])]
  transfers between devices with their start and end apart: 16 -> 16, of which waited for: 7 -> 10; matrix products, arithmetic and copies ran while one was open for 1% -> 1% of each run, Pallas kernels for 39% -> 43%
where the time goes in v2:
time: 114 us
  Pallas kernels  56.5 us (50%)
  waiting for transfers between devices  36.4 us (32%)
  starting transfers between devices  13.9 us (12%)
  local copies, waits for them, and re-layouts  6.45 us (6%)
    ppermute x5, waiting for transfers between devices, onward(): lax.ppermute(value, 'ctx', [(i, (i + steps) % count) for i in range(count)])  21.8 us
    ppermute x11, waiting for transfers between devices, exchanged(): lax.ppermute(value, axis, [(i, i ^ bit) for i in range(lax.axis_size(axis...  14.6 us
    pallas_call x1, Pallas kernels, prepare(): pl.pallas_call(functools.partial(prepare_kernel, scale=scale), grid=(head...  12.9 us
    pallas_call x2, Pallas kernels, partner_part(): pl.pallas_call(functools.partial(partner_kernel, scale=scale), grid_spec=...  12.6 us
    ppermute x11, starting transfers between devices, exchanged(): lax.ppermute(value, axis, [(i, i ^ bit) for i in range(lax.axis_size(axis...  10.2 us
    pallas_call x2, Pallas kernels, own_part(): pl.pallas_call(functools.partial(own_kernel, scale=scale), grid_spec=pltp...  9.43 us
    pallas_call x1, Pallas kernels, project(): pl.pallas_call(project_kernel, grid=(width // tile,), in_specs=a_spec + [...  7.65 us
    pallas_call x1, Pallas kernels, weight_halves(): pl.pallas_call(halves_kernel, grid=(depth // tile,), in_specs=[spec] * 2,...  7.34 us
  transfers between devices with their start and end apart: 16, of which 10 were waited for; matrix products, arithmetic and copies ran while one was open for 1% of the time, Pallas kernels for 43%

profile of v2, /device:TPU:0, one launch (start us, length us, event | category | flops | bytes accessed | tf_op | source)
XLA Modules:
  0.0 113.8 jit_solution(9555242541300089535)
XLA Ops:
  0.0 0.5 collective-permute-start.1
  0.5 1.1 slice.12
  1.5 0.0 copy-start
  1.5 2.6 %collective-permute-start = (f32[256,512]{1,0:T(8,128)S(1)}, f32[256,512]{1,0:T(8,128)S(1)}, u32[]{:S(2)}, u32[]{:S(2)}) collective-permute-start(f32[256,512]{1,0:T(8,128)S(1)} %slice.12), channel_id=1, source_target_pairs={{0,8},{2,10},{4,12},{6,14},{8,16},{10,18},{12,20},{14,22},{16,24},... | collective-permute-start | bytes 1572872 | tf_op jit(solution)/shard_map/ppermute | solution.py:476
  4.2 12.9 %prepare.1 = (f32[4,520,128]{2,1,0:T(8,128)}, f32[4,520,128]{2,1,0:T(8,128)}, f32[4,128,128]{2,1,0:T(8,128)}, f32[4,512,128]{2,1,0:T(8,128)}, f32[4,512,128]{2,1,0:T(8,128)}) custom-call(f32[512,512]{1,0:T(8,128)} %q_ref.1, f32[512,512]{1,0:T(8,128)} %k_ref.1, f32[512,512]{1,0:T(8,128)} %vo_ref.3, f32[512,512]{1,0:T(8,128)} %w_ref.1, f32[4,512]{1,0:T(4,128)} %beta_ref.1, ...), custom_call_target="tpu_custom_call" | custom-call | flops 14949999616 | bytes 1000 | tf_op jit(solution)/shard_map/prepare/pallas_call | solution.py:219
  17.1 0.0 copy-start.1
  17.1 1.7 %collective-permute-done.v2a_ref = f32[256,512]{1,0:T(8,128)S(1)} collective-permute-done((f32[256,512]{1,0:T(8,128)S(1)}, f32[256,512]{1,0:T(8,128)S(1)}, u32[]{:S(2)}, u32[]{:S(2)}) %collective-permute-start) | collective-permute-done | bytes 524320 | tf_op jit(solution)/shard_map/ppermute | solution.py:476
  18.8 0.0 collective-permute-done.1.other_ref
  18.8 0.0 copy-done
  18.8 0.1 broadcast_select_fusion.3
  18.9 0.7 copy-done.5
  19.6 0.0 collective-permute-start.4
  19.6 1.5 %collective-permute-start.5 = (f32[256,512]{1,0:T(8,128)S(1)}, f32[256,512]{1,0:T(8,128)S(1)}, u32[]{:S(2)}, u32[]{:S(2)}) collective-permute-start(f32[256,512]{1,0:T(8,128)S(1)} %get-tuple-element.73), channel_id=1, source_target_pairs={{0,4},{2,6},{4,0},{6,2},{8,12},{10,14},{12,8},{14,10},{16,20},{18,... | collective-permute-start | bytes 1572872 | tf_op jit(solution)/shard_map/ppermute | solution.py:480
  21.2 0.0 copy-done.12
  21.2 1.5 %collective-permute-start.2 = (f32[4,128,128]{2,1,0:T(8,128)S(1)}, f32[4,128,128]{2,1,0:T(8,128)S(1)}, u32[]{:S(2)}, u32[]{:S(2)}) collective-permute-start(f32[4,128,128]{2,1,0:T(8,128)S(1)} %copy-done.12), channel_id=1, source_target_pairs={{0,2},{2,0},{4,6},{6,4},{8,10},{10,8},{12,14},{14,12},{16,18},{18,... | collective-permute-start | bytes 786440 | tf_op jit(solution)/shard_map/ppermute | solution.py:480
  22.6 0.0 copy-done.1
  22.6 0.1 fusion
  22.7 6.2 %collective-permute-done.2.near_ref.s_ref = f32[4,128,128]{2,1,0:T(8,128)S(1)} collective-permute-done((f32[4,128,128]{2,1,0:T(8,128)S(1)}, f32[4,128,128]{2,1,0:T(8,128)S(1)}, u32[]{:S(2)}, u32[]{:S(2)}) %collective-permute-start.2) | collective-permute-done | bytes 262176 | tf_op jit(solution)/shard_map/ppermute | solution.py:480
  28.9 0.7 copy-done.13
  29.6 2.0 %joined_steps.1 = f32[4,128,128]{2,1,0:T(8,128)} custom-call(s32[1]{0:T(128)} %bitcast.1.place_ref, f32[4,128,128]{2,1,0:T(8,128)} %get-tuple-element.44.own_ref.s_ref, f32[4,128,128]{2,1,0:T(8,128)} %copy-done.13), custom_call_target="tpu_custom_call" | custom-call | flops 2300000000 | bytes 1000 | tf_op jit(solution)/shard_map/joined_steps/pallas_call | solution.py:250
  31.6 0.6 collective-permute-start.3
  32.2 1.4 %collective-permute-start.10 = (f32[4,520,128]{2,1,0:T(8,128)}, f32[4,520,128]{2,1,0:T(8,128)}, u32[]{:S(2)}, u32[]{:S(2)}) collective-permute-start(f32[4,520,128]{2,1,0:T(8,128)} %get-tuple-element.64.qo_ref), channel_id=1, source_target_pairs={{0,2},{2,0},{4,6},{6,4},{8,10},{10,8},{12,14},{14,12},{16,18},{18,... | collective-permute-start | bytes 3194888 | tf_op jit(solution)/shard_map/ppermute | solution.py:480
  33.6 1.5 %collective-permute-done.4.v2b_ref = f32[256,512]{1,0:T(8,128)S(1)} collective-permute-done((f32[256,512]{1,0:T(8,128)S(1)}, f32[256,512]{1,0:T(8,128)S(1)}, u32[]{:S(2)}, u32[]{:S(2)}) %collective-permute-start.4) | collective-permute-done | bytes 524320 | tf_op jit(solution)/shard_map/ppermute | solution.py:476
  35.2 0.0 collective-permute-done.5.v1a_ref
  35.2 0.1 broadcast_select_fusion.2
  35.3 1.6 %collective-permute-start.7 = (f32[256,512]{1,0:T(8,128)S(1)}, f32[256,512]{1,0:T(8,128)S(1)}, u32[]{:S(2)}, u32[]{:S(2)}) collective-permute-start(f32[256,512]{1,0:T(8,128)S(1)} %broadcast_select_fusion.2), channel_id=1, source_target_pairs={{0,4},{2,6},{4,0},{6,2},{8,12},{10,14},{12,8},{14,10},{16,20},{18,... | collective-permute-start | bytes 1572872 | tf_op jit(solution)/shard_map/ppermute | solution.py:480
  36.9 4.8 %collective-permute-done.3.u_ref = f32[4,128,128]{2,1,0:T(8,128)S(1)} collective-permute-done((f32[4,128,128]{2,1,0:T(8,128)}, f32[4,128,128]{2,1,0:T(8,128)S(1)}, u32[]{:S(2)}, u32[]{:S(2)}) %collective-permute-start.3) | collective-permute-done | bytes 262176 | tf_op jit(solution)/shard_map/ppermute | solution.py:476
  41.7 0.0 collective-permute-start.8
  41.7 7.3 %weight_halves.1 = (bf16[512,2048]{1,0:T(8,128)(2,1)}, bf16[512,2048]{1,0:T(8,128)(2,1)}, bf16[512,2048]{1,0:T(8,128)(2,1)}, bf16[512,2048]{1,0:T(8,128)(2,1)}) custom-call(f32[512,2048]{1,0:T(8,128)} %own_ref.1, f32[512,2048]{1,0:T(8,128)} %collective-permute-done.1.other_ref), custom_call_target="tpu_custom_call" | custom-call | flops 8049999872 | bytes 1000 | tf_op jit(solution)/shard_map/weight_halves/pallas_call | solution.py:432
  49.1 0.0 copy-done.10
  49.1 0.5 collective-permute-start.6
  49.6 3.3 %collective-permute-done.7.v1b_ref = f32[256,512]{1,0:T(8,128)S(1)} collective-permute-done((f32[256,512]{1,0:T(8,128)S(1)}, f32[256,512]{1,0:T(8,128)S(1)}, u32[]{:S(2)}, u32[]{:S(2)}) %collective-permute-start.7) | collective-permute-done | bytes 524320 | tf_op jit(solution)/shard_map/ppermute | solution.py:480
  52.9 5.7 %collective-permute-done.8.k2_ref = f32[2,520,128]{2,1,0:T(8,128)S(1)} collective-permute-done((f32[2,520,128]{2,1,0:T(8,128)S(1)}, f32[2,520,128]{2,1,0:T(8,128)S(1)}, u32[]{:S(2)}, u32[]{:S(2)}) %collective-permute-start.8) | collective-permute-done | bytes 532512 | tf_op jit(solution)/shard_map/ppermute | solution.py:476
  58.6 0.1 broadcast_select_fusion
  58.6 0.0 copy-done.11
  58.6 0.1 collective-permute-start.12
  58.7 8.1 %collective-permute-done.6.k2_ref = f32[2,520,128]{2,1,0:T(8,128)S(1)} collective-permute-done((f32[2,520,128]{2,1,0:T(8,128)S(1)}, f32[2,520,128]{2,1,0:T(8,128)S(1)}, u32[]{:S(2)}, u32[]{:S(2)}) %collective-permute-start.6) | collective-permute-done | bytes 532512 | tf_op jit(solution)/shard_map/ppermute | solution.py:476
  66.8 0.1 broadcast_select_fusion.1
  66.9 0.1 collective-permute-start.9
  66.9 0.0 collective-permute-done.10.qp_ref
  67.0 2.5 %collective-permute-done.12.k1_ref = f32[2,520,128]{2,1,0:T(8,128)S(1)} collective-permute-done((f32[2,520,128]{2,1,0:T(8,128)S(1)}, f32[2,520,128]{2,1,0:T(8,128)S(1)}, u32[]{:S(2)}, u32[]{:S(2)}) %collective-permute-start.12) | collective-permute-done | bytes 532512 | tf_op jit(solution)/shard_map/ppermute | solution.py:480
  69.4 0.8 copy-done.6
  70.2 6.3 %partner.3 = f32[2,520,128]{2,1,0:T(8,128)} custom-call(s32[1]{0:T(128)} %bitcast.1.place_ref, f32[4,520,128]{2,1,0:T(8,128)} %collective-permute-done.10.qp_ref, f32[4,520,128]{2,1,0:T(8,128)} %get-tuple-element.43.ko_ref, f32[512,512]{1,0:T(8,128)} %vo_ref.3, f32[2,520,128]{2,1,0:T(8,128)} %copy-done.6, f32[256,512]{1,0:T(8,128)} %copy-done.10, ...), custom_call_target="tpu_custom_call" | custom-call | flops 6899999744 | bytes 1000 | tf_op jit(solution)/shard_map/partner/pallas_call | solution.py:348
  76.6 1.6 %collective-permute-start.13 = (f32[2,520,128]{2,1,0:T(8,128)}, f32[2,520,128]{2,1,0:T(8,128)S(1)}, u32[]{:S(2)}, u32[]{:S(2)}) collective-permute-start(f32[2,520,128]{2,1,0:T(8,128)} %partner.3), channel_id=1, source_target_pairs={{0,2},{2,0},{4,6},{6,4},{8,10},{10,8},{12,14},{14,12},{16,18},{18,... | collective-permute-start | bytes 1597448 | tf_op jit(solution)/shard_map/ppermute | solution.py:480
  78.1 1.2 %collective-permute-done.9.k1_ref = f32[2,520,128]{2,1,0:T(8,128)S(1)} collective-permute-done((f32[2,520,128]{2,1,0:T(8,128)S(1)}, f32[2,520,128]{2,1,0:T(8,128)S(1)}, u32[]{:S(2)}, u32[]{:S(2)}) %collective-permute-start.9) | collective-permute-done | bytes 532512 | tf_op jit(solution)/shard_map/ppermute | solution.py:480
  79.4 0.8 copy-done.7
  80.2 6.3 %partner.2 = f32[2,520,128]{2,1,0:T(8,128)} custom-call(s32[1]{0:T(128)} %bitcast.1.place_ref, f32[4,520,128]{2,1,0:T(8,128)} %collective-permute-done.10.qp_ref, f32[4,520,128]{2,1,0:T(8,128)} %get-tuple-element.43.ko_ref, f32[512,512]{1,0:T(8,128)} %vo_ref.3, f32[2,520,128]{2,1,0:T(8,128)} %copy-done.7, f32[256,512]{1,0:T(8,128)} %copy-done.10, ...), custom_call_target="tpu_custom_call" | custom-call | flops 6899999744 | bytes 1000 | tf_op jit(solution)/shard_map/partner/pallas_call | solution.py:348
  86.5 1.5 %collective-permute-start.11 = (f32[2,520,128]{2,1,0:T(8,128)}, f32[2,520,128]{2,1,0:T(8,128)S(1)}, u32[]{:S(2)}, u32[]{:S(2)}) collective-permute-start(f32[2,520,128]{2,1,0:T(8,128)} %partner.2), channel_id=1, source_target_pairs={{0,2},{2,0},{4,6},{6,4},{8,10},{10,8},{12,14},{14,12},{16,18},{18,... | collective-permute-start | bytes 1597448 | tf_op jit(solution)/shard_map/ppermute | solution.py:480
  88.0 4.7 %own.3 = (f32[2,512,128]{2,1,0:T(8,128)}, f32[2,512,128]{2,1,0:T(8,128)}) custom-call(s32[1]{0:T(128)} %bitcast.1.place_ref, f32[4,520,128]{2,1,0:T(8,128)} %get-tuple-element.64.qo_ref, f32[2,520,128]{2,1,0:T(8,128)} %copy-done.6, f32[256,512]{1,0:T(8,128)} %copy-done.10, f32[256,512]{1,0:T(8,128)} %copy-done.11, f32[4,128,128]{2,1,0:T(8,128)} %copy-done.13, ...), custom_call_target="tpu_custom_call" | custom-call | flops 5175000064 | bytes 1000 | tf_op jit(solution)/shard_map/own/pallas_call | solution.py:369
  92.7 4.7 %own.2 = (f32[2,512,128]{2,1,0:T(8,128)}, f32[2,512,128]{2,1,0:T(8,128)}) custom-call(s32[1]{0:T(128)} %bitcast.1.place_ref, f32[4,520,128]{2,1,0:T(8,128)} %get-tuple-element.64.qo_ref, f32[2,520,128]{2,1,0:T(8,128)} %copy-done.7, f32[256,512]{1,0:T(8,128)} %copy-done.10, f32[256,512]{1,0:T(8,128)} %copy-done.11, f32[4,128,128]{2,1,0:T(8,128)} %copy-done.13, ...), custom_call_target="tpu_custom_call" | custom-call | flops 5175000064 | bytes 1000 | tf_op jit(solution)/shard_map/own/pallas_call | solution.py:369
  97.4 0.0 collective-permute-done.13.msg_ref
  97.4 0.0 copy-start.9
  97.4 0.8 copy-done.9
  98.2 2.3 %merge.3 = (f32[256,256]{1,0:T(8,128)}, f32[256,256]{1,0:T(8,128)}) custom-call(s32[1]{0:T(128)} %bitcast.core_ref, f32[2,512,128]{2,1,0:T(8,128)} %get-tuple-element.66.o_ref, f32[2,512,128]{2,1,0:T(8,128)} %get-tuple-element.67.lse_ref, f32[2,520,128]{2,1,0:T(8,128)} %copy-done.9), custom_call_target="tpu_custom_call" | custom-call | flops 2529999872 | bytes 1000 | tf_op jit(solution)/shard_map/merge/pallas_call | solution.py:408
  100.5 0.0 collective-permute-start.15
  100.5 0.0 collective-permute-done.11.msg_ref
  100.5 0.0 copy-start.8
  100.5 0.8 copy-done.8
  101.3 2.3 %merge.2 = (f32[256,256]{1,0:T(8,128)}, f32[256,256]{1,0:T(8,128)}) custom-call(s32[1]{0:T(128)} %bitcast.core_ref, f32[2,512,128]{2,1,0:T(8,128)} %get-tuple-element.62.o_ref, f32[2,512,128]{2,1,0:T(8,128)} %get-tuple-element.63.lse_ref, f32[2,520,128]{2,1,0:T(8,128)} %copy-done.8), custom_call_target="tpu_custom_call" | custom-call | flops 2529999872 | bytes 1000 | tf_op jit(solution)/shard_map/merge/pallas_call | solution.py:408
  103.6 0.5 collective-permute-start.14
  104.1 0.0 collective-permute-done.15.refs_3_
  104.1 1.4 %collective-permute-done.14.refs_2_ = f32[256,256]{1,0:T(8,128)S(1)} collective-permute-done((f32[256,256]{1,0:T(8,128)}, f32[256,256]{1,0:T(8,128)S(1)}, u32[]{:S(2)}, u32[]{:S(2)}) %collective-permute-start.14) | collective-permute-done | bytes 262176 | tf_op jit(solution)/shard_map/ppermute | solution.py:480
  105.4 0.7 copy-done.16
  106.1 7.7 %project.1 = f32[256,2048]{1,0:T(8,128)} custom-call(f32[256,256]{1,0:T(8,128)} %get-tuple-element.65.refs_0_, f32[256,256]{1,0:T(8,128)} %get-tuple-element.68.refs_1_, f32[256,256]{1,0:T(8,128)} %copy-done.16, f32[256,256]{1,0:T(8,128)} %copy-done.15, bf16[512,2048]{1,0:T(8,128)(2,1)} %get-tuple-element.51.refs_4_, ...), custom_call_target="tpu_custom_call" | custom-call | flops 8625000448 | bytes 1000 | tf_op jit(solution)/shard_map/project/pallas_call | solution.py:462
  (18 shorter events, 0.0 us)
Async XLA Ops:
  0.0 18.8 %collective-permute-start.1 = (f32[512,2048]{1,0:T(8,128)}, f32[512,2048]{1,0:T(8,128)}, u32[]{:S(2)}, u32[]{:S(2)}) collective-permute-start(f32[512,2048]{1,0:T(8,128)} %own_ref.1), channel_id=1, source_target_pairs={{0,1},{1,0},{2,3},{3,2},{4,5},{5,4},{6,7},{7,6},{8,9},{9,8},{10,11... | collective-permute-start | bytes 12582920 | tf_op jit(solution)/shard_map/ppermute | solution.py:480
  1.5 17.3 %copy-start = (f32[512,512]{1,0:T(8,128)S(1)}, f32[512,512]{1,0:T(8,128)}, u32[]{:S(2)}) copy-start(f32[512,512]{1,0:T(8,128)} %vo_ref.3) | copy-start | bytes 3145732
  1.5 17.2 %collective-permute-start = (f32[256,512]{1,0:T(8,128)S(1)}, f32[256,512]{1,0:T(8,128)S(1)}, u32[]{:S(2)}, u32[]{:S(2)}) collective-permute-start(f32[256,512]{1,0:T(8,128)S(1)} %slice.12), channel_id=1, source_target_pairs={{0,8},{2,10},{4,12},{6,14},{8,16},{10,18},{12,20},{14,22},{16,24},... | collective-permute-start | bytes 1572872 | tf_op jit(solution)/shard_map/ppermute | solution.py:476
  17.1 4.1 %copy-start.12 = (f32[4,128,128]{2,1,0:T(8,128)S(1)}, f32[4,128,128]{2,1,0:T(8,128)}, u32[]{:S(2)}) copy-start(f32[4,128,128]{2,1,0:T(8,128)} %get-tuple-element.44.own_ref.s_ref) | copy-start | bytes 786436
  17.1 5.5 %copy-start.1 = (f32[4,520,128]{2,1,0:T(8,128)S(1)}, f32[4,520,128]{2,1,0:T(8,128)}, u32[]{:S(2)}) copy-start(f32[4,520,128]{2,1,0:T(8,128)} %get-tuple-element.43.ko_ref) | copy-start | bytes 3194884
  18.8 0.8 copy-start.5
  19.6 15.6 %collective-permute-start.4 = (f32[256,512]{1,0:T(8,128)S(1)}, f32[256,512]{1,0:T(8,128)S(1)}, u32[]{:S(2)}, u32[]{:S(2)}) collective-permute-start(f32[256,512]{1,0:T(8,128)S(1)} %get-tuple-element.45), channel_id=1, source_target_pairs={{0,8},{2,10},{4,12},{6,14},{8,16},{10,18},{12,20},{14,22},{16,24},... | collective-permute-start | bytes 1572872 | tf_op jit(solution)/shard_map/ppermute | solution.py:476
  19.6 15.6 %collective-permute-start.5 = (f32[256,512]{1,0:T(8,128)S(1)}, f32[256,512]{1,0:T(8,128)S(1)}, u32[]{:S(2)}, u32[]{:S(2)}) collective-permute-start(f32[256,512]{1,0:T(8,128)S(1)} %get-tuple-element.73), channel_id=1, source_target_pairs={{0,4},{2,6},{4,0},{6,2},{8,12},{10,14},{12,8},{14,10},{16,20},{18,... | collective-permute-start | bytes 1572872 | tf_op jit(solution)/shard_map/ppermute | solution.py:480
  21.2 7.8 %collective-permute-start.2 = (f32[4,128,128]{2,1,0:T(8,128)S(1)}, f32[4,128,128]{2,1,0:T(8,128)S(1)}, u32[]{:S(2)}, u32[]{:S(2)}) collective-permute-start(f32[4,128,128]{2,1,0:T(8,128)S(1)} %copy-done.12), channel_id=1, source_target_pairs={{0,2},{2,0},{4,6},{6,4},{8,10},{10,8},{12,14},{14,12},{16,18},{18,... | collective-permute-start | bytes 786440 | tf_op jit(solution)/shard_map/ppermute | solution.py:480
  28.9 0.7 copy-start.13
  31.6 10.1 %collective-permute-start.3 = (f32[4,128,128]{2,1,0:T(8,128)}, f32[4,128,128]{2,1,0:T(8,128)S(1)}, u32[]{:S(2)}, u32[]{:S(2)}) collective-permute-start(f32[4,128,128]{2,1,0:T(8,128)} %joined_steps.1), channel_id=1, source_target_pairs={{0,4},{2,6},{4,8},{6,10},{8,12},{10,14},{12,16},{14,18},{16,20},{1... | collective-permute-start | bytes 786440 | tf_op jit(solution)/shard_map/ppermute | solution.py:476
  32.2 34.7 %collective-permute-start.10 = (f32[4,520,128]{2,1,0:T(8,128)}, f32[4,520,128]{2,1,0:T(8,128)}, u32[]{:S(2)}, u32[]{:S(2)}) collective-permute-start(f32[4,520,128]{2,1,0:T(8,128)} %get-tuple-element.64.qo_ref), channel_id=1, source_target_pairs={{0,2},{2,0},{4,6},{6,4},{8,10},{10,8},{12,14},{14,12},{16,18},{18,... | collective-permute-start | bytes 3194888 | tf_op jit(solution)/shard_map/ppermute | solution.py:480
  35.2 13.9 %copy-start.4 = (f32[256,512]{1,0:T(8,128)}, f32[256,512]{1,0:T(8,128)S(1)}, u32[]{:S(2)}) copy-start(f32[256,512]{1,0:T(8,128)S(1)} %collective-permute-done.4.v2b_ref) | copy-start | bytes 1572868
  35.2 13.9 %copy-start.10 = (f32[256,512]{1,0:T(8,128)}, f32[256,512]{1,0:T(8,128)S(1)}, u32[]{:S(2)}) copy-start(f32[256,512]{1,0:T(8,128)S(1)} %collective-permute-done.5.v1a_ref) | copy-start | bytes 1572868
  35.3 17.6 %collective-permute-start.7 = (f32[256,512]{1,0:T(8,128)S(1)}, f32[256,512]{1,0:T(8,128)S(1)}, u32[]{:S(2)}, u32[]{:S(2)}) collective-permute-start(f32[256,512]{1,0:T(8,128)S(1)} %broadcast_select_fusion.2), channel_id=1, source_target_pairs={{0,4},{2,6},{4,0},{6,2},{8,12},{10,14},{12,8},{14,10},{16,20},{18,... | collective-permute-start | bytes 1572872 | tf_op jit(solution)/shard_map/ppermute | solution.py:480
  41.7 7.4 %copy-start.14 = (f32[4,128,128]{2,1,0:T(8,128)}, f32[4,128,128]{2,1,0:T(8,128)S(1)}, u32[]{:S(2)}) copy-start(f32[4,128,128]{2,1,0:T(8,128)S(1)} %collective-permute-done.3.u_ref) | copy-start | bytes 786436
  41.7 16.8 %collective-permute-start.8 = (f32[2,520,128]{2,1,0:T(8,128)S(1)}, f32[2,520,128]{2,1,0:T(8,128)S(1)}, u32[]{:S(2)}, u32[]{:S(2)}) collective-permute-start(f32[2,520,128]{2,1,0:T(8,128)S(1)} %get-tuple-element.57), channel_id=1, source_target_pairs={{0,8},{2,10},{4,12},{6,14},{8,16},{10,18},{12,20},{14,22},{16,24},... | collective-permute-start | bytes 1597448 | tf_op jit(solution)/shard_map/ppermute | solution.py:476
  49.1 17.7 %collective-permute-start.6 = (f32[2,520,128]{2,1,0:T(8,128)S(1)}, f32[2,520,128]{2,1,0:T(8,128)S(1)}, u32[]{:S(2)}, u32[]{:S(2)}) collective-permute-start(f32[2,520,128]{2,1,0:T(8,128)S(1)} %get-tuple-element.55), channel_id=1, source_target_pairs={{0,8},{2,10},{4,12},{6,14},{8,16},{10,18},{12,20},{14,22},{16,24},... | collective-permute-start | bytes 1597448 | tf_op jit(solution)/shard_map/ppermute | solution.py:476
  52.9 5.8 %copy-start.11 = (f32[256,512]{1,0:T(8,128)}, f32[256,512]{1,0:T(8,128)S(1)}, u32[]{:S(2)}) copy-start(f32[256,512]{1,0:T(8,128)S(1)} %collective-permute-done.7.v1b_ref) | copy-start | bytes 1572868
  58.6 10.9 %copy-start.3 = (f32[2,520,128]{2,1,0:T(8,128)}, f32[2,520,128]{2,1,0:T(8,128)S(1)}, u32[]{:S(2)}) copy-start(f32[2,520,128]{2,1,0:T(8,128)S(1)} %collective-permute-done.8.k2_ref) | copy-start | bytes 1597444
  58.6 10.8 %collective-permute-start.12 = (f32[2,520,128]{2,1,0:T(8,128)S(1)}, f32[2,520,128]{2,1,0:T(8,128)S(1)}, u32[]{:S(2)}, u32[]{:S(2)}) collective-permute-start(f32[2,520,128]{2,1,0:T(8,128)S(1)} %broadcast_select_fusion), channel_id=1, source_target_pairs={{0,4},{2,6},{4,0},{6,2},{8,12},{10,14},{12,8},{14,10},{16,20},{18,... | collective-permute-start | bytes 1597448 | tf_op jit(solution)/shard_map/ppermute | solution.py:480
  66.8 9.8 %copy-start.2 = (f32[2,520,128]{2,1,0:T(8,128)}, f32[2,520,128]{2,1,0:T(8,128)S(1)}, u32[]{:S(2)}) copy-start(f32[2,520,128]{2,1,0:T(8,128)S(1)} %collective-permute-done.6.k2_ref) | copy-start | bytes 1597444
  66.9 12.5 %collective-permute-start.9 = (f32[2,520,128]{2,1,0:T(8,128)S(1)}, f32[2,520,128]{2,1,0:T(8,128)S(1)}, u32[]{:S(2)}, u32[]{:S(2)}) collective-permute-start(f32[2,520,128]{2,1,0:T(8,128)S(1)} %broadcast_select_fusion.1), channel_id=1, source_target_pairs={{0,4},{2,6},{4,0},{6,2},{8,12},{10,14},{12,8},{14,10},{16,20},{18,... | collective-permute-start | bytes 1597448 | tf_op jit(solution)/shard_map/ppermute | solution.py:480
  69.4 0.8 copy-start.6
  76.6 20.9 %collective-permute-start.13 = (f32[2,520,128]{2,1,0:T(8,128)}, f32[2,520,128]{2,1,0:T(8,128)S(1)}, u32[]{:S(2)}, u32[]{:S(2)}) collective-permute-start(f32[2,520,128]{2,1,0:T(8,128)} %partner.3), channel_id=1, source_target_pairs={{0,2},{2,0},{4,6},{6,4},{8,10},{10,8},{12,14},{14,12},{16,18},{18,... | collective-permute-start | bytes 1597448 | tf_op jit(solution)/shard_map/ppermute | solution.py:480
  79.4 0.8 copy-start.7
  86.5 14.0 %collective-permute-start.11 = (f32[2,520,128]{2,1,0:T(8,128)}, f32[2,520,128]{2,1,0:T(8,128)S(1)}, u32[]{:S(2)}, u32[]{:S(2)}) collective-permute-start(f32[2,520,128]{2,1,0:T(8,128)} %partner.2), channel_id=1, source_target_pairs={{0,2},{2,0},{4,6},{6,4},{8,10},{10,8},{12,14},{14,12},{16,18},{18,... | collective-permute-start | bytes 1597448 | tf_op jit(solution)/shard_map/ppermute | solution.py:480
  97.4 0.8 copy-start.9
  100.5 3.6 %collective-permute-start.15 = (f32[256,256]{1,0:T(8,128)}, f32[256,256]{1,0:T(8,128)S(1)}, u32[]{:S(2)}, u32[]{:S(2)}) collective-permute-start(f32[256,256]{1,0:T(8,128)} %get-tuple-element.70), channel_id=1, source_target_pairs={{0,1},{1,0},{2,3},{3,2},{4,5},{5,4},{6,7},{7,6},{8,9},{9,8},{10,11... | collective-permute-start | bytes 786440 | tf_op jit(solution)/shard_map/ppermute | solution.py:480
  100.5 0.8 copy-start.8
  103.6 1.9 %collective-permute-start.14 = (f32[256,256]{1,0:T(8,128)}, f32[256,256]{1,0:T(8,128)S(1)}, u32[]{:S(2)}, u32[]{:S(2)}) collective-permute-start(f32[256,256]{1,0:T(8,128)} %get-tuple-element.69), channel_id=1, source_target_pairs={{0,1},{1,0},{2,3},{3,2},{4,5},{5,4},{6,7},{7,6},{8,9},{9,8},{10,11... | collective-permute-start | bytes 786440 | tf_op jit(solution)/shard_map/ppermute | solution.py:480
  104.1 1.4 %copy-start.15 = (f32[256,256]{1,0:T(8,128)}, f32[256,256]{1,0:T(8,128)S(1)}, u32[]{:S(2)}) copy-start(f32[256,256]{1,0:T(8,128)S(1)} %collective-permute-done.15.refs_3_) | copy-start | bytes 786436
  105.4 0.7 copy-start.16

commit v3 on v2

--- a/solution.py
+++ b/solution.py
@@ -13,9 +13,11 @@
 SEED = 16
 BATCH = 2
 ROWS = 256
+TILE = 512
 GROUPS = 2
 FAR = -1e30
-VMEM_BYTES = 56 * 2**20
+VMEM_BYTES = 36 * 2**20
+PREPARE_BYTES = 60 * 2**20
 COST = 1.15e9
 
 
@@ -232,7 +234,7 @@
             jax.ShapeDtypeStruct((heads, length, dh), f32),
             jax.ShapeDtypeStruct((heads, length, dh), f32),
         ],
-        compiler_params=pltpu.CompilerParams(vmem_limit_bytes=VMEM_BYTES),
+        compiler_params=pltpu.CompilerParams(vmem_limit_bytes=PREPARE_BYTES),
         name="prepare",
         cost_estimate=lasting(13),
     )(queries, keys, values, transitions, betas, documents)
@@ -269,38 +271,54 @@
     return jnp.where(wide == row, scores, FAR)
 
 
-def partner_kernel(
-    place_ref, qp_ref, ko_ref, vo_ref, k1_ref, v1a_ref, v1b_ref, k2_ref, v2a_ref, v2b_ref, s_ref, u_ref, msg_ref, *, scale
-):
-    length = vo_ref.shape[0]
+def attended_part(query, keys, values, docs, col):
+    parts = []
+    for start in range(0, query.shape[0], ROWS):
+        span = slice(start, start + ROWS)
+        parts.append((span, *softmax_part(masked(scored(query[span], keys), col[span], docs), values)))
+    return parts
+
+
+def joined_parts(out, lse, other, other_lse):
+    peak = jnp.maximum(lse, other_lse)
+    w, w_other = jnp.exp2(lse - peak), jnp.exp2(other_lse - peak)
+    total = w + w_other
+    return (out * w + other * w_other) / total, peak + jnp.log2(total)
+
+
+def early_kernel(place_ref, qp_ref, ko_ref, vo_ref, k2_ref, v2a_ref, v2b_ref, u_ref, out_ref, lse_ref, *, scale):
+    length, dh = vo_ref.shape
     place = place_ref[0]
-    even = lax.rem(place, 2) == 0
-    pick = lambda a, b: jnp.where(even, a, b)
+    pick = lambda a, b: jnp.where(lax.rem(place, 2) == 0, a, b)
+    docs = pick(doc_line(ko_ref, length, True), doc_line(k2_ref, length, place >= 4))
+    keys = stacked_keys(pick(ko_ref[0, :length, :], mm(k2_ref[0, :length, :], u_ref[0])))
+    values = stacked_values(
+        pick(vo_ref[...], jnp.concatenate([v2a_ref[...], v2b_ref[...]], axis=0))
+    )
+    query = stacked_queries(qp_ref[0, :length, :] * scale)
+    col = columns_of(doc_line(qp_ref, length, True))
+    for span, out, lse in attended_part(query, keys, values, docs, col):
+        out_ref[0, span, :] = out
+        lse_ref[0, span, :] = jnp.broadcast_to(lse, (ROWS, dh))
+
+
+def late_kernel(place_ref, qp_ref, k1_ref, v1a_ref, v1b_ref, s_ref, u_ref, oe_ref, le_ref, msg_ref, *, scale):
+    length = oe_ref.shape[1]
+    place = place_ref[0]
+    pick = lambda a, b: jnp.where(lax.rem(place, 2) == 0, a, b)
+    docs = doc_line(k1_ref, length, place >= 2)
     k1 = k1_ref[0, :length, :]
-    v1 = jnp.concatenate([v1a_ref[...], v1b_ref[...]], axis=0)
-    v2 = jnp.concatenate([v2a_ref[...], v2b_ref[...]], axis=0)
-    near, far = place >= 2, place >= 4
-    doc_1 = doc_line(k1_ref, length, near)
-    docs = jnp.concatenate(
-        [pick(doc_line(ko_ref, length, True), doc_1), pick(doc_1, doc_line(k2_ref, length, far))], axis=1
-    )
-    keys_a = stacked_keys(pick(ko_ref[0, :length, :], k1))
-    keys_b = stacked_keys(mm(pick(k1, k2_ref[0, :length, :]), u_ref[0]))
-    values = jnp.concatenate(
-        [stacked_values(pick(vo_ref[...], v1)), stacked_values(pick(v1, v2))], axis=0
-    )
+    keys = stacked_keys(pick(mm(k1, u_ref[0]), k1))
+    values = stacked_values(jnp.concatenate([v1a_ref[...], v1b_ref[...]], axis=0))
     query = qp_ref[0, :length, :] * scale
-    query_a = stacked_queries(query)
-    query_b = stacked_queries(pick(mm_nt(query, s_ref[0]), query))
+    query = stacked_queries(pick(mm_nt(query, s_ref[0]), query))
     col = columns_of(doc_line(qp_ref, length, True))
-    for start in range(0, length, ROWS):
-        span = slice(start, start + ROWS)
-        scores = jnp.concatenate([scored(query_a[span], keys_a), scored(query_b[span], keys_b)], axis=1)
-        out, lse = softmax_part(masked(scores, col[span], docs), values)
+    for span, out, lse in attended_part(query, keys, values, docs, col):
+        out, lse = joined_parts(out, lse, oe_ref[0, span, :], le_ref[0, span, :])
         msg_ref[0, span, :] = out
         for i in range(0, ROWS, PIECE):
-            line = length + (start + i) // PIECE
-            msg_ref[0, line : line + 1, :] = jnp.broadcast_to(lse[i : i + PIECE], (PIECE, PIECE)).T[:1]
+            line = length + (span.start + i) // PIECE
+            msg_ref[0, line : line + 1, :] = lse[i : i + PIECE].T[:1]
     first = length + length // PIECE
     msg_ref[0, first:, :] = jnp.zeros((msg_ref.shape[1] - first, msg_ref.shape[2]), jnp.float32)
 
@@ -317,15 +335,10 @@
     query = qo_ref[0, :length, :] * scale
     query = stacked_queries(pick(query, mm_nt(query, s_ref[0])))
     col = columns_of(doc_line(qo_ref, length, True))
-    for start in range(0, length, ROWS):
-        span = slice(start, start + ROWS)
-        out, lse = softmax_part(masked(scored(query[span], keys), col[span], docs), values)
-        lse_d = ld_ref[0, span, :]
-        peak = jnp.maximum(lse, lse_d)
-        w, w_d = jnp.exp2(lse - peak), jnp.exp2(lse_d - peak)
-        total = w + w_d
-        out_ref[0, span, :] = (out * w + od_ref[0, span, :] * w_d) / total
-        lse_ref[0, span, :] = peak + jnp.log2(total)
+    for span, out, lse in attended_part(query, keys, values, docs, col):
+        out, lse = joined_parts(out, lse, od_ref[0, span, :], ld_ref[0, span, :])
+        out_ref[0, span, :] = out
+        lse_ref[0, span, :] = lse
 
 
 def cross_specs(group, per_group, length, rows, dh):
@@ -340,13 +353,34 @@
     }
 
 
-def partner_part(group, per_group, place, q_near, k_own, values, k1, v1, k2, v2, steps, joined, scale):
+def early_part(group, per_group, place, q_near, k_own, values, k2, v2, joined, scale):
     length = values.shape[0]
     _, rows, dh = q_near.shape
     spec = cross_specs(group, per_group, length, rows, dh)
-    names = ["all", "all", "all_values", "part"] + ["half_values"] * 2 + ["part"] + ["half_values"] * 2 + ["step"] * 2
-    return pl.pallas_call(
-        functools.partial(partner_kernel, scale=scale),
+    names = ["all", "all", "all_values", "part", "half_values", "half_values", "step"]
+    shape = jax.ShapeDtypeStruct((per_group, length, dh), jnp.float32)
+    return pl.pallas_call(
+        functools.partial(early_kernel, scale=scale),
+        grid_spec=pltpu.PrefetchScalarGridSpec(
+            num_scalar_prefetch=1,
+            grid=(per_group,),
+            in_specs=[spec[name] for name in names],
+            out_specs=[spec["plain"], spec["plain"]],
+        ),
+        out_shape=[shape, shape],
+        compiler_params=pltpu.CompilerParams(vmem_limit_bytes=VMEM_BYTES),
+        name="early",
+        cost_estimate=lasting(4.5),
+    )(place, q_near, k_own, values, k2, *v2, joined)
+
+
+def late_part(group, per_group, place, q_near, k1, v1, steps, joined, early, scale):
+    _, rows, dh = q_near.shape
+    length = early[0].shape[1]
+    spec = cross_specs(group, per_group, length, rows, dh)
+    names = ["all", "part", "half_values", "half_values", "step", "step", "plain", "plain"]
+    return pl.pallas_call(
+        functools.partial(late_kernel, scale=scale),
         grid_spec=pltpu.PrefetchScalarGridSpec(
             num_scalar_prefetch=1,
             grid=(per_group,),
@@ -355,9 +389,9 @@
         ),
         out_shape=jax.ShapeDtypeStruct((per_group, rows, dh), jnp.float32),
         compiler_params=pltpu.CompilerParams(vmem_limit_bytes=VMEM_BYTES),
-        name="partner",
-        cost_estimate=lasting(6),
-    )(place, q_near, k_own, values, k1, *v1, k2, *v2, steps, joined)
+        name="late",
+        cost_estimate=lasting(4.5),
+    )(place, q_near, k1, *v1, steps, joined, *early)
 
 
 def own_part(group, per_group, place, q_own, k1, v1, near_steps, joined, od, ld, scale):
@@ -422,19 +456,20 @@
 
 def halves_kernel(own_ref, other_ref, *out_refs):
     for ref, (high, low) in zip((own_ref, other_ref), (out_refs[:2], out_refs[2:])):
-        high[...], low[...] = split(ref[...])
+        high[pl.program_id(0)], low[pl.program_id(0)] = split(ref[...])
 
 
 def weight_halves(w_own, w_other):
     depth, width = w_own.shape
-    tile = depth // 4
-    spec = pl.BlockSpec((tile, width), lambda n: (n, 0))
+    tile = min(width, TILE)
+    spec = pl.BlockSpec((depth, tile), lambda n: (0, n))
+    kept = pl.BlockSpec(memory_space=pltpu.VMEM)
     return pl.pallas_call(
         halves_kernel,
-        grid=(depth // tile,),
+        grid=(width // tile,),
         in_specs=[spec] * 2,
-        out_specs=[spec] * 4,
-        out_shape=[jax.ShapeDtypeStruct((depth, width), jnp.bfloat16)] * 4,
+        out_specs=[kept] * 4,
+        out_shape=[pltpu.VMEM((width // tile, depth, tile), jnp.bfloat16)] * 4,
         compiler_params=pltpu.CompilerParams(vmem_limit_bytes=VMEM_BYTES),
         name="weight_halves",
         cost_estimate=lasting(7),
@@ -447,21 +482,21 @@
     parts = []
     for part, high, low in ((a_refs[:half], own_high, own_low), (a_refs[half:], other_high, other_low)):
         a_high, a_low = split(jnp.concatenate([r[...] for r in part], axis=1))
-        stacked = scored(jnp.concatenate([a_high, a_low], axis=0), high[...])
+        stacked = scored(jnp.concatenate([a_high, a_low], axis=0), high[pl.program_id(0)])
         rows = a_high.shape[0]
-        parts.append(stacked[:rows] + (stacked[rows:] + scored(a_high, low[...])))
+        parts.append(stacked[:rows] + (stacked[rows:] + scored(a_high, low[pl.program_id(0)])))
     out_ref[...] = parts[0] + parts[1]
 
 
 def project(kept, received, weights):
     share = kept[0].shape[0]
-    depth, width = weights[0].shape
-    tile = min(width, 512)
+    tiles, depth, tile = weights[0].shape
+    width = tiles * tile
     a_spec = [pl.BlockSpec(a.shape, lambda n: (0, 0)) for a in kept + received]
-    w_spec = pl.BlockSpec((depth, tile), lambda n: (0, n))
+    w_spec = pl.BlockSpec(memory_space=pltpu.VMEM)
     return pl.pallas_call(
         project_kernel,
-        grid=(width // tile,),
+        grid=(tiles,),
         in_specs=a_spec + [w_spec] * 4,
         out_specs=pl.BlockSpec((share, tile), lambda n: (0, n)),
         out_shape=jax.ShapeDtypeStruct((share, width), jnp.float32),
@@ -515,13 +550,18 @@
     v1_last = exchanged(source, "ctx", 2)
     k2 = [onward(after(block, joined, source), 4) for block in own_k]
     weights = weight_halves(out_weight, after(w_other, joined, source))
-    sources = [chosen(after(own_k[g], v1_last, *weights), k2[g]) for g in groups]
+    sources = [chosen(after(own_k[0], v1_last), k2[0])]
+    v1, v2 = (v1_first, v1_last), (v2_first, v2_last)
+    early = []
+    for g in groups:
+        if g:
+            sources.append(chosen(after(own_k[g], early[-1][0]), k2[g]))
+        ready = after(place, sources[g], *weights)
+        early.append(early_part(g, per_group, ready, q_near, k_msg, values, k2[g], v2, joined, scale))
     k1 = [exchanged(source, "ctx", 2) for source in sources]
-    place = after(place, *sources)
-    v1, v2 = (v1_first, v1_last), (v2_first, v2_last)
     kept, received = [], []
     for g in groups:
-        msg = partner_part(g, per_group, place, q_near, k_msg, values, k1[g], v1, k2[g], v2, steps, joined, scale)
+        msg = late_part(g, per_group, place, q_near, k1[g], v1, steps, joined, early[g], scale)
         out, lse = own_part(g, per_group, place, q_msg, k1[g], v1, near_steps, joined, od, ld, scale)
         keep, send = merge(core, out, lse, exchanged(msg, "ctx", 1))
         kept.append(keep)

time: 114 us -> 106 us (0.930)
  Pallas kernels: 56.5 us -> 43.6 us
  waiting for transfers between devices: 36.4 us -> 43.8 us
  local copies, waits for them, and re-layouts: 6.45 us -> 2.71 us
    ppermute x11, waiting for transfers between devices: 14.6 us -> 23.3 us  [exchanged(): lax.ppermute(value, axis, [(i, i ^ bit) for i in range(lax.axis_size(axis...]
    pallas_call x4 -> x6, Pallas kernels: 27.6 us -> 22.6 us  [the longest x2 7.26 us: late_part(): pl.pallas_call(functools.partial(late_kernel, scale=scale), grid_spec=plt...]
    unnamed x34 -> x28, local copies, waits for them, and re-layouts: 5.3 us -> 1.56 us
    pallas_call x2, Pallas kernels: 4.53 us -> 0.93 us  [merge(): pl.pallas_call(merge_kernel, grid_spec=pltpu.PrefetchScalarGridSpec(num_s...]
    pallas_call x2, Pallas kernels: 9.43 us -> 6.92 us  [own_part(): pl.pallas_call(functools.partial(own_kernel, scale=scale), grid_spec=pltp...]
    pallas_call x1, Pallas kernels: 2 us -> 0.26 us  [joined_steps(): pl.pallas_call(steps_kernel, grid_spec=pltpu.PrefetchScalarGridSpec(num_s...]
    ppermute x5, waiting for transfers between devices: 21.8 us -> 20.4 us  [onward(): lax.ppermute(value, 'ctx', [(i, (i + steps) % count) for i in range(count)])]
  transfers between devices with their start and end apart: 16 -> 16, of which waited for: 10 -> 9; matrix products, arithmetic and copies ran while one was open for 1% -> 1% of each run, Pallas kernels for 43% -> 37%
where the time goes in v3:
time: 106 us
  waiting for transfers between devices  43.8 us (41%)
  Pallas kernels  43.6 us (41%)
  starting transfers between devices  14.3 us (13%)
  local copies, waits for them, and re-layouts  2.71 us (3%)
  other arithmetic  1.44 us (1%)
    ppermute x11, waiting for transfers between devices, exchanged(): lax.ppermute(value, axis, [(i, i ^ bit) for i in range(lax.axis_size(axis...  23.3 us
    ppermute x5, waiting for transfers between devices, onward(): lax.ppermute(value, 'ctx', [(i, (i + steps) % count) for i in range(count)])  20.4 us
    pallas_call x1, Pallas kernels, prepare(): pl.pallas_call(functools.partial(prepare_kernel, scale=scale), grid=(head...  12.9 us
    ppermute x11, starting transfers between devices, exchanged(): lax.ppermute(value, axis, [(i, i ^ bit) for i in range(lax.axis_size(axis...  10.8 us
    pallas_call x2, Pallas kernels, late_part(): pl.pallas_call(functools.partial(late_kernel, scale=scale), grid_spec=plt...  7.26 us
    pallas_call x2, Pallas kernels, early_part(): pl.pallas_call(functools.partial(early_kernel, scale=scale), grid_spec=pl...  6.99 us
    pallas_call x2, Pallas kernels, own_part(): pl.pallas_call(functools.partial(own_kernel, scale=scale), grid_spec=pltp...  6.92 us
    pallas_call x1, Pallas kernels, project(): pl.pallas_call(project_kernel, grid=(tiles,), in_specs=a_spec + [w_spec]...  4.72 us
  transfers between devices with their start and end apart: 16, of which 9 were waited for; matrix products, arithmetic and copies ran while one was open for 1% of the time, Pallas kernels for 37%

profile of v3, /device:TPU:0, one launch (start us, length us, event | category | flops | bytes accessed | tf_op | source)
XLA Modules:
  0.0 106.1 jit_solution(10467425918429137048)
XLA Ops:
  0.0 0.5 collective-permute-start.1
  0.5 1.1 %slice.12 = f32[256,512]{1,0:T(8,128)S(1)} slice(f32[512,512]{1,0:T(8,128)} %vo_ref.3), slice={[0:256], [0:512]} | slice | bytes 1048576 | tf_op jit(solution)/shard_map/slice | solution.py:533
  1.5 0.0 copy-start
  1.5 2.6 %collective-permute-start = (f32[256,512]{1,0:T(8,128)S(1)}, f32[256,512]{1,0:T(8,128)S(1)}, u32[]{:S(2)}, u32[]{:S(2)}) collective-permute-start(f32[256,512]{1,0:T(8,128)S(1)} %slice.12), channel_id=1, source_target_pairs={{0,8},{2,10},{4,12},{6,14},{8,16},{10,18},{12,20},{14,22},{16,24},... | collective-permute-start | bytes 1572872 | tf_op jit(solution)/shard_map/ppermute | solution.py:511
  4.2 12.9 %prepare.1 = (f32[4,520,128]{2,1,0:T(8,128)}, f32[4,520,128]{2,1,0:T(8,128)}, f32[4,128,128]{2,1,0:T(8,128)}, f32[4,512,128]{2,1,0:T(8,128)}, f32[4,512,128]{2,1,0:T(8,128)}) custom-call(f32[512,512]{1,0:T(8,128)} %q_ref.1, f32[512,512]{1,0:T(8,128)} %k_ref.1, f32[512,512]{1,0:T(8,128)} %vo_ref.3, f32[512,512]{1,0:T(8,128)} %w_ref.1, f32[4,512]{1,0:T(4,128)} %beta_ref.1, ...), custom_call_target="tpu_custom_call" | custom-call | flops 14949999616 | bytes 1000 | tf_op jit(solution)/shard_map/prepare/pallas_call | solution.py:221
  17.1 0.0 copy-start.1
  17.1 1.7 %collective-permute-done.v2a_ref = f32[256,512]{1,0:T(8,128)S(1)} collective-permute-done((f32[256,512]{1,0:T(8,128)S(1)}, f32[256,512]{1,0:T(8,128)S(1)}, u32[]{:S(2)}, u32[]{:S(2)}) %collective-permute-start) | collective-permute-done | bytes 524320 | tf_op jit(solution)/shard_map/ppermute | solution.py:511
  18.8 0.0 collective-permute-done.1.other_ref
  18.8 0.0 copy-done
  18.8 1.2 %broadcast_select_fusion.3 = (f32[256,512]{1,0:T(8,128)}, f32[256,512]{1,0:T(8,128)}) fusion(f32[256,512]{1,0:T(8,128)S(1)} %collective-permute-done.v2a_ref, pred[]{:T(512)S(6)} %ge.3, f32[512,512]{1,0:T(8,128)S(1)} %copy-done), kind=kLoop, calls=%fused_computation.3 | loop fusion | flops 131072 | bytes 2621441 | tf_op jit(solution)/shard_map/jit(_where)/select_n | solution.py:536
  20.0 0.0 collective-permute-start.4
  20.0 1.5 %collective-permute-start.5 = (f32[256,512]{1,0:T(8,128)}, f32[256,512]{1,0:T(8,128)}, u32[]{:S(2)}, u32[]{:S(2)}) collective-permute-start(f32[256,512]{1,0:T(8,128)} %get-tuple-element.83), channel_id=1, source_target_pairs={{0,4},{2,6},{4,0},{6,2},{8,12},{10,14},{12,8},{14,10},{16,20},{18,... | collective-permute-start | bytes 1572872 | tf_op jit(solution)/shard_map/ppermute | solution.py:515
  21.5 0.0 copy-done.7
  21.5 1.5 %collective-permute-start.2 = (f32[4,128,128]{2,1,0:T(8,128)S(1)}, f32[4,128,128]{2,1,0:T(8,128)S(1)}, u32[]{:S(2)}, u32[]{:S(2)}) collective-permute-start(f32[4,128,128]{2,1,0:T(8,128)S(1)} %copy-done.7), channel_id=1, source_target_pairs={{0,2},{2,0},{4,6},{6,4},{8,10},{10,8},{12,14},{14,12},{16,18},{18,... | collective-permute-start | bytes 786440 | tf_op jit(solution)/shard_map/ppermute | solution.py:515
  23.0 0.0 copy-done.1
  23.0 0.1 fusion
  23.1 6.2 %collective-permute-done.2.near_ref.s_ref = f32[4,128,128]{2,1,0:T(8,128)S(1)} collective-permute-done((f32[4,128,128]{2,1,0:T(8,128)S(1)}, f32[4,128,128]{2,1,0:T(8,128)S(1)}, u32[]{:S(2)}, u32[]{:S(2)}) %collective-permute-start.2) | collective-permute-done | bytes 262176 | tf_op jit(solution)/shard_map/ppermute | solution.py:515
  29.3 0.3 joined_steps.1
  29.6 0.6 collective-permute-start.3
  30.2 0.3 copy-done.3
  30.5 1.5 %collective-permute-start.9 = (f32[4,520,128]{2,1,0:T(8,128)S(1)}, f32[4,520,128]{2,1,0:T(8,128)S(1)}, u32[]{:S(2)}, u32[]{:S(2)}) collective-permute-start(f32[4,520,128]{2,1,0:T(8,128)S(1)} %copy-done.3), channel_id=1, source_target_pairs={{0,2},{2,0},{4,6},{6,4},{8,10},{10,8},{12,14},{14,12},{16,18},{18,... | collective-permute-start | bytes 3194888 | tf_op jit(solution)/shard_map/ppermute | solution.py:515
  32.0 3.7 %collective-permute-done.4.v2b_ref = f32[256,512]{1,0:T(8,128)S(1)} collective-permute-done((f32[256,512]{1,0:T(8,128)}, f32[256,512]{1,0:T(8,128)S(1)}, u32[]{:S(2)}, u32[]{:S(2)}) %collective-permute-start.4) | collective-permute-done | bytes 524320 | tf_op jit(solution)/shard_map/ppermute | solution.py:511
  35.8 0.0 collective-permute-done.5.v1a_ref
  35.8 0.1 broadcast_select_fusion.2
  35.8 2.6 %collective-permute-start.7 = (f32[256,512]{1,0:T(8,128)S(1)}, f32[256,512]{1,0:T(8,128)S(1)}, u32[]{:S(2)}, u32[]{:S(2)}) collective-permute-start(f32[256,512]{1,0:T(8,128)S(1)} %broadcast_select_fusion.2), channel_id=1, source_target_pairs={{0,4},{2,6},{4,0},{6,2},{8,12},{10,14},{12,8},{14,10},{16,20},{18,... | collective-permute-start | bytes 1572872 | tf_op jit(solution)/shard_map/ppermute | solution.py:515
  38.5 3.8 %collective-permute-done.3.u_ref = f32[4,128,128]{2,1,0:T(8,128)S(1)} collective-permute-done((f32[4,128,128]{2,1,0:T(8,128)S(1)}, f32[4,128,128]{2,1,0:T(8,128)S(1)}, u32[]{:S(2)}, u32[]{:S(2)}) %collective-permute-start.3) | collective-permute-done | bytes 262176 | tf_op jit(solution)/shard_map/ppermute | solution.py:511
  42.3 0.0 collective-permute-start.6
  42.3 0.3 collective-permute-start.11
  42.6 0.0 copy-done.2
  42.6 3.6 %weight_halves.1 = (bf16[4,512,512]{2,1,0:T(8,128)(2,1)S(1)}, bf16[4,512,512]{2,1,0:T(8,128)(2,1)S(1)}, bf16[4,512,512]{2,1,0:T(8,128)(2,1)S(1)}, bf16[4,512,512]{2,1,0:T(8,128)(2,1)S(1)}) custom-call(f32[512,2048]{1,0:T(8,128)S(1)} %copy-done.2, f32[512,2048]{1,0:T(8,128)} %collective-permute-done.1.other_ref), custom_call_target="tpu_custom_call" | custom-call | flops 8049999872 | bytes 1000 | tf_op jit(solution)/shard_map/weight_halves/pallas_call | solution.py:467
  46.2 0.0 copy-start.10
  46.2 0.0 copy-start.12
  46.2 7.1 %collective-permute-done.7.v1b_ref = f32[256,512]{1,0:T(8,128)S(1)} collective-permute-done((f32[256,512]{1,0:T(8,128)S(1)}, f32[256,512]{1,0:T(8,128)S(1)}, u32[]{:S(2)}, u32[]{:S(2)}) %collective-permute-start.7) | collective-permute-done | bytes 524320 | tf_op jit(solution)/shard_map/ppermute | solution.py:515
  53.3 5.8 %collective-permute-done.6.k2_ref = f32[2,520,128]{2,1,0:T(8,128)S(1)} collective-permute-done((f32[2,520,128]{2,1,0:T(8,128)S(1)}, f32[2,520,128]{2,1,0:T(8,128)S(1)}, u32[]{:S(2)}, u32[]{:S(2)}) %collective-permute-start.6) | collective-permute-done | bytes 532512 | tf_op jit(solution)/shard_map/ppermute | solution.py:511
  59.1 0.1 broadcast_select_fusion.1
  59.2 0.2 collective-permute-start.8
  59.4 0.0 collective-permute-done.9.qp_ref
  59.4 3.5 %early.2 = (f32[2,512,128]{2,1,0:T(8,128)S(1)}, f32[2,512,128]{2,1,0:T(8,128)S(1)}) custom-call(s32[1]{0:T(128)} %bitcast.1.place_ref, f32[4,520,128]{2,1,0:T(8,128)S(1)} %collective-permute-done.9.qp_ref, f32[4,520,128]{2,1,0:T(8,128)S(1)} %copy-done.1, f32[512,512]{1,0:T(8,128)S(1)} %copy-done, f32[2,520,128]{2,1,0:T(8,128)S(1)} %collective-permute-done.6.k2_ref, ...), custom_call_target="tpu_custom_call" | custom-call | flops 5175000064 | bytes 1000 | tf_op jit(solution)/shard_map/early/pallas_call | solution.py:362
  62.9 0.0 copy-done.10
  62.9 0.0 copy-done.12
  62.9 5.4 %collective-permute-done.11.k2_ref = f32[2,520,128]{2,1,0:T(8,128)S(1)} collective-permute-done((f32[2,520,128]{2,1,0:T(8,128)S(1)}, f32[2,520,128]{2,1,0:T(8,128)S(1)}, u32[]{:S(2)}, u32[]{:S(2)}) %collective-permute-start.11) | collective-permute-done | bytes 532512 | tf_op jit(solution)/shard_map/ppermute | solution.py:511
  68.3 0.1 broadcast_select_fusion
  68.4 0.1 collective-permute-start.12
  68.5 3.5 %early.3 = (f32[2,512,128]{2,1,0:T(8,128)S(1)}, f32[2,512,128]{2,1,0:T(8,128)S(1)}) custom-call(s32[1]{0:T(128)} %bitcast.1.place_ref, f32[4,520,128]{2,1,0:T(8,128)S(1)} %collective-permute-done.9.qp_ref, f32[4,520,128]{2,1,0:T(8,128)S(1)} %copy-done.1, f32[512,512]{1,0:T(8,128)S(1)} %copy-done, f32[2,520,128]{2,1,0:T(8,128)S(1)} %collective-permute-done.11.k2_ref, ...), custom_call_target="tpu_custom_call" | custom-call | flops 5175000064 | bytes 1000 | tf_op jit(solution)/shard_map/early/pallas_call | solution.py:362
  72.0 0.0 collective-permute-done.8.k1_ref
  72.0 0.0 copy-start.8
  72.1 3.7 %late.2 = f32[2,520,128]{2,1,0:T(8,128)S(1)} custom-call(s32[1]{0:T(128)} %bitcast.1.place_ref, f32[4,520,128]{2,1,0:T(8,128)S(1)} %collective-permute-done.9.qp_ref, f32[2,520,128]{2,1,0:T(8,128)S(1)} %collective-permute-done.8.k1_ref, f32[256,512]{1,0:T(8,128)} %collective-permute-done.5.v1a_ref, f32[256,512]{1,0:T(8,128)S(1)} %collective-permute-done.7.v1b_ref, ...), custom_call_target="tpu_custom_call" | custom-call | flops 5175000064 | bytes 1000 | tf_op jit(solution)/shard_map/late/pallas_call | solution.py:382
  75.7 1.6 %collective-permute-start.10 = (f32[2,520,128]{2,1,0:T(8,128)S(1)}, f32[2,520,128]{2,1,0:T(8,128)S(1)}, u32[]{:S(2)}, u32[]{:S(2)}) collective-permute-start(f32[2,520,128]{2,1,0:T(8,128)S(1)} %late.2), channel_id=1, source_target_pairs={{0,2},{2,0},{4,6},{6,4},{8,10},{10,8},{12,14},{14,12},{16,18},{18,... | collective-permute-start | bytes 1597448 | tf_op jit(solution)/shard_map/ppermute | solution.py:515
  77.3 3.5 %own.2 = (f32[2,512,128]{2,1,0:T(8,128)S(1)}, f32[2,512,128]{2,1,0:T(8,128)S(1)}) custom-call(s32[1]{0:T(128)} %bitcast.1.place_ref, f32[4,520,128]{2,1,0:T(8,128)S(1)} %copy-done.3, f32[2,520,128]{2,1,0:T(8,128)S(1)} %collective-permute-done.8.k1_ref, f32[256,512]{1,0:T(8,128)} %collective-permute-done.5.v1a_ref, ...), custom_call_target="tpu_custom_call" | custom-call | flops 5175000064 | bytes 1000 | tf_op jit(solution)/shard_map/own/pallas_call | solution.py:403
  80.8 0.0 collective-permute-done.12.k1_ref
  80.8 1.0 copy-done.5
  81.8 3.6 %late.3 = f32[2,520,128]{2,1,0:T(8,128)S(1)} custom-call(s32[1]{0:T(128)} %bitcast.1.place_ref, f32[4,520,128]{2,1,0:T(8,128)S(1)} %collective-permute-done.9.qp_ref, f32[2,520,128]{2,1,0:T(8,128)S(1)} %collective-permute-done.12.k1_ref, f32[256,512]{1,0:T(8,128)} %collective-permute-done.5.v1a_ref, f32[256,512]{1,0:T(8,128)S(1)} %copy-done.5, ...), custom_call_target="tpu_custom_call" | custom-call | flops 5175000064 | bytes 1000 | tf_op jit(solution)/shard_map/late/pallas_call | solution.py:382
  85.4 1.2 %collective-permute-start.13 = (f32[2,520,128]{2,1,0:T(8,128)S(1)}, f32[2,520,128]{2,1,0:T(8,128)S(1)}, u32[]{:S(2)}, u32[]{:S(2)}) collective-permute-start(f32[2,520,128]{2,1,0:T(8,128)S(1)} %late.3), channel_id=1, source_target_pairs={{0,2},{2,0},{4,6},{6,4},{8,10},{10,8},{12,14},{14,12},{16,18},{18,... | collective-permute-start | bytes 1597448 | tf_op jit(solution)/shard_map/ppermute | solution.py:515
  86.6 3.5 %own.3 = (f32[2,512,128]{2,1,0:T(8,128)S(1)}, f32[2,512,128]{2,1,0:T(8,128)S(1)}) custom-call(s32[1]{0:T(128)} %bitcast.1.place_ref, f32[4,520,128]{2,1,0:T(8,128)S(1)} %copy-done.3, f32[2,520,128]{2,1,0:T(8,128)S(1)} %collective-permute-done.12.k1_ref, f32[256,512]{1,0:T(8,128)} %collective-permute-done.5.v1a_ref, f32[256,512]{1,0:T(8,128)S(1)} %copy-done.6, ...), custom_call_target="tpu_custom_call" | custom-call | flops 5175000064 | bytes 1000 | tf_op jit(solution)/shard_map/own/pallas_call | solution.py:403
  90.1 0.0 collective-permute-done.10.msg_ref
  90.1 0.5 merge.2
  90.5 0.1 collective-permute-start.14
  90.6 8.5 %collective-permute-done.13.msg_ref = f32[2,520,128]{2,1,0:T(8,128)S(1)} collective-permute-done((f32[2,520,128]{2,1,0:T(8,128)S(1)}, f32[2,520,128]{2,1,0:T(8,128)S(1)}, u32[]{:S(2)}, u32[]{:S(2)}) %collective-permute-start.13) | collective-permute-done | bytes 532512 | tf_op jit(solution)/shard_map/ppermute | solution.py:515
  99.1 0.5 merge.3
  99.6 0.1 collective-permute-start.15
  99.7 0.0 collective-permute-done.14.refs_2_
  99.7 1.5 %collective-permute-done.15.refs_3_ = f32[256,256]{1,0:T(8,128)S(1)} collective-permute-done((f32[256,256]{1,0:T(8,128)S(1)}, f32[256,256]{1,0:T(8,128)S(1)}, u32[]{:S(2)}, u32[]{:S(2)}) %collective-permute-start.15) | collective-permute-done | bytes 262176 | tf_op jit(solution)/shard_map/ppermute | solution.py:515
  101.2 0.2 copy-done.13
  101.3 4.7 %project.1 = f32[256,2048]{1,0:T(8,128)} custom-call(f32[256,256]{1,0:T(8,128)S(1)} %get-tuple-element.70.refs_0_, f32[256,256]{1,0:T(8,128)S(1)} %get-tuple-element.78.refs_1_, f32[256,256]{1,0:T(8,128)S(1)} %collective-permute-done.14.refs_2_, f32[256,256]{1,0:T(8,128)S(1)} %collective-permute-done.15.refs_3_, bf16[4,512,512]{2,1,0:T(8,128)(2,1)S(1)} %copy-done.11, ...), custom_call_target="tpu_custom_call" | custom-call | flops 8625000448 | bytes 1000 | tf_op jit(solution)/shard_map/project/pallas_call | solution.py:497
  (14 shorter events, 0.0 us)
Async XLA Ops:
  0.0 18.8 %collective-permute-start.1 = (f32[512,2048]{1,0:T(8,128)}, f32[512,2048]{1,0:T(8,128)}, u32[]{:S(2)}, u32[]{:S(2)}) collective-permute-start(f32[512,2048]{1,0:T(8,128)} %own_ref.1), channel_id=1, source_target_pairs={{0,1},{1,0},{2,3},{3,2},{4,5},{5,4},{6,7},{7,6},{8,9},{9,8},{10,11... | collective-permute-start | bytes 12582920 | tf_op jit(solution)/shard_map/ppermute | solution.py:515
  1.5 17.3 %copy-start = (f32[512,512]{1,0:T(8,128)S(1)}, f32[512,512]{1,0:T(8,128)}, u32[]{:S(2)}) copy-start(f32[512,512]{1,0:T(8,128)} %vo_ref.3) | copy-start | bytes 3145732
  1.5 17.2 %collective-permute-start = (f32[256,512]{1,0:T(8,128)S(1)}, f32[256,512]{1,0:T(8,128)S(1)}, u32[]{:S(2)}, u32[]{:S(2)}) collective-permute-start(f32[256,512]{1,0:T(8,128)S(1)} %slice.12), channel_id=1, source_target_pairs={{0,8},{2,10},{4,12},{6,14},{8,16},{10,18},{12,20},{14,22},{16,24},... | collective-permute-start | bytes 1572872 | tf_op jit(solution)/shard_map/ppermute | solution.py:511
  17.1 4.4 %copy-start.7 = (f32[4,128,128]{2,1,0:T(8,128)S(1)}, f32[4,128,128]{2,1,0:T(8,128)}, u32[]{:S(2)}) copy-start(f32[4,128,128]{2,1,0:T(8,128)} %get-tuple-element.50.own_ref.s_ref) | copy-start | bytes 786436
  17.1 5.9 %copy-start.1 = (f32[4,520,128]{2,1,0:T(8,128)S(1)}, f32[4,520,128]{2,1,0:T(8,128)}, u32[]{:S(2)}) copy-start(f32[4,520,128]{2,1,0:T(8,128)} %get-tuple-element.49.ko_ref) | copy-start | bytes 3194884
  20.0 15.8 %collective-permute-start.4 = (f32[256,512]{1,0:T(8,128)}, f32[256,512]{1,0:T(8,128)S(1)}, u32[]{:S(2)}, u32[]{:S(2)}) collective-permute-start(f32[256,512]{1,0:T(8,128)} %get-tuple-element.51), channel_id=1, source_target_pairs={{0,8},{2,10},{4,12},{6,14},{8,16},{10,18},{12,20},{14,22},{16,24},... | collective-permute-start | bytes 1572872 | tf_op jit(solution)/shard_map/ppermute | solution.py:511
  20.0 15.8 %collective-permute-start.5 = (f32[256,512]{1,0:T(8,128)}, f32[256,512]{1,0:T(8,128)}, u32[]{:S(2)}, u32[]{:S(2)}) collective-permute-start(f32[256,512]{1,0:T(8,128)} %get-tuple-element.83), channel_id=1, source_target_pairs={{0,4},{2,6},{4,0},{6,2},{8,12},{10,14},{12,8},{14,10},{16,20},{18,... | collective-permute-start | bytes 1572872 | tf_op jit(solution)/shard_map/ppermute | solution.py:515
  21.5 7.8 %collective-permute-start.2 = (f32[4,128,128]{2,1,0:T(8,128)S(1)}, f32[4,128,128]{2,1,0:T(8,128)S(1)}, u32[]{:S(2)}, u32[]{:S(2)}) collective-permute-start(f32[4,128,128]{2,1,0:T(8,128)S(1)} %copy-done.7), channel_id=1, source_target_pairs={{0,2},{2,0},{4,6},{6,4},{8,10},{10,8},{12,14},{14,12},{16,18},{18,... | collective-permute-start | bytes 786440 | tf_op jit(solution)/shard_map/ppermute | solution.py:515
  29.3 1.2 %copy-start.3 = (f32[4,520,128]{2,1,0:T(8,128)S(1)}, f32[4,520,128]{2,1,0:T(8,128)}, u32[]{:S(2)}) copy-start(f32[4,520,128]{2,1,0:T(8,128)} %get-tuple-element.60.qo_ref) | copy-start | bytes 3194884
  29.3 13.3 %copy-start.2 = (f32[512,2048]{1,0:T(8,128)S(1)}, f32[512,2048]{1,0:T(8,128)}, u32[]{:S(2)}) copy-start(f32[512,2048]{1,0:T(8,128)} %own_ref.1) | copy-start | bytes 12582916
  29.6 12.7 %collective-permute-start.3 = (f32[4,128,128]{2,1,0:T(8,128)S(1)}, f32[4,128,128]{2,1,0:T(8,128)S(1)}, u32[]{:S(2)}, u32[]{:S(2)}) collective-permute-start(f32[4,128,128]{2,1,0:T(8,128)S(1)} %joined_steps.1), channel_id=1, source_target_pairs={{0,4},{2,6},{4,8},{6,10},{8,12},{10,14},{12,16},{14,18},{16,20},{1... | collective-permute-start | bytes 786440 | tf_op jit(solution)/shard_map/ppermute | solution.py:511
  30.5 28.9 %collective-permute-start.9 = (f32[4,520,128]{2,1,0:T(8,128)S(1)}, f32[4,520,128]{2,1,0:T(8,128)S(1)}, u32[]{:S(2)}, u32[]{:S(2)}) collective-permute-start(f32[4,520,128]{2,1,0:T(8,128)S(1)} %copy-done.3), channel_id=1, source_target_pairs={{0,2},{2,0},{4,6},{6,4},{8,10},{10,8},{12,14},{14,12},{16,18},{18,... | collective-permute-start | bytes 3194888 | tf_op jit(solution)/shard_map/ppermute | solution.py:515
  35.8 17.5 %collective-permute-start.7 = (f32[256,512]{1,0:T(8,128)S(1)}, f32[256,512]{1,0:T(8,128)S(1)}, u32[]{:S(2)}, u32[]{:S(2)}) collective-permute-start(f32[256,512]{1,0:T(8,128)S(1)} %broadcast_select_fusion.2), channel_id=1, source_target_pairs={{0,4},{2,6},{4,0},{6,2},{8,12},{10,14},{12,8},{14,10},{16,20},{18,... | collective-permute-start | bytes 1572872 | tf_op jit(solution)/shard_map/ppermute | solution.py:515
  42.3 16.8 %collective-permute-start.6 = (f32[2,520,128]{2,1,0:T(8,128)S(1)}, f32[2,520,128]{2,1,0:T(8,128)S(1)}, u32[]{:S(2)}, u32[]{:S(2)}) collective-permute-start(f32[2,520,128]{2,1,0:T(8,128)S(1)} %get-tuple-element.55), channel_id=1, source_target_pairs={{0,8},{2,10},{4,12},{6,14},{8,16},{10,18},{12,20},{14,22},{16,24},... | collective-permute-start | bytes 1597448 | tf_op jit(solution)/shard_map/ppermute | solution.py:511
  42.3 26.0 %collective-permute-start.11 = (f32[2,520,128]{2,1,0:T(8,128)S(1)}, f32[2,520,128]{2,1,0:T(8,128)S(1)}, u32[]{:S(2)}, u32[]{:S(2)}) collective-permute-start(f32[2,520,128]{2,1,0:T(8,128)S(1)} %get-tuple-element.72), channel_id=1, source_target_pairs={{0,8},{2,10},{4,12},{6,14},{8,16},{10,18},{12,20},{14,22},{16,24},... | collective-permute-start | bytes 1597448 | tf_op jit(solution)/shard_map/ppermute | solution.py:511
  46.2 16.7 %copy-start.10 = (bf16[4,512,512]{2,1,0:T(8,128)(2,1)}, bf16[4,512,512]{2,1,0:T(8,128)(2,1)S(1)}, u32[]{:S(2)}) copy-start(bf16[4,512,512]{2,1,0:T(8,128)(2,1)S(1)} %get-tuple-element.63.refs_4_) | copy-start | bytes 6291460
  46.2 16.7 %copy-start.12 = (bf16[4,512,512]{2,1,0:T(8,128)(2,1)}, bf16[4,512,512]{2,1,0:T(8,128)(2,1)S(1)}, u32[]{:S(2)}) copy-start(bf16[4,512,512]{2,1,0:T(8,128)(2,1)S(1)} %get-tuple-element.64.refs_5_) | copy-start | bytes 6291460
  53.3 24.0 %copy-start.4 = (f32[256,512]{1,0:T(8,128)}, f32[256,512]{1,0:T(8,128)S(1)}, u32[]{:S(2)}) copy-start(f32[256,512]{1,0:T(8,128)S(1)} %collective-permute-done.7.v1b_ref) | copy-start | bytes 1572868
  59.2 12.8 %collective-permute-start.8 = (f32[2,520,128]{2,1,0:T(8,128)S(1)}, f32[2,520,128]{2,1,0:T(8,128)S(1)}, u32[]{:S(2)}, u32[]{:S(2)}) collective-permute-start(f32[2,520,128]{2,1,0:T(8,128)S(1)} %broadcast_select_fusion.1), channel_id=1, source_target_pairs={{0,4},{2,6},{4,0},{6,2},{8,12},{10,14},{12,8},{14,10},{16,20},{18,... | collective-permute-start | bytes 1597448 | tf_op jit(solution)/shard_map/ppermute | solution.py:515
  68.4 12.3 %collective-permute-start.12 = (f32[2,520,128]{2,1,0:T(8,128)S(1)}, f32[2,520,128]{2,1,0:T(8,128)S(1)}, u32[]{:S(2)}, u32[]{:S(2)}) collective-permute-start(f32[2,520,128]{2,1,0:T(8,128)S(1)} %broadcast_select_fusion), channel_id=1, source_target_pairs={{0,4},{2,6},{4,0},{6,2},{8,12},{10,14},{12,8},{14,10},{16,20},{18,... | collective-permute-start | bytes 1597448 | tf_op jit(solution)/shard_map/ppermute | solution.py:515
  72.0 5.3 %copy-start.8 = (f32[4,512,128]{2,1,0:T(8,128)S(1)}, f32[4,512,128]{2,1,0:T(8,128)}, u32[]{:S(2)}) copy-start(f32[4,512,128]{2,1,0:T(8,128)} %get-tuple-element.56.od_ref) | copy-start | bytes 3145732
  72.1 5.3 %copy-start.9 = (f32[4,512,128]{2,1,0:T(8,128)S(1)}, f32[4,512,128]{2,1,0:T(8,128)}, u32[]{:S(2)}) copy-start(f32[4,512,128]{2,1,0:T(8,128)} %get-tuple-element.57.ld_ref) | copy-start | bytes 3145732
  75.7 14.3 %collective-permute-start.10 = (f32[2,520,128]{2,1,0:T(8,128)S(1)}, f32[2,520,128]{2,1,0:T(8,128)S(1)}, u32[]{:S(2)}, u32[]{:S(2)}) collective-permute-start(f32[2,520,128]{2,1,0:T(8,128)S(1)} %late.2), channel_id=1, source_target_pairs={{0,2},{2,0},{4,6},{6,4},{8,10},{10,8},{12,14},{14,12},{16,18},{18,... | collective-permute-start | bytes 1597448 | tf_op jit(solution)/shard_map/ppermute | solution.py:515
  80.8 1.0 copy-start.5
  81.8 4.8 %copy-start.6 = (f32[256,512]{1,0:T(8,128)S(1)}, f32[256,512]{1,0:T(8,128)}, u32[]{:S(2)}) copy-start(f32[256,512]{1,0:T(8,128)} %copy-done.4) | copy-start | bytes 1572868
  85.4 13.7 %collective-permute-start.13 = (f32[2,520,128]{2,1,0:T(8,128)S(1)}, f32[2,520,128]{2,1,0:T(8,128)S(1)}, u32[]{:S(2)}, u32[]{:S(2)}) collective-permute-start(f32[2,520,128]{2,1,0:T(8,128)S(1)} %late.3), channel_id=1, source_target_pairs={{0,2},{2,0},{4,6},{6,4},{8,10},{10,8},{12,14},{14,12},{16,18},{18,... | collective-permute-start | bytes 1597448 | tf_op jit(solution)/shard_map/ppermute | solution.py:515
  90.5 9.1 %collective-permute-start.14 = (f32[256,256]{1,0:T(8,128)S(1)}, f32[256,256]{1,0:T(8,128)S(1)}, u32[]{:S(2)}, u32[]{:S(2)}) collective-permute-start(f32[256,256]{1,0:T(8,128)S(1)} %get-tuple-element.79), channel_id=1, source_target_pairs={{0,1},{1,0},{2,3},{3,2},{4,5},{5,4},{6,7},{7,6},{8,9},{9,8},{10,11... | collective-permute-start | bytes 786440 | tf_op jit(solution)/shard_map/ppermute | solution.py:515
  99.1 2.1 %copy-start.11 = (bf16[4,512,512]{2,1,0:T(8,128)(2,1)S(1)}, bf16[4,512,512]{2,1,0:T(8,128)(2,1)}, u32[]{:S(2)}) copy-start(bf16[4,512,512]{2,1,0:T(8,128)(2,1)} %copy-done.10) | copy-start | bytes 6291460
  99.1 2.2 %copy-start.13 = (bf16[4,512,512]{2,1,0:T(8,128)(2,1)S(1)}, bf16[4,512,512]{2,1,0:T(8,128)(2,1)}, u32[]{:S(2)}) copy-start(bf16[4,512,512]{2,1,0:T(8,128)(2,1)} %copy-done.12) | copy-start | bytes 6291460
  99.6 1.6 %collective-permute-start.15 = (f32[256,256]{1,0:T(8,128)S(1)}, f32[256,256]{1,0:T(8,128)S(1)}, u32[]{:S(2)}, u32[]{:S(2)}) collective-permute-start(f32[256,256]{1,0:T(8,128)S(1)} %get-tuple-element.80), channel_id=1, source_target_pairs={{0,1},{1,0},{2,3},{3,2},{4,5},{5,4},{6,7},{7,6},{8,9},{9,8},{10,11... | collective-permute-start | bytes 786440 | tf_op jit(solution)/shard_map/ppermute | solution.py:515

commit v4 on v3

--- a/solution.py
+++ b/solution.py
@@ -546,11 +546,12 @@
     q_near = exchanged(after(q_msg, near_steps), "ctx", 1)
     joined = joined_steps(place, steps, near_steps)
     joined = onward(joined, 2)
-    source = chosen(v_last, after(v2_last, v1_first))
+    source = chosen(v_last, v2_last)
     v1_last = exchanged(source, "ctx", 2)
-    k2 = [onward(after(block, joined, source), 4) for block in own_k]
+    k2 = [onward(after(own_k[0], source), 4)]
+    k2 += [onward(after(block, joined, source), 4) for block in own_k[1:]]
     weights = weight_halves(out_weight, after(w_other, joined, source))
-    sources = [chosen(after(own_k[0], v1_last), k2[0])]
+    sources = [chosen(after(own_k[0], v1_first, v1_last), k2[0])]
     v1, v2 = (v1_first, v1_last), (v2_first, v2_last)
     early = []
     for g in groups:

time: 106 us -> 103 us (0.972)
  Pallas kernels: 43.6 us -> 40.1 us
  waiting for transfers between devices: 43.8 us -> 40.5 us
  starting transfers between devices: 14.3 us -> 17.4 us
    ppermute x5, waiting for transfers between devices: 20.4 us -> 17.1 us  [onward(): lax.ppermute(value, 'ctx', [(i, (i + steps) % count) for i in range(count)])]
    ppermute x11, starting transfers between devices: 10.8 us -> 13.3 us  [exchanged(): lax.ppermute(value, axis, [(i, i ^ bit) for i in range(lax.axis_size(axis...]
    pallas_call x2, Pallas kernels: 7.26 us -> 5.4 us  [late_part(): pl.pallas_call(functools.partial(late_kernel, scale=scale), grid_spec=plt...]
    pallas_call x2, Pallas kernels: 6.92 us -> 5.29 us  [own_part(): pl.pallas_call(functools.partial(own_kernel, scale=scale), grid_spec=pltp...]
    unnamed x28 -> x34, local copies, waits for them, and re-layouts: 1.56 us -> 2.3 us
  transfers between devices with their start and end apart: 16 -> 16, of which waited for: 9 -> 11; matrix products, arithmetic and copies ran while one was open for 1% -> 1% of each run, Pallas kernels for 37% -> 34%
where the time goes in v4:
time: 103 us
  waiting for transfers between devices  40.5 us (39%)
  Pallas kernels  40.1 us (39%)
  starting transfers between devices  17.4 us (17%)
  local copies, waits for them, and re-layouts  3.44 us (3%)
  other arithmetic  1.39 us (1%)
    ppermute x11, waiting for transfers between devices, exchanged(): lax.ppermute(value, axis, [(i, i ^ bit) for i in range(lax.axis_size(axis...  23.4 us
    ppermute x5, waiting for transfers between devices, onward(): lax.ppermute(value, 'ctx', [(i, (i + steps) % count) for i in range(count)])  17.1 us
    ppermute x11, starting transfers between devices, exchanged(): lax.ppermute(value, axis, [(i, i ^ bit) for i in range(lax.axis_size(axis...  13.3 us
    pallas_call x1, Pallas kernels, prepare(): pl.pallas_call(functools.partial(prepare_kernel, scale=scale), grid=(head...  12.9 us
    pallas_call x2, Pallas kernels, early_part(): pl.pallas_call(functools.partial(early_kernel, scale=scale), grid_spec=pl...  6.97 us
    pallas_call x2, Pallas kernels, late_part(): pl.pallas_call(functools.partial(late_kernel, scale=scale), grid_spec=plt...  5.4 us
    pallas_call x2, Pallas kernels, own_part(): pl.pallas_call(functools.partial(own_kernel, scale=scale), grid_spec=pltp...  5.29 us
    pallas_call x1, Pallas kernels, project(): pl.pallas_call(project_kernel, grid=(tiles,), in_specs=a_spec + [w_spec]...  4.71 us
  transfers between devices with their start and end apart: 16, of which 11 were waited for; matrix products, arithmetic and copies ran while one was open for 1% of the time, Pallas kernels for 34%

profile of v4, /device:TPU:0, one launch (start us, length us, event | category | flops | bytes accessed | tf_op | source)
XLA Modules:
  0.0 103.0 jit_solution(18413294302767596040)
XLA Ops:
  0.0 0.5 collective-permute-start.1
  0.5 1.1 %slice.12 = f32[256,512]{1,0:T(8,128)S(1)} slice(f32[512,512]{1,0:T(8,128)} %vo_ref.3), slice={[0:256], [0:512]} | slice | bytes 1048576 | tf_op jit(solution)/shard_map/slice | solution.py:533
  1.5 0.0 copy-start
  1.5 2.6 %collective-permute-start = (f32[256,512]{1,0:T(8,128)S(1)}, f32[256,512]{1,0:T(8,128)S(1)}, u32[]{:S(2)}, u32[]{:S(2)}) collective-permute-start(f32[256,512]{1,0:T(8,128)S(1)} %slice.12), channel_id=1, source_target_pairs={{0,8},{2,10},{4,12},{6,14},{8,16},{10,18},{12,20},{14,22},{16,24},... | collective-permute-start | bytes 1572872 | tf_op jit(solution)/shard_map/ppermute | solution.py:511
  4.2 12.9 %prepare.1 = (f32[4,520,128]{2,1,0:T(8,128)}, f32[4,520,128]{2,1,0:T(8,128)}, f32[4,128,128]{2,1,0:T(8,128)}, f32[4,512,128]{2,1,0:T(8,128)}, f32[4,512,128]{2,1,0:T(8,128)}) custom-call(f32[512,512]{1,0:T(8,128)} %q_ref.1, f32[512,512]{1,0:T(8,128)} %k_ref.1, f32[512,512]{1,0:T(8,128)} %vo_ref.3, f32[512,512]{1,0:T(8,128)} %w_ref.1, f32[4,512]{1,0:T(4,128)} %beta_ref.1, ...), custom_call_target="tpu_custom_call" | custom-call | flops 14949999616 | bytes 1000 | tf_op jit(solution)/shard_map/prepare/pallas_call | solution.py:221
  17.1 0.0 copy-start.1
  17.1 1.7 %collective-permute-done.v2a_ref = f32[256,512]{1,0:T(8,128)S(1)} collective-permute-done((f32[256,512]{1,0:T(8,128)S(1)}, f32[256,512]{1,0:T(8,128)S(1)}, u32[]{:S(2)}, u32[]{:S(2)}) %collective-permute-start) | collective-permute-done | bytes 524320 | tf_op jit(solution)/shard_map/ppermute | solution.py:511
  18.8 0.0 collective-permute-done.1.other_ref
  18.8 0.0 copy-done
  18.8 1.2 %broadcast_select_fusion.2 = (f32[256,512]{1,0:T(8,128)}, f32[256,512]{1,0:T(8,128)}) fusion(f32[256,512]{1,0:T(8,128)S(1)} %collective-permute-done.v2a_ref, pred[]{:T(512)S(6)} %ge.3, f32[512,512]{1,0:T(8,128)S(1)} %copy-done), kind=kLoop, calls=%fused_computation.2 | loop fusion | flops 131072 | bytes 2621441 | tf_op jit(solution)/shard_map/jit(_where)/select_n | solution.py:536
  20.0 0.0 collective-permute-start.2
  20.0 1.5 %collective-permute-start.7 = (f32[4,128,128]{2,1,0:T(8,128)S(1)}, f32[4,128,128]{2,1,0:T(8,128)S(1)}, u32[]{:S(2)}, u32[]{:S(2)}) collective-permute-start(f32[4,128,128]{2,1,0:T(8,128)S(1)} %copy-done.10), channel_id=1, source_target_pairs={{0,2},{2,0},{4,6},{6,4},{8,10},{10,8},{12,14},{14,12},{16,18},{18,... | collective-permute-start | bytes 786440 | tf_op jit(solution)/shard_map/ppermute | solution.py:515
  21.5 1.5 %collective-permute-start.4 = (f32[256,512]{1,0:T(8,128)}, f32[256,512]{1,0:T(8,128)S(1)}, u32[]{:S(2)}, u32[]{:S(2)}) collective-permute-start(f32[256,512]{1,0:T(8,128)} %get-tuple-element.81), channel_id=1, source_target_pairs={{0,4},{2,6},{4,0},{6,2},{8,12},{10,14},{12,8},{14,10},{16,20},{18,... | collective-permute-start | bytes 1572872 | tf_op jit(solution)/shard_map/ppermute | solution.py:515
  23.0 0.0 copy-done.1
  23.0 0.1 fusion
  23.1 5.1 %collective-permute-done.7.near_ref.s_ref = f32[4,128,128]{2,1,0:T(8,128)S(1)} collective-permute-done((f32[4,128,128]{2,1,0:T(8,128)S(1)}, f32[4,128,128]{2,1,0:T(8,128)S(1)}, u32[]{:S(2)}, u32[]{:S(2)}) %collective-permute-start.7) | collective-permute-done | bytes 262176 | tf_op jit(solution)/shard_map/ppermute | solution.py:515
  28.2 0.3 joined_steps.1
  28.4 1.5 %collective-permute-start.8 = (f32[4,128,128]{2,1,0:T(8,128)S(1)}, f32[4,128,128]{2,1,0:T(8,128)S(1)}, u32[]{:S(2)}, u32[]{:S(2)}) collective-permute-start(f32[4,128,128]{2,1,0:T(8,128)S(1)} %joined_steps.1), channel_id=1, source_target_pairs={{0,4},{2,6},{4,8},{6,10},{8,12},{10,14},{12,16},{14,18},{16,20},{1... | collective-permute-start | bytes 786440 | tf_op jit(solution)/shard_map/ppermute | solution.py:511
  29.9 1.5 %collective-permute-start.9 = (f32[4,520,128]{2,1,0:T(8,128)S(1)}, f32[4,520,128]{2,1,0:T(8,128)S(1)}, u32[]{:S(2)}, u32[]{:S(2)}) collective-permute-start(f32[4,520,128]{2,1,0:T(8,128)S(1)} %copy-done.3), channel_id=1, source_target_pairs={{0,2},{2,0},{4,6},{6,4},{8,10},{10,8},{12,14},{14,12},{16,18},{18,... | collective-permute-start | bytes 3194888 | tf_op jit(solution)/shard_map/ppermute | solution.py:515
  31.4 4.3 %collective-permute-done.2.v2b_ref = f32[256,512]{1,0:T(8,128)S(1)} collective-permute-done((f32[256,512]{1,0:T(8,128)}, f32[256,512]{1,0:T(8,128)S(1)}, u32[]{:S(2)}, u32[]{:S(2)}) %collective-permute-start.2) | collective-permute-done | bytes 524320 | tf_op jit(solution)/shard_map/ppermute | solution.py:511
  35.8 0.1 broadcast_select_fusion.3
  35.9 2.6 %collective-permute-start.5 = (f32[256,512]{1,0:T(8,128)S(1)}, f32[256,512]{1,0:T(8,128)S(1)}, u32[]{:S(2)}, u32[]{:S(2)}) collective-permute-start(f32[256,512]{1,0:T(8,128)S(1)} %broadcast_select_fusion.3), channel_id=1, source_target_pairs={{0,4},{2,6},{4,0},{6,2},{8,12},{10,14},{12,8},{14,10},{16,20},{18,... | collective-permute-start | bytes 1572872 | tf_op jit(solution)/shard_map/ppermute | solution.py:515
  38.5 0.0 collective-permute-start.3
  38.5 4.9 %collective-permute-done.8.u_ref = f32[4,128,128]{2,1,0:T(8,128)S(1)} collective-permute-done((f32[4,128,128]{2,1,0:T(8,128)S(1)}, f32[4,128,128]{2,1,0:T(8,128)S(1)}, u32[]{:S(2)}, u32[]{:S(2)}) %collective-permute-start.8) | collective-permute-done | bytes 262176 | tf_op jit(solution)/shard_map/ppermute | solution.py:511
  43.4 0.0 collective-permute-start.11
  43.4 0.0 copy-done.2
  43.5 3.6 %weight_halves.1 = (bf16[4,512,512]{2,1,0:T(8,128)(2,1)S(1)}, bf16[4,512,512]{2,1,0:T(8,128)(2,1)S(1)}, bf16[4,512,512]{2,1,0:T(8,128)(2,1)S(1)}, bf16[4,512,512]{2,1,0:T(8,128)(2,1)S(1)}) custom-call(f32[512,2048]{1,0:T(8,128)S(1)} %copy-done.2, f32[512,2048]{1,0:T(8,128)} %collective-permute-done.1.other_ref), custom_call_target="tpu_custom_call" | custom-call | flops 8049999872 | bytes 1000 | tf_op jit(solution)/shard_map/weight_halves/pallas_call | solution.py:467
  47.1 0.0 copy-start.13
  47.1 0.0 copy-start.15
  47.1 0.0 collective-permute-done.4.v1a_ref
  47.1 6.2 %collective-permute-done.5.v1b_ref = f32[256,512]{1,0:T(8,128)S(1)} collective-permute-done((f32[256,512]{1,0:T(8,128)S(1)}, f32[256,512]{1,0:T(8,128)S(1)}, u32[]{:S(2)}, u32[]{:S(2)}) %collective-permute-start.5) | collective-permute-done | bytes 524320 | tf_op jit(solution)/shard_map/ppermute | solution.py:515
  53.3 2.0 %collective-permute-done.3.k2_ref = f32[2,520,128]{2,1,0:T(8,128)S(1)} collective-permute-done((f32[2,520,128]{2,1,0:T(8,128)S(1)}, f32[2,520,128]{2,1,0:T(8,128)S(1)}, u32[]{:S(2)}, u32[]{:S(2)}) %collective-permute-start.3) | collective-permute-done | bytes 532512 | tf_op jit(solution)/shard_map/ppermute | solution.py:511
  55.3 0.1 broadcast_select_fusion.1
  55.4 0.2 collective-permute-start.6
  55.5 0.0 collective-permute-done.9.qp_ref
  55.5 3.5 %early.2 = (f32[2,512,128]{2,1,0:T(8,128)S(1)}, f32[2,512,128]{2,1,0:T(8,128)S(1)}) custom-call(s32[1]{0:T(128)} %bitcast.1.place_ref, f32[4,520,128]{2,1,0:T(8,128)S(1)} %collective-permute-done.9.qp_ref, f32[4,520,128]{2,1,0:T(8,128)S(1)} %copy-done.1, f32[512,512]{1,0:T(8,128)S(1)} %copy-done, f32[2,520,128]{2,1,0:T(8,128)S(1)} %collective-permute-done.3.k2_ref, ...), custom_call_target="tpu_custom_call" | custom-call | flops 5175000064 | bytes 1000 | tf_op jit(solution)/shard_map/early/pallas_call | solution.py:362
  59.0 4.1 %collective-permute-done.11.k2_ref = f32[2,520,128]{2,1,0:T(8,128)S(1)} collective-permute-done((f32[2,520,128]{2,1,0:T(8,128)S(1)}, f32[2,520,128]{2,1,0:T(8,128)S(1)}, u32[]{:S(2)}, u32[]{:S(2)}) %collective-permute-start.11) | collective-permute-done | bytes 532512 | tf_op jit(solution)/shard_map/ppermute | solution.py:511
  63.2 0.1 broadcast_select_fusion
  63.2 2.5 %collective-permute-start.12 = (f32[2,520,128]{2,1,0:T(8,128)S(1)}, f32[2,520,128]{2,1,0:T(8,128)S(1)}, u32[]{:S(2)}, u32[]{:S(2)}) collective-permute-start(f32[2,520,128]{2,1,0:T(8,128)S(1)} %broadcast_select_fusion), channel_id=1, source_target_pairs={{0,4},{2,6},{4,0},{6,2},{8,12},{10,14},{12,8},{14,10},{16,20},{18,... | collective-permute-start | bytes 1597448 | tf_op jit(solution)/shard_map/ppermute | solution.py:515
  65.8 3.5 %early.3 = (f32[2,512,128]{2,1,0:T(8,128)S(1)}, f32[2,512,128]{2,1,0:T(8,128)S(1)}) custom-call(s32[1]{0:T(128)} %bitcast.1.place_ref, f32[4,520,128]{2,1,0:T(8,128)S(1)} %collective-permute-done.9.qp_ref, f32[4,520,128]{2,1,0:T(8,128)S(1)} %copy-done.1, f32[512,512]{1,0:T(8,128)S(1)} %copy-done, f32[2,520,128]{2,1,0:T(8,128)S(1)} %collective-permute-done.11.k2_ref, ...), custom_call_target="tpu_custom_call" | custom-call | flops 5175000064 | bytes 1000 | tf_op jit(solution)/shard_map/early/pallas_call | solution.py:362
  69.3 0.0 collective-permute-done.6.k1_ref
  69.3 0.0 copy-done.4
  69.3 0.0 copy-done.7
  69.3 0.0 copy-start.11
  69.3 0.0 copy-start.12
  69.3 2.7 %late.2 = f32[2,520,128]{2,1,0:T(8,128)S(1)} custom-call(s32[1]{0:T(128)} %bitcast.1.place_ref, f32[4,520,128]{2,1,0:T(8,128)S(1)} %collective-permute-done.9.qp_ref, f32[2,520,128]{2,1,0:T(8,128)S(1)} %collective-permute-done.6.k1_ref, f32[256,512]{1,0:T(8,128)S(1)} %collective-permute-done.4.v1a_ref, f32[256,512]{1,0:T(8,128)S(1)} %collective-permute-done.5.v1b_ref, ...), custom_call_target="tpu_custom_call" | custom-call | flops 5175000064 | bytes 1000 | tf_op jit(solution)/shard_map/late/pallas_call | solution.py:382
  72.0 1.6 %collective-permute-start.10 = (f32[2,520,128]{2,1,0:T(8,128)S(1)}, f32[2,520,128]{2,1,0:T(8,128)S(1)}, u32[]{:S(2)}, u32[]{:S(2)}) collective-permute-start(f32[2,520,128]{2,1,0:T(8,128)S(1)} %late.2), channel_id=1, source_target_pairs={{0,2},{2,0},{4,6},{6,4},{8,10},{10,8},{12,14},{14,12},{16,18},{18,... | collective-permute-start | bytes 1597448 | tf_op jit(solution)/shard_map/ppermute | solution.py:515
  73.6 1.0 %copy-done.5 = f32[256,512]{1,0:T(8,128)S(1)} copy-done((f32[256,512]{1,0:T(8,128)S(1)}, f32[256,512]{1,0:T(8,128)}, u32[]{:S(2)}) %copy-start.5) | copy-done | bytes 524312
  74.6 1.0 %copy-done.8 = f32[256,512]{1,0:T(8,128)S(1)} copy-done((f32[256,512]{1,0:T(8,128)S(1)}, f32[256,512]{1,0:T(8,128)}, u32[]{:S(2)}) %copy-start.8) | copy-done | bytes 524312
  75.7 2.6 %own.2 = (f32[2,512,128]{2,1,0:T(8,128)S(1)}, f32[2,512,128]{2,1,0:T(8,128)S(1)}) custom-call(s32[1]{0:T(128)} %bitcast.1.place_ref, f32[4,520,128]{2,1,0:T(8,128)S(1)} %copy-done.3, f32[2,520,128]{2,1,0:T(8,128)S(1)} %collective-permute-done.6.k1_ref, f32[256,512]{1,0:T(8,128)S(1)} %copy-done.5, f32[256,512]{1,0:T(8,128)S(1)} %copy-done.8, ...), custom_call_target="tpu_custom_call" | custom-call | flops 5175000064 | bytes 1000 | tf_op jit(solution)/shard_map/own/pallas_call | solution.py:403
  78.3 0.5 collective-permute-done.12.k1_ref
  78.8 2.7 %late.3 = f32[2,520,128]{2,1,0:T(8,128)S(1)} custom-call(s32[1]{0:T(128)} %bitcast.1.place_ref, f32[4,520,128]{2,1,0:T(8,128)S(1)} %collective-permute-done.9.qp_ref, f32[2,520,128]{2,1,0:T(8,128)S(1)} %collective-permute-done.12.k1_ref, f32[256,512]{1,0:T(8,128)S(1)} %copy-done.6, f32[256,512]{1,0:T(8,128)S(1)} %copy-done.9, f32[4,128,128]{2,1,0:T(8,128)S(1)} %copy-done.10, ...), custom_call_target="tpu_custom_call" | custom-call | flops 5175000064 | bytes 1000 | tf_op jit(solution)/shard_map/late/pallas_call | solution.py:382
  81.5 1.3 %collective-permute-start.13 = (f32[2,520,128]{2,1,0:T(8,128)S(1)}, f32[2,520,128]{2,1,0:T(8,128)S(1)}, u32[]{:S(2)}, u32[]{:S(2)}) collective-permute-start(f32[2,520,128]{2,1,0:T(8,128)S(1)} %late.3), channel_id=1, source_target_pairs={{0,2},{2,0},{4,6},{6,4},{8,10},{10,8},{12,14},{14,12},{16,18},{18,... | collective-permute-start | bytes 1597448 | tf_op jit(solution)/shard_map/ppermute | solution.py:515
  82.8 2.6 %own.3 = (f32[2,512,128]{2,1,0:T(8,128)S(1)}, f32[2,512,128]{2,1,0:T(8,128)S(1)}) custom-call(s32[1]{0:T(128)} %bitcast.1.place_ref, f32[4,520,128]{2,1,0:T(8,128)S(1)} %copy-done.3, f32[2,520,128]{2,1,0:T(8,128)S(1)} %collective-permute-done.12.k1_ref, f32[256,512]{1,0:T(8,128)S(1)} %copy-done.6, f32[256,512]{1,0:T(8,128)S(1)} %copy-done.9, ...), custom_call_target="tpu_custom_call" | custom-call | flops 5175000064 | bytes 1000 | tf_op jit(solution)/shard_map/own/pallas_call | solution.py:403
  85.4 1.4 %collective-permute-done.10.msg_ref = f32[2,520,128]{2,1,0:T(8,128)S(1)} collective-permute-done((f32[2,520,128]{2,1,0:T(8,128)S(1)}, f32[2,520,128]{2,1,0:T(8,128)S(1)}, u32[]{:S(2)}, u32[]{:S(2)}) %collective-permute-start.10) | collective-permute-done | bytes 532512 | tf_op jit(solution)/shard_map/ppermute | solution.py:515
  86.8 0.5 merge.2
  87.3 0.1 collective-permute-start.14
  87.4 8.7 %collective-permute-done.13.msg_ref = f32[2,520,128]{2,1,0:T(8,128)S(1)} collective-permute-done((f32[2,520,128]{2,1,0:T(8,128)S(1)}, f32[2,520,128]{2,1,0:T(8,128)S(1)}, u32[]{:S(2)}, u32[]{:S(2)}) %collective-permute-start.13) | collective-permute-done | bytes 532512 | tf_op jit(solution)/shard_map/ppermute | solution.py:515
  96.1 0.5 merge.3
  96.6 0.1 collective-permute-start.15
  96.6 0.0 collective-permute-done.14.refs_2_
  96.7 1.5 %collective-permute-done.15.refs_3_ = f32[256,256]{1,0:T(8,128)S(1)} collective-permute-done((f32[256,256]{1,0:T(8,128)S(1)}, f32[256,256]{1,0:T(8,128)S(1)}, u32[]{:S(2)}, u32[]{:S(2)}) %collective-permute-start.15) | collective-permute-done | bytes 262176 | tf_op jit(solution)/shard_map/ppermute | solution.py:515
  98.2 0.2 copy-done.16
  98.3 4.7 %project.1 = f32[256,2048]{1,0:T(8,128)} custom-call(f32[256,256]{1,0:T(8,128)S(1)} %get-tuple-element.68.refs_0_, f32[256,256]{1,0:T(8,128)S(1)} %get-tuple-element.76.refs_1_, f32[256,256]{1,0:T(8,128)S(1)} %collective-permute-done.14.refs_2_, f32[256,256]{1,0:T(8,128)S(1)} %collective-permute-done.15.refs_3_, bf16[4,512,512]{2,1,0:T(8,128)(2,1)S(1)} %copy-done.14, ...), custom_call_target="tpu_custom_call" | custom-call | flops 8625000448 | bytes 1000 | tf_op jit(solution)/shard_map/project/pallas_call | solution.py:497
  (20 shorter events, 0.0 us)
Async XLA Ops:
  0.0 18.8 %collective-permute-start.1 = (f32[512,2048]{1,0:T(8,128)}, f32[512,2048]{1,0:T(8,128)}, u32[]{:S(2)}, u32[]{:S(2)}) collective-permute-start(f32[512,2048]{1,0:T(8,128)} %own_ref.1), channel_id=1, source_target_pairs={{0,1},{1,0},{2,3},{3,2},{4,5},{5,4},{6,7},{7,6},{8,9},{9,8},{10,11... | collective-permute-start | bytes 12582920 | tf_op jit(solution)/shard_map/ppermute | solution.py:515
  1.5 17.3 %copy-start = (f32[512,512]{1,0:T(8,128)S(1)}, f32[512,512]{1,0:T(8,128)}, u32[]{:S(2)}) copy-start(f32[512,512]{1,0:T(8,128)} %vo_ref.3) | copy-start | bytes 3145732
  1.5 17.2 %collective-permute-start = (f32[256,512]{1,0:T(8,128)S(1)}, f32[256,512]{1,0:T(8,128)S(1)}, u32[]{:S(2)}, u32[]{:S(2)}) collective-permute-start(f32[256,512]{1,0:T(8,128)S(1)} %slice.12), channel_id=1, source_target_pairs={{0,8},{2,10},{4,12},{6,14},{8,16},{10,18},{12,20},{14,22},{16,24},... | collective-permute-start | bytes 1572872 | tf_op jit(solution)/shard_map/ppermute | solution.py:511
  17.1 2.9 %copy-start.10 = (f32[4,128,128]{2,1,0:T(8,128)S(1)}, f32[4,128,128]{2,1,0:T(8,128)}, u32[]{:S(2)}) copy-start(f32[4,128,128]{2,1,0:T(8,128)} %get-tuple-element.49.own_ref.s_ref) | copy-start | bytes 786436
  17.1 5.9 %copy-start.1 = (f32[4,520,128]{2,1,0:T(8,128)S(1)}, f32[4,520,128]{2,1,0:T(8,128)}, u32[]{:S(2)}) copy-start(f32[4,520,128]{2,1,0:T(8,128)} %get-tuple-element.48.ko_ref) | copy-start | bytes 3194884
  20.0 15.8 %collective-permute-start.2 = (f32[256,512]{1,0:T(8,128)}, f32[256,512]{1,0:T(8,128)S(1)}, u32[]{:S(2)}, u32[]{:S(2)}) collective-permute-start(f32[256,512]{1,0:T(8,128)} %get-tuple-element.50), channel_id=1, source_target_pairs={{0,8},{2,10},{4,12},{6,14},{8,16},{10,18},{12,20},{14,22},{16,24},... | collective-permute-start | bytes 1572872 | tf_op jit(solution)/shard_map/ppermute | solution.py:511
  20.0 8.1 %collective-permute-start.7 = (f32[4,128,128]{2,1,0:T(8,128)S(1)}, f32[4,128,128]{2,1,0:T(8,128)S(1)}, u32[]{:S(2)}, u32[]{:S(2)}) collective-permute-start(f32[4,128,128]{2,1,0:T(8,128)S(1)} %copy-done.10), channel_id=1, source_target_pairs={{0,2},{2,0},{4,6},{6,4},{8,10},{10,8},{12,14},{14,12},{16,18},{18,... | collective-permute-start | bytes 786440 | tf_op jit(solution)/shard_map/ppermute | solution.py:515
  21.5 25.6 %collective-permute-start.4 = (f32[256,512]{1,0:T(8,128)}, f32[256,512]{1,0:T(8,128)S(1)}, u32[]{:S(2)}, u32[]{:S(2)}) collective-permute-start(f32[256,512]{1,0:T(8,128)} %get-tuple-element.81), channel_id=1, source_target_pairs={{0,4},{2,6},{4,0},{6,2},{8,12},{10,14},{12,8},{14,10},{16,20},{18,... | collective-permute-start | bytes 1572872 | tf_op jit(solution)/shard_map/ppermute | solution.py:515
  28.1 1.8 %copy-start.3 = (f32[4,520,128]{2,1,0:T(8,128)S(1)}, f32[4,520,128]{2,1,0:T(8,128)}, u32[]{:S(2)}) copy-start(f32[4,520,128]{2,1,0:T(8,128)} %get-tuple-element.58.qo_ref) | copy-start | bytes 3194884
  28.1 15.3 %copy-start.2 = (f32[512,2048]{1,0:T(8,128)S(1)}, f32[512,2048]{1,0:T(8,128)}, u32[]{:S(2)}) copy-start(f32[512,2048]{1,0:T(8,128)} %own_ref.1) | copy-start | bytes 12582916
  28.4 15.0 %collective-permute-start.8 = (f32[4,128,128]{2,1,0:T(8,128)S(1)}, f32[4,128,128]{2,1,0:T(8,128)S(1)}, u32[]{:S(2)}, u32[]{:S(2)}) collective-permute-start(f32[4,128,128]{2,1,0:T(8,128)S(1)} %joined_steps.1), channel_id=1, source_target_pairs={{0,4},{2,6},{4,8},{6,10},{8,12},{10,14},{12,16},{14,18},{16,20},{1... | collective-permute-start | bytes 786440 | tf_op jit(solution)/shard_map/ppermute | solution.py:511
  29.9 25.6 %collective-permute-start.9 = (f32[4,520,128]{2,1,0:T(8,128)S(1)}, f32[4,520,128]{2,1,0:T(8,128)S(1)}, u32[]{:S(2)}, u32[]{:S(2)}) collective-permute-start(f32[4,520,128]{2,1,0:T(8,128)S(1)} %copy-done.3), channel_id=1, source_target_pairs={{0,2},{2,0},{4,6},{6,4},{8,10},{10,8},{12,14},{14,12},{16,18},{18,... | collective-permute-start | bytes 3194888 | tf_op jit(solution)/shard_map/ppermute | solution.py:515
  35.9 17.5 %collective-permute-start.5 = (f32[256,512]{1,0:T(8,128)S(1)}, f32[256,512]{1,0:T(8,128)S(1)}, u32[]{:S(2)}, u32[]{:S(2)}) collective-permute-start(f32[256,512]{1,0:T(8,128)S(1)} %broadcast_select_fusion.3), channel_id=1, source_target_pairs={{0,4},{2,6},{4,0},{6,2},{8,12},{10,14},{12,8},{14,10},{16,20},{18,... | collective-permute-start | bytes 1572872 | tf_op jit(solution)/shard_map/ppermute | solution.py:515
  38.5 16.8 %collective-permute-start.3 = (f32[2,520,128]{2,1,0:T(8,128)S(1)}, f32[2,520,128]{2,1,0:T(8,128)S(1)}, u32[]{:S(2)}, u32[]{:S(2)}) collective-permute-start(f32[2,520,128]{2,1,0:T(8,128)S(1)} %get-tuple-element.53), channel_id=1, source_target_pairs={{0,8},{2,10},{4,12},{6,14},{8,16},{10,18},{12,20},{14,22},{16,24},... | collective-permute-start | bytes 1597448 | tf_op jit(solution)/shard_map/ppermute | solution.py:511
  43.4 19.7 %collective-permute-start.11 = (f32[2,520,128]{2,1,0:T(8,128)S(1)}, f32[2,520,128]{2,1,0:T(8,128)S(1)}, u32[]{:S(2)}, u32[]{:S(2)}) collective-permute-start(f32[2,520,128]{2,1,0:T(8,128)S(1)} %get-tuple-element.70), channel_id=1, source_target_pairs={{0,8},{2,10},{4,12},{6,14},{8,16},{10,18},{12,20},{14,22},{16,24},... | collective-permute-start | bytes 1597448 | tf_op jit(solution)/shard_map/ppermute | solution.py:511
  47.1 11.9 %copy-start.13 = (bf16[4,512,512]{2,1,0:T(8,128)(2,1)}, bf16[4,512,512]{2,1,0:T(8,128)(2,1)S(1)}, u32[]{:S(2)}) copy-start(bf16[4,512,512]{2,1,0:T(8,128)(2,1)S(1)} %get-tuple-element.61.refs_4_) | copy-start | bytes 6291460
  47.1 11.9 %copy-start.15 = (bf16[4,512,512]{2,1,0:T(8,128)(2,1)}, bf16[4,512,512]{2,1,0:T(8,128)(2,1)S(1)}, u32[]{:S(2)}) copy-start(bf16[4,512,512]{2,1,0:T(8,128)(2,1)S(1)} %get-tuple-element.62.refs_5_) | copy-start | bytes 6291460
  47.1 22.2 %copy-start.4 = (f32[256,512]{1,0:T(8,128)}, f32[256,512]{1,0:T(8,128)S(1)}, u32[]{:S(2)}) copy-start(f32[256,512]{1,0:T(8,128)S(1)} %collective-permute-done.4.v1a_ref) | copy-start | bytes 1572868
  53.3 15.9 %copy-start.7 = (f32[256,512]{1,0:T(8,128)}, f32[256,512]{1,0:T(8,128)S(1)}, u32[]{:S(2)}) copy-start(f32[256,512]{1,0:T(8,128)S(1)} %collective-permute-done.5.v1b_ref) | copy-start | bytes 1572868
  55.4 13.9 %collective-permute-start.6 = (f32[2,520,128]{2,1,0:T(8,128)S(1)}, f32[2,520,128]{2,1,0:T(8,128)S(1)}, u32[]{:S(2)}, u32[]{:S(2)}) collective-permute-start(f32[2,520,128]{2,1,0:T(8,128)S(1)} %broadcast_select_fusion.1), channel_id=1, source_target_pairs={{0,4},{2,6},{4,0},{6,2},{8,12},{10,14},{12,8},{14,10},{16,20},{18,... | collective-permute-start | bytes 1597448 | tf_op jit(solution)/shard_map/ppermute | solution.py:515
  63.2 15.6 %collective-permute-start.12 = (f32[2,520,128]{2,1,0:T(8,128)S(1)}, f32[2,520,128]{2,1,0:T(8,128)S(1)}, u32[]{:S(2)}, u32[]{:S(2)}) collective-permute-start(f32[2,520,128]{2,1,0:T(8,128)S(1)} %broadcast_select_fusion), channel_id=1, source_target_pairs={{0,4},{2,6},{4,0},{6,2},{8,12},{10,14},{12,8},{14,10},{16,20},{18,... | collective-permute-start | bytes 1597448 | tf_op jit(solution)/shard_map/ppermute | solution.py:515
  69.3 4.3 %copy-start.11 = (f32[4,512,128]{2,1,0:T(8,128)S(1)}, f32[4,512,128]{2,1,0:T(8,128)}, u32[]{:S(2)}) copy-start(f32[4,512,128]{2,1,0:T(8,128)} %get-tuple-element.54.od_ref) | copy-start | bytes 3145732
  69.3 4.3 %copy-start.12 = (f32[4,512,128]{2,1,0:T(8,128)S(1)}, f32[4,512,128]{2,1,0:T(8,128)}, u32[]{:S(2)}) copy-start(f32[4,512,128]{2,1,0:T(8,128)} %get-tuple-element.55.ld_ref) | copy-start | bytes 3145732
  72.0 14.8 %collective-permute-start.10 = (f32[2,520,128]{2,1,0:T(8,128)S(1)}, f32[2,520,128]{2,1,0:T(8,128)S(1)}, u32[]{:S(2)}, u32[]{:S(2)}) collective-permute-start(f32[2,520,128]{2,1,0:T(8,128)S(1)} %late.2), channel_id=1, source_target_pairs={{0,2},{2,0},{4,6},{6,4},{8,10},{10,8},{12,14},{14,12},{16,18},{18,... | collective-permute-start | bytes 1597448 | tf_op jit(solution)/shard_map/ppermute | solution.py:515
  73.6 1.0 %copy-start.5 = (f32[256,512]{1,0:T(8,128)S(1)}, f32[256,512]{1,0:T(8,128)}, u32[]{:S(2)}) copy-start(f32[256,512]{1,0:T(8,128)} %copy-done.4) | copy-start | bytes 1572868
  74.6 1.0 %copy-start.8 = (f32[256,512]{1,0:T(8,128)S(1)}, f32[256,512]{1,0:T(8,128)}, u32[]{:S(2)}) copy-start(f32[256,512]{1,0:T(8,128)} %copy-done.7) | copy-start | bytes 1572868
  75.7 3.1 %copy-start.6 = (f32[256,512]{1,0:T(8,128)S(1)}, f32[256,512]{1,0:T(8,128)}, u32[]{:S(2)}) copy-start(f32[256,512]{1,0:T(8,128)} %copy-done.4) | copy-start | bytes 1572868
  75.7 3.1 %copy-start.9 = (f32[256,512]{1,0:T(8,128)S(1)}, f32[256,512]{1,0:T(8,128)}, u32[]{:S(2)}) copy-start(f32[256,512]{1,0:T(8,128)} %copy-done.7) | copy-start | bytes 1572868
  81.5 14.6 %collective-permute-start.13 = (f32[2,520,128]{2,1,0:T(8,128)S(1)}, f32[2,520,128]{2,1,0:T(8,128)S(1)}, u32[]{:S(2)}, u32[]{:S(2)}) collective-permute-start(f32[2,520,128]{2,1,0:T(8,128)S(1)} %late.3), channel_id=1, source_target_pairs={{0,2},{2,0},{4,6},{6,4},{8,10},{10,8},{12,14},{14,12},{16,18},{18,... | collective-permute-start | bytes 1597448 | tf_op jit(solution)/shard_map/ppermute | solution.py:515
  87.3 9.3 %collective-permute-start.14 = (f32[256,256]{1,0:T(8,128)S(1)}, f32[256,256]{1,0:T(8,128)S(1)}, u32[]{:S(2)}, u32[]{:S(2)}) collective-permute-start(f32[256,256]{1,0:T(8,128)S(1)} %get-tuple-element.77), channel_id=1, source_target_pairs={{0,1},{1,0},{2,3},{3,2},{4,5},{5,4},{6,7},{7,6},{8,9},{9,8},{10,11... | collective-permute-start | bytes 786440 | tf_op jit(solution)/shard_map/ppermute | solution.py:515
  96.1 2.1 %copy-start.14 = (bf16[4,512,512]{2,1,0:T(8,128)(2,1)S(1)}, bf16[4,512,512]{2,1,0:T(8,128)(2,1)}, u32[]{:S(2)}) copy-start(bf16[4,512,512]{2,1,0:T(8,128)(2,1)} %copy-done.13) | copy-start | bytes 6291460
  96.1 2.2 %copy-start.16 = (bf16[4,512,512]{2,1,0:T(8,128)(2,1)S(1)}, bf16[4,512,512]{2,1,0:T(8,128)(2,1)}, u32[]{:S(2)}) copy-start(bf16[4,512,512]{2,1,0:T(8,128)(2,1)} %copy-done.15) | copy-start | bytes 6291460
  96.6 1.6 %collective-permute-start.15 = (f32[256,256]{1,0:T(8,128)S(1)}, f32[256,256]{1,0:T(8,128)S(1)}, u32[]{:S(2)}, u32[]{:S(2)}) collective-permute-start(f32[256,256]{1,0:T(8,128)S(1)} %get-tuple-element.78), channel_id=1, source_target_pairs={{0,1},{1,0},{2,3},{3,2},{4,5},{5,4},{6,7},{7,6},{8,9},{9,8},{10,11... | collective-permute-start | bytes 786440 | tf_op jit(solution)/shard_map/ppermute | solution.py:515

commit v5 on v4

--- a/solution.py
+++ b/solution.py
@@ -341,15 +341,15 @@
         lse_ref[0, span, :] = lse
 
 
-def cross_specs(group, per_group, length, rows, dh):
+def cross_specs(group, per_group, length, rows, dh, skip=0):
     return {
-        "all": pl.BlockSpec((1, rows, dh), lambda h, p: (group * per_group + h, 0, 0)),
-        "part": pl.BlockSpec((1, rows, dh), lambda h, p: (h, 0, 0)),
-        "all_values": pl.BlockSpec((length, dh), lambda h, p: (0, group * per_group + h)),
-        "half_values": pl.BlockSpec((length // 2, dh), lambda h, p: (0, group * per_group + h)),
-        "step": pl.BlockSpec((1, dh, dh), lambda h, p: (group * per_group + h, 0, 0)),
-        "all_plain": pl.BlockSpec((1, length, dh), lambda h, p: (group * per_group + h, 0, 0)),
-        "plain": pl.BlockSpec((1, length, dh), lambda h, p: (h, 0, 0)),
+        "all": pl.BlockSpec((1, rows, dh), lambda h, p: (group * per_group + skip + h, 0, 0)),
+        "part": pl.BlockSpec((1, rows, dh), lambda h, p: (skip + h, 0, 0)),
+        "all_values": pl.BlockSpec((length, dh), lambda h, p: (0, group * per_group + skip + h)),
+        "half_values": pl.BlockSpec((length // 2, dh), lambda h, p: (0, group * per_group + skip + h)),
+        "step": pl.BlockSpec((1, dh, dh), lambda h, p: (group * per_group + skip + h, 0, 0)),
+        "all_plain": pl.BlockSpec((1, length, dh), lambda h, p: (group * per_group + skip + h, 0, 0)),
+        "plain": pl.BlockSpec((1, length, dh), lambda h, p: (skip + h, 0, 0)),
     }
 
 
@@ -374,23 +374,23 @@
     )(place, q_near, k_own, values, k2, *v2, joined)
 
 
-def late_part(group, per_group, place, q_near, k1, v1, steps, joined, early, scale):
+def late_part(group, per_group, skip, count, place, q_near, k1, v1, steps, joined, early, scale):
     _, rows, dh = q_near.shape
     length = early[0].shape[1]
-    spec = cross_specs(group, per_group, length, rows, dh)
+    spec = cross_specs(group, per_group, length, rows, dh, skip)
     names = ["all", "part", "half_values", "half_values", "step", "step", "plain", "plain"]
     return pl.pallas_call(
         functools.partial(late_kernel, scale=scale),
         grid_spec=pltpu.PrefetchScalarGridSpec(
             num_scalar_prefetch=1,
-            grid=(per_group,),
+            grid=(count,),
             in_specs=[spec[name] for name in names],
-            out_specs=spec["part"],
+            out_specs=pl.BlockSpec((1, rows, dh), lambda h, p: (h, 0, 0)),
         ),
-        out_shape=jax.ShapeDtypeStruct((per_group, rows, dh), jnp.float32),
+        out_shape=jax.ShapeDtypeStruct((count, rows, dh), jnp.float32),
         compiler_params=pltpu.CompilerParams(vmem_limit_bytes=VMEM_BYTES),
         name="late",
-        cost_estimate=lasting(4.5),
+        cost_estimate=lasting(2 * count),
     )(place, q_near, k1, *v1, steps, joined, *early)
 
 
@@ -433,17 +433,18 @@
     send_ref[...] = jnp.where(first, high, low)
 
 
-def merge(core, o, lse, msg):
-    per_group, length, dh = o.shape
+def merge(core, o, lse, msg, skip):
+    _, length, dh = o.shape
+    count = msg.shape[0]
     share = length // 2
-    head = pl.BlockSpec((1, length, dh), lambda h, c: (h, 0, 0))
+    head = pl.BlockSpec((1, length, dh), lambda h, c: (skip + h, 0, 0))
     out = pl.BlockSpec((share, dh), lambda h, c: (0, h))
-    shape = jax.ShapeDtypeStruct((share, per_group * dh), jnp.float32)
+    shape = jax.ShapeDtypeStruct((share, count * dh), jnp.float32)
     return pl.pallas_call(
         merge_kernel,
         grid_spec=pltpu.PrefetchScalarGridSpec(
             num_scalar_prefetch=1,
-            grid=(per_group,),
+            grid=(count,),
             in_specs=[head, head, pl.BlockSpec((1,) + msg.shape[1:], lambda h, c: (h, 0, 0))],
             out_specs=[out, out],
         ),
@@ -562,11 +563,17 @@
     k1 = [exchanged(source, "ctx", 2) for source in sources]
     kept, received = [], []
     for g in groups:
-        msg = late_part(g, per_group, place, q_near, k1[g], v1, steps, joined, early[g], scale)
+        count = per_group if g < GROUPS - 1 else 1
+        spans = range(0, per_group, count)
+        messages = [
+            late_part(g, per_group, skip, count, place, q_near, k1[g], v1, steps, joined, early[g], scale)
+            for skip in spans
+        ]
         out, lse = own_part(g, per_group, place, q_msg, k1[g], v1, near_steps, joined, od, ld, scale)
-        keep, send = merge(core, out, lse, exchanged(msg, "ctx", 1))
-        kept.append(keep)
-        received.append(exchanged(send, "head", 1))
+        for skip, msg in zip(spans, messages):
+            keep, send = merge(core, out, lse, exchanged(msg, "ctx", 1), skip)
+            kept.append(keep)
+            received.append(exchanged(send, "head", 1))
     return project(kept, received, weights)
 
 

time: 103 us -> 103 us (level)
  local copies, waits for them, and re-layouts: 3.44 us -> 2.25 us
    unnamed x34 -> x28, local copies, waits for them, and re-layouts: 2.3 us -> 1.1 us
    ppermute x11 -> x13, starting transfers between devices: 13.3 us -> 14.2 us  [exchanged(): lax.ppermute(value, axis, [(i, i ^ bit) for i in range(lax.axis_size(axis...]
    ppermute x11 -> x13, waiting for transfers between devices: 23.4 us -> 23.2 us  [exchanged(): lax.ppermute(value, axis, [(i, i ^ bit) for i in range(lax.axis_size(axis...]
    pallas_call x2 -> x3, Pallas kernels: 5.4 us -> 5.33 us  [late_part(): pl.pallas_call(functools.partial(late_kernel, scale=scale), grid_spec=plt...]
  transfers between devices with their start and end apart: 16 -> 18, of which waited for: 11 -> 12; matrix products, arithmetic and copies ran while one was open for 1% -> 1% of each run, Pallas kernels for 34% -> 34%
where the time goes in v5:
time: 103 us
  waiting for transfers between devices  40.3 us (39%)
  Pallas kernels  40 us (39%)
  starting transfers between devices  18.3 us (18%)
  local copies, waits for them, and re-layouts  2.25 us (2%)
  other arithmetic  1.39 us (1%)
    ppermute x13, waiting for transfers between devices, exchanged(): lax.ppermute(value, axis, [(i, i ^ bit) for i in range(lax.axis_size(axis...  23.2 us
    ppermute x5, waiting for transfers between devices, onward(): lax.ppermute(value, 'ctx', [(i, (i + steps) % count) for i in range(count)])  17.1 us
    ppermute x13, starting transfers between devices, exchanged(): lax.ppermute(value, axis, [(i, i ^ bit) for i in range(lax.axis_size(axis...  14.2 us
    pallas_call x1, Pallas kernels, prepare(): pl.pallas_call(functools.partial(prepare_kernel, scale=scale), grid=(head...  12.9 us
    pallas_call x2, Pallas kernels, early_part(): pl.pallas_call(functools.partial(early_kernel, scale=scale), grid_spec=pl...  6.97 us
    pallas_call x3, Pallas kernels, late_part(): pl.pallas_call(functools.partial(late_kernel, scale=scale), grid_spec=plt...  5.33 us
    pallas_call x2, Pallas kernels, own_part(): pl.pallas_call(functools.partial(own_kernel, scale=scale), grid_spec=pltp...  5.28 us
    pallas_call x1, Pallas kernels, project(): pl.pallas_call(project_kernel, grid=(tiles,), in_specs=a_spec + [w_spec]...  4.76 us
  transfers between devices with their start and end apart: 18, of which 12 were waited for; matrix products, arithmetic and copies ran while one was open for 1% of the time, Pallas kernels for 34%

profile of v5, /device:TPU:0, one launch (start us, length us, event | category | flops | bytes accessed | tf_op | source)
XLA Modules:
  0.0 102.5 jit_solution(13855075556685972266)
XLA Ops:
  0.0 0.5 collective-permute-start.1
  0.5 1.1 %slice.12 = f32[256,512]{1,0:T(8,128)S(1)} slice(f32[512,512]{1,0:T(8,128)} %vo_ref.3), slice={[0:256], [0:512]} | slice | bytes 1048576 | tf_op jit(solution)/shard_map/slice | solution.py:534
  1.5 0.0 copy-start
  1.5 2.6 %collective-permute-start = (f32[256,512]{1,0:T(8,128)S(1)}, f32[256,512]{1,0:T(8,128)S(1)}, u32[]{:S(2)}, u32[]{:S(2)}) collective-permute-start(f32[256,512]{1,0:T(8,128)S(1)} %slice.12), channel_id=1, source_target_pairs={{0,8},{2,10},{4,12},{6,14},{8,16},{10,18},{12,20},{14,22},{16,24},... | collective-permute-start | bytes 1572872 | tf_op jit(solution)/shard_map/ppermute | solution.py:512
  4.2 12.9 %prepare.1 = (f32[4,520,128]{2,1,0:T(8,128)}, f32[4,520,128]{2,1,0:T(8,128)}, f32[4,128,128]{2,1,0:T(8,128)}, f32[4,512,128]{2,1,0:T(8,128)}, f32[4,512,128]{2,1,0:T(8,128)}) custom-call(f32[512,512]{1,0:T(8,128)} %q_ref.1, f32[512,512]{1,0:T(8,128)} %k_ref.1, f32[512,512]{1,0:T(8,128)} %vo_ref.3, f32[512,512]{1,0:T(8,128)} %w_ref.1, f32[4,512]{1,0:T(4,128)} %beta_ref.1, ...), custom_call_target="tpu_custom_call" | custom-call | flops 14949999616 | bytes 1000 | tf_op jit(solution)/shard_map/prepare/pallas_call | solution.py:221
  17.1 1.7 %collective-permute-done.v2a_ref = f32[256,512]{1,0:T(8,128)S(1)} collective-permute-done((f32[256,512]{1,0:T(8,128)S(1)}, f32[256,512]{1,0:T(8,128)S(1)}, u32[]{:S(2)}, u32[]{:S(2)}) %collective-permute-start) | collective-permute-done | bytes 524320 | tf_op jit(solution)/shard_map/ppermute | solution.py:512
  18.8 0.0 collective-permute-done.1.other_ref
  18.8 1.2 %broadcast_select_fusion.2 = (f32[256,512]{1,0:T(8,128)}, f32[256,512]{1,0:T(8,128)}) fusion(f32[256,512]{1,0:T(8,128)S(1)} %collective-permute-done.v2a_ref, pred[]{:T(512)S(6)} %ge.3, f32[512,512]{1,0:T(8,128)S(1)} %copy-done), kind=kLoop, calls=%fused_computation.2 | loop fusion | flops 131072 | bytes 2621441 | tf_op jit(solution)/shard_map/jit(_where)/select_n | solution.py:537
  20.0 0.0 collective-permute-start.2
  20.0 0.0 copy-done.7
  20.0 1.5 %collective-permute-start.7 = (f32[4,128,128]{2,1,0:T(8,128)S(1)}, f32[4,128,128]{2,1,0:T(8,128)S(1)}, u32[]{:S(2)}, u32[]{:S(2)}) collective-permute-start(f32[4,128,128]{2,1,0:T(8,128)S(1)} %copy-done.7), channel_id=1, source_target_pairs={{0,2},{2,0},{4,6},{6,4},{8,10},{10,8},{12,14},{14,12},{16,18},{18,... | collective-permute-start | bytes 786440 | tf_op jit(solution)/shard_map/ppermute | solution.py:516
  21.5 1.5 %collective-permute-start.4 = (f32[256,512]{1,0:T(8,128)}, f32[256,512]{1,0:T(8,128)S(1)}, u32[]{:S(2)}, u32[]{:S(2)}) collective-permute-start(f32[256,512]{1,0:T(8,128)} %get-tuple-element.85), channel_id=1, source_target_pairs={{0,4},{2,6},{4,0},{6,2},{8,12},{10,14},{12,8},{14,10},{16,20},{18,... | collective-permute-start | bytes 1572872 | tf_op jit(solution)/shard_map/ppermute | solution.py:516
  23.0 0.1 fusion
  23.1 5.1 %collective-permute-done.7.near_ref.s_ref = f32[4,128,128]{2,1,0:T(8,128)S(1)} collective-permute-done((f32[4,128,128]{2,1,0:T(8,128)S(1)}, f32[4,128,128]{2,1,0:T(8,128)S(1)}, u32[]{:S(2)}, u32[]{:S(2)}) %collective-permute-start.7) | collective-permute-done | bytes 262176 | tf_op jit(solution)/shard_map/ppermute | solution.py:516
  28.2 0.3 joined_steps.1
  28.4 1.5 %collective-permute-start.8 = (f32[4,128,128]{2,1,0:T(8,128)S(1)}, f32[4,128,128]{2,1,0:T(8,128)S(1)}, u32[]{:S(2)}, u32[]{:S(2)}) collective-permute-start(f32[4,128,128]{2,1,0:T(8,128)S(1)} %joined_steps.1), channel_id=1, source_target_pairs={{0,4},{2,6},{4,8},{6,10},{8,12},{10,14},{12,16},{14,18},{16,20},{1... | collective-permute-start | bytes 786440 | tf_op jit(solution)/shard_map/ppermute | solution.py:512
  29.9 1.5 %collective-permute-start.9 = (f32[4,520,128]{2,1,0:T(8,128)S(1)}, f32[4,520,128]{2,1,0:T(8,128)S(1)}, u32[]{:S(2)}, u32[]{:S(2)}) collective-permute-start(f32[4,520,128]{2,1,0:T(8,128)S(1)} %copy-done.3), channel_id=1, source_target_pairs={{0,2},{2,0},{4,6},{6,4},{8,10},{10,8},{12,14},{14,12},{16,18},{18,... | collective-permute-start | bytes 3194888 | tf_op jit(solution)/shard_map/ppermute | solution.py:516
  31.4 4.3 %collective-permute-done.2.v2b_ref = f32[256,512]{1,0:T(8,128)S(1)} collective-permute-done((f32[256,512]{1,0:T(8,128)}, f32[256,512]{1,0:T(8,128)S(1)}, u32[]{:S(2)}, u32[]{:S(2)}) %collective-permute-start.2) | collective-permute-done | bytes 524320 | tf_op jit(solution)/shard_map/ppermute | solution.py:512
  35.8 0.1 broadcast_select_fusion.3
  35.9 2.6 %collective-permute-start.5 = (f32[256,512]{1,0:T(8,128)S(1)}, f32[256,512]{1,0:T(8,128)S(1)}, u32[]{:S(2)}, u32[]{:S(2)}) collective-permute-start(f32[256,512]{1,0:T(8,128)S(1)} %broadcast_select_fusion.3), channel_id=1, source_target_pairs={{0,4},{2,6},{4,0},{6,2},{8,12},{10,14},{12,8},{14,10},{16,20},{18,... | collective-permute-start | bytes 1572872 | tf_op jit(solution)/shard_map/ppermute | solution.py:516
  38.5 0.0 collective-permute-start.3
  38.5 4.9 %collective-permute-done.8.u_ref = f32[4,128,128]{2,1,0:T(8,128)S(1)} collective-permute-done((f32[4,128,128]{2,1,0:T(8,128)S(1)}, f32[4,128,128]{2,1,0:T(8,128)S(1)}, u32[]{:S(2)}, u32[]{:S(2)}) %collective-permute-start.8) | collective-permute-done | bytes 262176 | tf_op jit(solution)/shard_map/ppermute | solution.py:512
  43.4 0.0 collective-permute-start.11
  43.4 0.0 copy-done.2
  43.5 3.6 %weight_halves.1 = (bf16[4,512,512]{2,1,0:T(8,128)(2,1)S(1)}, bf16[4,512,512]{2,1,0:T(8,128)(2,1)S(1)}, bf16[4,512,512]{2,1,0:T(8,128)(2,1)S(1)}, bf16[4,512,512]{2,1,0:T(8,128)(2,1)S(1)}) custom-call(f32[512,2048]{1,0:T(8,128)S(1)} %copy-done.2, f32[512,2048]{1,0:T(8,128)} %collective-permute-done.1.other_ref), custom_call_target="tpu_custom_call" | custom-call | flops 8049999872 | bytes 1000 | tf_op jit(solution)/shard_map/weight_halves/pallas_call | solution.py:468
  47.1 0.0 copy-start.10
  47.1 0.0 collective-permute-done.4.v1a_ref
  47.1 0.0 copy-start.4
  47.1 6.2 %collective-permute-done.5.v1b_ref = f32[256,512]{1,0:T(8,128)S(1)} collective-permute-done((f32[256,512]{1,0:T(8,128)S(1)}, f32[256,512]{1,0:T(8,128)S(1)}, u32[]{:S(2)}, u32[]{:S(2)}) %collective-permute-start.5) | collective-permute-done | bytes 524320 | tf_op jit(solution)/shard_map/ppermute | solution.py:516
  53.3 2.0 %collective-permute-done.3.k2_ref = f32[2,520,128]{2,1,0:T(8,128)S(1)} collective-permute-done((f32[2,520,128]{2,1,0:T(8,128)S(1)}, f32[2,520,128]{2,1,0:T(8,128)S(1)}, u32[]{:S(2)}, u32[]{:S(2)}) %collective-permute-start.3) | collective-permute-done | bytes 532512 | tf_op jit(solution)/shard_map/ppermute | solution.py:512
  55.3 0.1 broadcast_select_fusion.1
  55.4 0.2 collective-permute-start.6
  55.5 0.0 collective-permute-done.9.qp_ref
  55.5 3.5 %early.2 = (f32[2,512,128]{2,1,0:T(8,128)S(1)}, f32[2,512,128]{2,1,0:T(8,128)S(1)}) custom-call(s32[1]{0:T(128)} %bitcast.1.place_ref, f32[4,520,128]{2,1,0:T(8,128)S(1)} %collective-permute-done.9.qp_ref, f32[4,520,128]{2,1,0:T(8,128)S(1)} %copy-done.1, f32[512,512]{1,0:T(8,128)S(1)} %copy-done, f32[2,520,128]{2,1,0:T(8,128)S(1)} %collective-permute-done.3.k2_ref, ...), custom_call_target="tpu_custom_call" | custom-call | flops 5175000064 | bytes 1000 | tf_op jit(solution)/shard_map/early/pallas_call | solution.py:362
  59.0 4.1 %collective-permute-done.11.k2_ref = f32[2,520,128]{2,1,0:T(8,128)S(1)} collective-permute-done((f32[2,520,128]{2,1,0:T(8,128)S(1)}, f32[2,520,128]{2,1,0:T(8,128)S(1)}, u32[]{:S(2)}, u32[]{:S(2)}) %collective-permute-start.11) | collective-permute-done | bytes 532512 | tf_op jit(solution)/shard_map/ppermute | solution.py:512
  63.2 0.1 broadcast_select_fusion
  63.2 2.5 %collective-permute-start.12 = (f32[2,520,128]{2,1,0:T(8,128)S(1)}, f32[2,520,128]{2,1,0:T(8,128)S(1)}, u32[]{:S(2)}, u32[]{:S(2)}) collective-permute-start(f32[2,520,128]{2,1,0:T(8,128)S(1)} %broadcast_select_fusion), channel_id=1, source_target_pairs={{0,4},{2,6},{4,0},{6,2},{8,12},{10,14},{12,8},{14,10},{16,20},{18,... | collective-permute-start | bytes 1597448 | tf_op jit(solution)/shard_map/ppermute | solution.py:516
  65.8 3.5 %early.3 = (f32[2,512,128]{2,1,0:T(8,128)S(1)}, f32[2,512,128]{2,1,0:T(8,128)S(1)}) custom-call(s32[1]{0:T(128)} %bitcast.1.place_ref, f32[4,520,128]{2,1,0:T(8,128)S(1)} %collective-permute-done.9.qp_ref, f32[4,520,128]{2,1,0:T(8,128)S(1)} %copy-done.1, f32[512,512]{1,0:T(8,128)S(1)} %copy-done, f32[2,520,128]{2,1,0:T(8,128)S(1)} %collective-permute-done.11.k2_ref, ...), custom_call_target="tpu_custom_call" | custom-call | flops 5175000064 | bytes 1000 | tf_op jit(solution)/shard_map/early/pallas_call | solution.py:362
  69.3 0.0 collective-permute-done.6.k1_ref
  69.3 2.7 %late.3 = f32[2,520,128]{2,1,0:T(8,128)S(1)} custom-call(s32[1]{0:T(128)} %bitcast.1.place_ref, f32[4,520,128]{2,1,0:T(8,128)S(1)} %collective-permute-done.9.qp_ref, f32[2,520,128]{2,1,0:T(8,128)S(1)} %collective-permute-done.6.k1_ref, f32[256,512]{1,0:T(8,128)S(1)} %collective-permute-done.4.v1a_ref, f32[256,512]{1,0:T(8,128)S(1)} %collective-permute-done.5.v1b_ref, ...), custom_call_target="tpu_custom_call" | custom-call | flops 4600000000 | bytes 1000 | tf_op jit(solution)/shard_map/late/pallas_call | solution.py:382
  72.0 1.6 %collective-permute-start.10 = (f32[2,520,128]{2,1,0:T(8,128)S(1)}, f32[2,520,128]{2,1,0:T(8,128)S(1)}, u32[]{:S(2)}, u32[]{:S(2)}) collective-permute-start(f32[2,520,128]{2,1,0:T(8,128)S(1)} %late.3), channel_id=1, source_target_pairs={{0,2},{2,0},{4,6},{6,4},{8,10},{10,8},{12,14},{14,12},{16,18},{18,... | collective-permute-start | bytes 1597448 | tf_op jit(solution)/shard_map/ppermute | solution.py:516
  73.6 1.0 %copy-done.5 = f32[256,512]{1,0:T(8,128)S(1)} copy-done((f32[256,512]{1,0:T(8,128)S(1)}, f32[256,512]{1,0:T(8,128)}, u32[]{:S(2)}) %copy-start.5) | copy-done | bytes 524312
  74.6 2.6 %own.2 = (f32[2,512,128]{2,1,0:T(8,128)S(1)}, f32[2,512,128]{2,1,0:T(8,128)S(1)}) custom-call(s32[1]{0:T(128)} %bitcast.1.place_ref, f32[4,520,128]{2,1,0:T(8,128)S(1)} %copy-done.3, f32[2,520,128]{2,1,0:T(8,128)S(1)} %collective-permute-done.6.k1_ref, f32[256,512]{1,0:T(8,128)S(1)} %copy-done.5, f32[256,512]{1,0:T(8,128)S(1)} %collective-permute-done.5.v1b_ref, ...), custom_call_target="tpu_custom_call" | custom-call | flops 5175000064 | bytes 1000 | tf_op jit(solution)/shard_map/own/pallas_call | solution.py:403
  77.3 1.5 %collective-permute-done.12.k1_ref = f32[2,520,128]{2,1,0:T(8,128)S(1)} collective-permute-done((f32[2,520,128]{2,1,0:T(8,128)S(1)}, f32[2,520,128]{2,1,0:T(8,128)S(1)}, u32[]{:S(2)}, u32[]{:S(2)}) %collective-permute-start.12) | collective-permute-done | bytes 532512 | tf_op jit(solution)/shard_map/ppermute | solution.py:516
  78.8 0.0 copy-done.6
  78.8 1.3 %late.5 = f32[1,520,128]{2,1,0:T(8,128)S(1)} custom-call(s32[1]{0:T(128)} %bitcast.1.place_ref, f32[4,520,128]{2,1,0:T(8,128)S(1)} %collective-permute-done.9.qp_ref, f32[2,520,128]{2,1,0:T(8,128)S(1)} %collective-permute-done.12.k1_ref, f32[256,512]{1,0:T(8,128)S(1)} %copy-done.6, f32[256,512]{1,0:T(8,128)S(1)} %collective-permute-done.5.v1b_ref, ...), custom_call_target="tpu_custom_call" | custom-call | flops 2300000000 | bytes 1000 | tf_op jit(solution)/shard_map/late/pallas_call | solution.py:382
  80.1 1.3 %collective-permute-start.14 = (f32[1,520,128]{2,1,0:T(8,128)S(1)}, f32[1,520,128]{2,1,0:T(8,128)S(1)}, u32[]{:S(2)}, u32[]{:S(2)}) collective-permute-start(f32[1,520,128]{2,1,0:T(8,128)S(1)} %late.5), channel_id=1, source_target_pairs={{0,2},{2,0},{4,6},{6,4},{8,10},{10,8},{12,14},{14,12},{16,18},{18,... | collective-permute-start | bytes 798728 | tf_op jit(solution)/shard_map/ppermute | solution.py:516
  81.4 1.3 %late.4 = f32[1,520,128]{2,1,0:T(8,128)S(1)} custom-call(s32[1]{0:T(128)} %bitcast.1.place_ref, f32[4,520,128]{2,1,0:T(8,128)S(1)} %collective-permute-done.9.qp_ref, f32[2,520,128]{2,1,0:T(8,128)S(1)} %collective-permute-done.12.k1_ref, f32[256,512]{1,0:T(8,128)S(1)} %copy-done.6, f32[256,512]{1,0:T(8,128)S(1)} %collective-permute-done.5.v1b_ref, ...), custom_call_target="tpu_custom_call" | custom-call | flops 2300000000 | bytes 1000 | tf_op jit(solution)/shard_map/late/pallas_call | solution.py:382
  82.7 0.8 collective-permute-start.13
  83.5 2.6 %own.3 = (f32[2,512,128]{2,1,0:T(8,128)S(1)}, f32[2,512,128]{2,1,0:T(8,128)S(1)}) custom-call(s32[1]{0:T(128)} %bitcast.1.place_ref, f32[4,520,128]{2,1,0:T(8,128)S(1)} %copy-done.3, f32[2,520,128]{2,1,0:T(8,128)S(1)} %collective-permute-done.12.k1_ref, f32[256,512]{1,0:T(8,128)S(1)} %copy-done.6, f32[256,512]{1,0:T(8,128)S(1)} %collective-permute-done.5.v1b_ref, ...), custom_call_target="tpu_custom_call" | custom-call | flops 5175000064 | bytes 1000 | tf_op jit(solution)/shard_map/own/pallas_call | solution.py:403
  86.2 1.0 collective-permute-done.10.msg_ref
  87.1 0.5 merge.3
  87.6 0.1 collective-permute-start.15
  87.7 5.2 %collective-permute-done.14.msg_ref = f32[1,520,128]{2,1,0:T(8,128)S(1)} collective-permute-done((f32[1,520,128]{2,1,0:T(8,128)S(1)}, f32[1,520,128]{2,1,0:T(8,128)S(1)}, u32[]{:S(2)}, u32[]{:S(2)}) %collective-permute-start.14) | collective-permute-done | bytes 266272 | tf_op jit(solution)/shard_map/ppermute | solution.py:516
  92.8 0.2 merge.5
  93.0 0.0 copy-start.11
  93.1 0.1 collective-permute-start.17
  93.1 3.0 %collective-permute-done.13.msg_ref = f32[1,520,128]{2,1,0:T(8,128)S(1)} collective-permute-done((f32[1,520,128]{2,1,0:T(8,128)S(1)}, f32[1,520,128]{2,1,0:T(8,128)S(1)}, u32[]{:S(2)}, u32[]{:S(2)}) %collective-permute-start.13) | collective-permute-done | bytes 266272 | tf_op jit(solution)/shard_map/ppermute | solution.py:516
  96.1 0.2 merge.4
  96.3 0.1 collective-permute-start.16
  96.4 0.0 collective-permute-done.17.refs_5_
  96.4 1.3 %collective-permute-done.16.refs_4_ = f32[256,128]{1,0:T(8,128)S(1)} collective-permute-done((f32[256,128]{1,0:T(8,128)S(1)}, f32[256,128]{1,0:T(8,128)S(1)}, u32[]{:S(2)}, u32[]{:S(2)}) %collective-permute-start.16) | collective-permute-done | bytes 131104 | tf_op jit(solution)/shard_map/ppermute | solution.py:516
  97.7 0.0 collective-permute-done.15.refs_3_
  97.7 4.8 %project.1 = f32[256,2048]{1,0:T(8,128)} custom-call(f32[256,256]{1,0:T(8,128)S(1)} %get-tuple-element.70.refs_0_, f32[256,128]{1,0:T(8,128)S(1)} %get-tuple-element.78.refs_1_, f32[256,128]{1,0:T(8,128)S(1)} %get-tuple-element.79.refs_2_, f32[256,256]{1,0:T(8,128)S(1)} %collective-permute-done.15.refs_3_, f32[256,128]{1,0:T(8,128)S(1)} %collective-permute-done.16.refs_4_, ...), custom_call_target="tpu_custom_call" | custom-call | flops 8625000448 | bytes 1000 | tf_op jit(solution)/shard_map/project/pallas_call | solution.py:498
  (20 shorter events, 0.0 us)
Async XLA Ops:
  0.0 18.8 %collective-permute-start.1 = (f32[512,2048]{1,0:T(8,128)}, f32[512,2048]{1,0:T(8,128)}, u32[]{:S(2)}, u32[]{:S(2)}) collective-permute-start(f32[512,2048]{1,0:T(8,128)} %own_ref.1), channel_id=1, source_target_pairs={{0,1},{1,0},{2,3},{3,2},{4,5},{5,4},{6,7},{7,6},{8,9},{9,8},{10,11... | collective-permute-start | bytes 12582920 | tf_op jit(solution)/shard_map/ppermute | solution.py:516
  1.5 17.3 %copy-start = (f32[512,512]{1,0:T(8,128)S(1)}, f32[512,512]{1,0:T(8,128)}, u32[]{:S(2)}) copy-start(f32[512,512]{1,0:T(8,128)} %vo_ref.3) | copy-start | bytes 3145732
  1.5 17.2 %collective-permute-start = (f32[256,512]{1,0:T(8,128)S(1)}, f32[256,512]{1,0:T(8,128)S(1)}, u32[]{:S(2)}, u32[]{:S(2)}) collective-permute-start(f32[256,512]{1,0:T(8,128)S(1)} %slice.12), channel_id=1, source_target_pairs={{0,8},{2,10},{4,12},{6,14},{8,16},{10,18},{12,20},{14,22},{16,24},... | collective-permute-start | bytes 1572872 | tf_op jit(solution)/shard_map/ppermute | solution.py:512
  17.1 2.9 %copy-start.7 = (f32[4,128,128]{2,1,0:T(8,128)S(1)}, f32[4,128,128]{2,1,0:T(8,128)}, u32[]{:S(2)}) copy-start(f32[4,128,128]{2,1,0:T(8,128)} %get-tuple-element.51.own_ref.s_ref) | copy-start | bytes 786436
  17.1 5.9 %copy-start.1 = (f32[4,520,128]{2,1,0:T(8,128)S(1)}, f32[4,520,128]{2,1,0:T(8,128)}, u32[]{:S(2)}) copy-start(f32[4,520,128]{2,1,0:T(8,128)} %get-tuple-element.50.ko_ref) | copy-start | bytes 3194884
  20.0 15.8 %collective-permute-start.2 = (f32[256,512]{1,0:T(8,128)}, f32[256,512]{1,0:T(8,128)S(1)}, u32[]{:S(2)}, u32[]{:S(2)}) collective-permute-start(f32[256,512]{1,0:T(8,128)} %get-tuple-element.52), channel_id=1, source_target_pairs={{0,8},{2,10},{4,12},{6,14},{8,16},{10,18},{12,20},{14,22},{16,24},... | collective-permute-start | bytes 1572872 | tf_op jit(solution)/shard_map/ppermute | solution.py:512
  20.0 8.1 %collective-permute-start.7 = (f32[4,128,128]{2,1,0:T(8,128)S(1)}, f32[4,128,128]{2,1,0:T(8,128)S(1)}, u32[]{:S(2)}, u32[]{:S(2)}) collective-permute-start(f32[4,128,128]{2,1,0:T(8,128)S(1)} %copy-done.7), channel_id=1, source_target_pairs={{0,2},{2,0},{4,6},{6,4},{8,10},{10,8},{12,14},{14,12},{16,18},{18,... | collective-permute-start | bytes 786440 | tf_op jit(solution)/shard_map/ppermute | solution.py:516
  21.5 25.6 %collective-permute-start.4 = (f32[256,512]{1,0:T(8,128)}, f32[256,512]{1,0:T(8,128)S(1)}, u32[]{:S(2)}, u32[]{:S(2)}) collective-permute-start(f32[256,512]{1,0:T(8,128)} %get-tuple-element.85), channel_id=1, source_target_pairs={{0,4},{2,6},{4,0},{6,2},{8,12},{10,14},{12,8},{14,10},{16,20},{18,... | collective-permute-start | bytes 1572872 | tf_op jit(solution)/shard_map/ppermute | solution.py:516
  28.1 1.8 %copy-start.3 = (f32[4,520,128]{2,1,0:T(8,128)S(1)}, f32[4,520,128]{2,1,0:T(8,128)}, u32[]{:S(2)}) copy-start(f32[4,520,128]{2,1,0:T(8,128)} %get-tuple-element.60.qo_ref) | copy-start | bytes 3194884
  28.1 15.3 %copy-start.2 = (f32[512,2048]{1,0:T(8,128)S(1)}, f32[512,2048]{1,0:T(8,128)}, u32[]{:S(2)}) copy-start(f32[512,2048]{1,0:T(8,128)} %own_ref.1) | copy-start | bytes 12582916
  28.4 15.0 %collective-permute-start.8 = (f32[4,128,128]{2,1,0:T(8,128)S(1)}, f32[4,128,128]{2,1,0:T(8,128)S(1)}, u32[]{:S(2)}, u32[]{:S(2)}) collective-permute-start(f32[4,128,128]{2,1,0:T(8,128)S(1)} %joined_steps.1), channel_id=1, source_target_pairs={{0,4},{2,6},{4,8},{6,10},{8,12},{10,14},{12,16},{14,18},{16,20},{1... | collective-permute-start | bytes 786440 | tf_op jit(solution)/shard_map/ppermute | solution.py:512
  29.9 25.6 %collective-permute-start.9 = (f32[4,520,128]{2,1,0:T(8,128)S(1)}, f32[4,520,128]{2,1,0:T(8,128)S(1)}, u32[]{:S(2)}, u32[]{:S(2)}) collective-permute-start(f32[4,520,128]{2,1,0:T(8,128)S(1)} %copy-done.3), channel_id=1, source_target_pairs={{0,2},{2,0},{4,6},{6,4},{8,10},{10,8},{12,14},{14,12},{16,18},{18,... | collective-permute-start | bytes 3194888 | tf_op jit(solution)/shard_map/ppermute | solution.py:516
  35.9 17.5 %collective-permute-start.5 = (f32[256,512]{1,0:T(8,128)S(1)}, f32[256,512]{1,0:T(8,128)S(1)}, u32[]{:S(2)}, u32[]{:S(2)}) collective-permute-start(f32[256,512]{1,0:T(8,128)S(1)} %broadcast_select_fusion.3), channel_id=1, source_target_pairs={{0,4},{2,6},{4,0},{6,2},{8,12},{10,14},{12,8},{14,10},{16,20},{18,... | collective-permute-start | bytes 1572872 | tf_op jit(solution)/shard_map/ppermute | solution.py:516
  38.5 16.8 %collective-permute-start.3 = (f32[2,520,128]{2,1,0:T(8,128)S(1)}, f32[2,520,128]{2,1,0:T(8,128)S(1)}, u32[]{:S(2)}, u32[]{:S(2)}) collective-permute-start(f32[2,520,128]{2,1,0:T(8,128)S(1)} %get-tuple-element.55), channel_id=1, source_target_pairs={{0,8},{2,10},{4,12},{6,14},{8,16},{10,18},{12,20},{14,22},{16,24},... | collective-permute-start | bytes 1597448 | tf_op jit(solution)/shard_map/ppermute | solution.py:512
  43.4 19.7 %collective-permute-start.11 = (f32[2,520,128]{2,1,0:T(8,128)S(1)}, f32[2,520,128]{2,1,0:T(8,128)S(1)}, u32[]{:S(2)}, u32[]{:S(2)}) collective-permute-start(f32[2,520,128]{2,1,0:T(8,128)S(1)} %get-tuple-element.72), channel_id=1, source_target_pairs={{0,8},{2,10},{4,12},{6,14},{8,16},{10,18},{12,20},{14,22},{16,24},... | collective-permute-start | bytes 1597448 | tf_op jit(solution)/shard_map/ppermute | solution.py:512
  47.1 11.9 %copy-start.10 = (bf16[4,512,512]{2,1,0:T(8,128)(2,1)}, bf16[4,512,512]{2,1,0:T(8,128)(2,1)S(1)}, u32[]{:S(2)}) copy-start(bf16[4,512,512]{2,1,0:T(8,128)(2,1)S(1)} %get-tuple-element.63.refs_6_) | copy-start | bytes 6291460
  47.1 11.9 %copy-start.12 = (bf16[4,512,512]{2,1,0:T(8,128)(2,1)}, bf16[4,512,512]{2,1,0:T(8,128)(2,1)S(1)}, u32[]{:S(2)}) copy-start(bf16[4,512,512]{2,1,0:T(8,128)(2,1)S(1)} %get-tuple-element.64.refs_7_) | copy-start | bytes 6291460
  47.1 22.2 %copy-start.4 = (f32[256,512]{1,0:T(8,128)}, f32[256,512]{1,0:T(8,128)S(1)}, u32[]{:S(2)}) copy-start(f32[256,512]{1,0:T(8,128)S(1)} %collective-permute-done.4.v1a_ref) | copy-start | bytes 1572868
  55.4 13.9 %collective-permute-start.6 = (f32[2,520,128]{2,1,0:T(8,128)S(1)}, f32[2,520,128]{2,1,0:T(8,128)S(1)}, u32[]{:S(2)}, u32[]{:S(2)}) collective-permute-start(f32[2,520,128]{2,1,0:T(8,128)S(1)} %broadcast_select_fusion.1), channel_id=1, source_target_pairs={{0,4},{2,6},{4,0},{6,2},{8,12},{10,14},{12,8},{14,10},{16,20},{18,... | collective-permute-start | bytes 1597448 | tf_op jit(solution)/shard_map/ppermute | solution.py:516
  63.2 15.6 %collective-permute-start.12 = (f32[2,520,128]{2,1,0:T(8,128)S(1)}, f32[2,520,128]{2,1,0:T(8,128)S(1)}, u32[]{:S(2)}, u32[]{:S(2)}) collective-permute-start(f32[2,520,128]{2,1,0:T(8,128)S(1)} %broadcast_select_fusion), channel_id=1, source_target_pairs={{0,4},{2,6},{4,0},{6,2},{8,12},{10,14},{12,8},{14,10},{16,20},{18,... | collective-permute-start | bytes 1597448 | tf_op jit(solution)/shard_map/ppermute | solution.py:516
  69.3 4.3 %copy-start.8 = (f32[4,512,128]{2,1,0:T(8,128)S(1)}, f32[4,512,128]{2,1,0:T(8,128)}, u32[]{:S(2)}) copy-start(f32[4,512,128]{2,1,0:T(8,128)} %get-tuple-element.56.od_ref) | copy-start | bytes 3145732
  69.3 4.3 %copy-start.9 = (f32[4,512,128]{2,1,0:T(8,128)S(1)}, f32[4,512,128]{2,1,0:T(8,128)}, u32[]{:S(2)}) copy-start(f32[4,512,128]{2,1,0:T(8,128)} %get-tuple-element.57.ld_ref) | copy-start | bytes 3145732
  72.0 15.1 %collective-permute-start.10 = (f32[2,520,128]{2,1,0:T(8,128)S(1)}, f32[2,520,128]{2,1,0:T(8,128)S(1)}, u32[]{:S(2)}, u32[]{:S(2)}) collective-permute-start(f32[2,520,128]{2,1,0:T(8,128)S(1)} %late.3), channel_id=1, source_target_pairs={{0,2},{2,0},{4,6},{6,4},{8,10},{10,8},{12,14},{14,12},{16,18},{18,... | collective-permute-start | bytes 1597448 | tf_op jit(solution)/shard_map/ppermute | solution.py:516
  73.6 1.0 %copy-start.5 = (f32[256,512]{1,0:T(8,128)S(1)}, f32[256,512]{1,0:T(8,128)}, u32[]{:S(2)}) copy-start(f32[256,512]{1,0:T(8,128)} %copy-done.4) | copy-start | bytes 1572868
  74.6 4.2 %copy-start.6 = (f32[256,512]{1,0:T(8,128)S(1)}, f32[256,512]{1,0:T(8,128)}, u32[]{:S(2)}) copy-start(f32[256,512]{1,0:T(8,128)} %copy-done.4) | copy-start | bytes 1572868
  80.1 12.7 %collective-permute-start.14 = (f32[1,520,128]{2,1,0:T(8,128)S(1)}, f32[1,520,128]{2,1,0:T(8,128)S(1)}, u32[]{:S(2)}, u32[]{:S(2)}) collective-permute-start(f32[1,520,128]{2,1,0:T(8,128)S(1)} %late.5), channel_id=1, source_target_pairs={{0,2},{2,0},{4,6},{6,4},{8,10},{10,8},{12,14},{14,12},{16,18},{18,... | collective-permute-start | bytes 798728 | tf_op jit(solution)/shard_map/ppermute | solution.py:516
  82.7 13.4 %collective-permute-start.13 = (f32[1,520,128]{2,1,0:T(8,128)S(1)}, f32[1,520,128]{2,1,0:T(8,128)S(1)}, u32[]{:S(2)}, u32[]{:S(2)}) collective-permute-start(f32[1,520,128]{2,1,0:T(8,128)S(1)} %late.4), channel_id=1, source_target_pairs={{0,2},{2,0},{4,6},{6,4},{8,10},{10,8},{12,14},{14,12},{16,18},{18,... | collective-permute-start | bytes 798728 | tf_op jit(solution)/shard_map/ppermute | solution.py:516
  87.6 10.1 %collective-permute-start.15 = (f32[256,256]{1,0:T(8,128)S(1)}, f32[256,256]{1,0:T(8,128)S(1)}, u32[]{:S(2)}, u32[]{:S(2)}) collective-permute-start(f32[256,256]{1,0:T(8,128)S(1)} %get-tuple-element.80), channel_id=1, source_target_pairs={{0,1},{1,0},{2,3},{3,2},{4,5},{5,4},{6,7},{7,6},{8,9},{9,8},{10,11... | collective-permute-start | bytes 786440 | tf_op jit(solution)/shard_map/ppermute | solution.py:516
  93.0 4.7 %copy-start.11 = (bf16[4,512,512]{2,1,0:T(8,128)(2,1)S(1)}, bf16[4,512,512]{2,1,0:T(8,128)(2,1)}, u32[]{:S(2)}) copy-start(bf16[4,512,512]{2,1,0:T(8,128)(2,1)} %copy-done.10) | copy-start | bytes 6291460
  93.0 4.7 %copy-start.13 = (bf16[4,512,512]{2,1,0:T(8,128)(2,1)S(1)}, bf16[4,512,512]{2,1,0:T(8,128)(2,1)}, u32[]{:S(2)}) copy-start(bf16[4,512,512]{2,1,0:T(8,128)(2,1)} %copy-done.12) | copy-start | bytes 6291460
  93.1 3.3 %collective-permute-start.17 = (f32[256,128]{1,0:T(8,128)S(1)}, f32[256,128]{1,0:T(8,128)S(1)}, u32[]{:S(2)}, u32[]{:S(2)}) collective-permute-start(f32[256,128]{1,0:T(8,128)S(1)} %get-tuple-element.82), channel_id=1, source_target_pairs={{0,1},{1,0},{2,3},{3,2},{4,5},{5,4},{6,7},{7,6},{8,9},{9,8},{10,11... | collective-permute-start | bytes 393224 | tf_op jit(solution)/shard_map/ppermute | solution.py:516
  96.3 1.4 %collective-permute-start.16 = (f32[256,128]{1,0:T(8,128)S(1)}, f32[256,128]{1,0:T(8,128)S(1)}, u32[]{:S(2)}, u32[]{:S(2)}) collective-permute-start(f32[256,128]{1,0:T(8,128)S(1)} %get-tuple-element.81), channel_id=1, source_target_pairs={{0,1},{1,0},{2,3},{3,2},{4,5},{5,4},{6,7},{7,6},{8,9},{9,8},{10,11... | collective-permute-start | bytes 393224 | tf_op jit(solution)/shard_map/ppermute | solution.py:516

commit v6 on v5

--- a/solution.py
+++ b/solution.py
@@ -12,7 +12,7 @@
 PIECE = 128
 SEED = 16
 BATCH = 2
-ROWS = 256
+ROWS = 512
 TILE = 512
 GROUPS = 2
 FAR = -1e30

time: 103 us -> 102 us (level)
  transfers between devices with their start and end apart: 18 -> 18, of which waited for: 12 -> 13; matrix products, arithmetic and copies ran while one was open for 1% -> 1% of each run, Pallas kernels for 34% -> 34%
where the time goes in v6:
time: 102 us
  waiting for transfers between devices  40.8 us (40%)
  Pallas kernels  39.3 us (39%)
  starting transfers between devices  18 us (18%)
  local copies, waits for them, and re-layouts  2.24 us (2%)
  other arithmetic  1.39 us (1%)
    ppermute x13, waiting for transfers between devices, exchanged(): lax.ppermute(value, axis, [(i, i ^ bit) for i in range(lax.axis_size(axis...  23.3 us
    ppermute x5, waiting for transfers between devices, onward(): lax.ppermute(value, 'ctx', [(i, (i + steps) % count) for i in range(count)])  17.6 us
    ppermute x13, starting transfers between devices, exchanged(): lax.ppermute(value, axis, [(i, i ^ bit) for i in range(lax.axis_size(axis...  13.8 us
    pallas_call x1, Pallas kernels, prepare(): pl.pallas_call(functools.partial(prepare_kernel, scale=scale), grid=(head...  12.9 us
    pallas_call x2, Pallas kernels, early_part(): pl.pallas_call(functools.partial(early_kernel, scale=scale), grid_spec=pl...  5.95 us
    pallas_call x2, Pallas kernels, own_part(): pl.pallas_call(functools.partial(own_kernel, scale=scale), grid_spec=pltp...  5.58 us
    pallas_call x3, Pallas kernels, late_part(): pl.pallas_call(functools.partial(late_kernel, scale=scale), grid_spec=plt...  5.41 us
    pallas_call x1, Pallas kernels, project(): pl.pallas_call(project_kernel, grid=(tiles,), in_specs=a_spec + [w_spec]...  4.76 us
  transfers between devices with their start and end apart: 18, of which 13 were waited for; matrix products, arithmetic and copies ran while one was open for 1% of the time, Pallas kernels for 34%

profile of v6, /device:TPU:0, one launch (start us, length us, event | category | flops | bytes accessed | tf_op | source)
XLA Modules:
  0.0 102.0 jit_solution(5586085098377440117)
XLA Ops:
  0.0 0.5 collective-permute-start.1
  0.5 1.1 %slice.12 = f32[256,512]{1,0:T(8,128)S(1)} slice(f32[512,512]{1,0:T(8,128)} %vo_ref.3), slice={[0:256], [0:512]} | slice | bytes 1048576 | tf_op jit(solution)/shard_map/slice | solution.py:534
  1.5 0.0 copy-start
  1.5 2.6 %collective-permute-start = (f32[256,512]{1,0:T(8,128)S(1)}, f32[256,512]{1,0:T(8,128)S(1)}, u32[]{:S(2)}, u32[]{:S(2)}) collective-permute-start(f32[256,512]{1,0:T(8,128)S(1)} %slice.12), channel_id=1, source_target_pairs={{0,8},{2,10},{4,12},{6,14},{8,16},{10,18},{12,20},{14,22},{16,24},... | collective-permute-start | bytes 1572872 | tf_op jit(solution)/shard_map/ppermute | solution.py:512
  4.2 12.9 %prepare.1 = (f32[4,520,128]{2,1,0:T(8,128)}, f32[4,520,128]{2,1,0:T(8,128)}, f32[4,128,128]{2,1,0:T(8,128)}, f32[4,512,128]{2,1,0:T(8,128)}, f32[4,512,128]{2,1,0:T(8,128)}) custom-call(f32[512,512]{1,0:T(8,128)} %q_ref.1, f32[512,512]{1,0:T(8,128)} %k_ref.1, f32[512,512]{1,0:T(8,128)} %vo_ref.3, f32[512,512]{1,0:T(8,128)} %w_ref.1, f32[4,512]{1,0:T(4,128)} %beta_ref.1, ...), custom_call_target="tpu_custom_call" | custom-call | flops 14949999616 | bytes 1000 | tf_op jit(solution)/shard_map/prepare/pallas_call | solution.py:221
  17.1 0.0 copy-start.1
  17.1 1.7 %collective-permute-done.v2a_ref = f32[256,512]{1,0:T(8,128)S(1)} collective-permute-done((f32[256,512]{1,0:T(8,128)S(1)}, f32[256,512]{1,0:T(8,128)S(1)}, u32[]{:S(2)}, u32[]{:S(2)}) %collective-permute-start) | collective-permute-done | bytes 524320 | tf_op jit(solution)/shard_map/ppermute | solution.py:512
  18.8 0.0 collective-permute-done.1.other_ref
  18.8 1.2 %broadcast_select_fusion.2 = (f32[256,512]{1,0:T(8,128)}, f32[256,512]{1,0:T(8,128)}) fusion(f32[256,512]{1,0:T(8,128)S(1)} %collective-permute-done.v2a_ref, pred[]{:T(512)S(6)} %ge.3, f32[512,512]{1,0:T(8,128)S(1)} %copy-done), kind=kLoop, calls=%fused_computation.2 | loop fusion | flops 131072 | bytes 2621441 | tf_op jit(solution)/shard_map/jit(_where)/select_n | solution.py:537
  20.0 0.0 collective-permute-start.2
  20.0 0.0 copy-done.7
  20.0 1.5 %collective-permute-start.7 = (f32[4,128,128]{2,1,0:T(8,128)S(1)}, f32[4,128,128]{2,1,0:T(8,128)S(1)}, u32[]{:S(2)}, u32[]{:S(2)}) collective-permute-start(f32[4,128,128]{2,1,0:T(8,128)S(1)} %copy-done.7), channel_id=1, source_target_pairs={{0,2},{2,0},{4,6},{6,4},{8,10},{10,8},{12,14},{14,12},{16,18},{18,... | collective-permute-start | bytes 786440 | tf_op jit(solution)/shard_map/ppermute | solution.py:516
  21.5 1.5 %collective-permute-start.4 = (f32[256,512]{1,0:T(8,128)}, f32[256,512]{1,0:T(8,128)S(1)}, u32[]{:S(2)}, u32[]{:S(2)}) collective-permute-start(f32[256,512]{1,0:T(8,128)} %get-tuple-element.85), channel_id=1, source_target_pairs={{0,4},{2,6},{4,0},{6,2},{8,12},{10,14},{12,8},{14,10},{16,20},{18,... | collective-permute-start | bytes 1572872 | tf_op jit(solution)/shard_map/ppermute | solution.py:516
  23.0 0.0 copy-done.1
  23.0 0.1 fusion
  23.1 5.1 %collective-permute-done.7.near_ref.s_ref = f32[4,128,128]{2,1,0:T(8,128)S(1)} collective-permute-done((f32[4,128,128]{2,1,0:T(8,128)S(1)}, f32[4,128,128]{2,1,0:T(8,128)S(1)}, u32[]{:S(2)}, u32[]{:S(2)}) %collective-permute-start.7) | collective-permute-done | bytes 262176 | tf_op jit(solution)/shard_map/ppermute | solution.py:516
  28.2 0.3 joined_steps.1
  28.4 1.5 %collective-permute-start.8 = (f32[4,128,128]{2,1,0:T(8,128)S(1)}, f32[4,128,128]{2,1,0:T(8,128)S(1)}, u32[]{:S(2)}, u32[]{:S(2)}) collective-permute-start(f32[4,128,128]{2,1,0:T(8,128)S(1)} %joined_steps.1), channel_id=1, source_target_pairs={{0,4},{2,6},{4,8},{6,10},{8,12},{10,14},{12,16},{14,18},{16,20},{1... | collective-permute-start | bytes 786440 | tf_op jit(solution)/shard_map/ppermute | solution.py:512
  29.9 1.5 %collective-permute-start.9 = (f32[4,520,128]{2,1,0:T(8,128)S(1)}, f32[4,520,128]{2,1,0:T(8,128)S(1)}, u32[]{:S(2)}, u32[]{:S(2)}) collective-permute-start(f32[4,520,128]{2,1,0:T(8,128)S(1)} %copy-done.3), channel_id=1, source_target_pairs={{0,2},{2,0},{4,6},{6,4},{8,10},{10,8},{12,14},{14,12},{16,18},{18,... | collective-permute-start | bytes 3194888 | tf_op jit(solution)/shard_map/ppermute | solution.py:516
  31.4 4.3 %collective-permute-done.2.v2b_ref = f32[256,512]{1,0:T(8,128)S(1)} collective-permute-done((f32[256,512]{1,0:T(8,128)}, f32[256,512]{1,0:T(8,128)S(1)}, u32[]{:S(2)}, u32[]{:S(2)}) %collective-permute-start.2) | collective-permute-done | bytes 524320 | tf_op jit(solution)/shard_map/ppermute | solution.py:512
  35.8 0.1 broadcast_select_fusion.3
  35.9 2.6 %collective-permute-start.5 = (f32[256,512]{1,0:T(8,128)S(1)}, f32[256,512]{1,0:T(8,128)S(1)}, u32[]{:S(2)}, u32[]{:S(2)}) collective-permute-start(f32[256,512]{1,0:T(8,128)S(1)} %broadcast_select_fusion.3), channel_id=1, source_target_pairs={{0,4},{2,6},{4,0},{6,2},{8,12},{10,14},{12,8},{14,10},{16,20},{18,... | collective-permute-start | bytes 1572872 | tf_op jit(solution)/shard_map/ppermute | solution.py:516
  38.5 0.0 collective-permute-start.3
  38.5 4.9 %collective-permute-done.8.u_ref = f32[4,128,128]{2,1,0:T(8,128)S(1)} collective-permute-done((f32[4,128,128]{2,1,0:T(8,128)S(1)}, f32[4,128,128]{2,1,0:T(8,128)S(1)}, u32[]{:S(2)}, u32[]{:S(2)}) %collective-permute-start.8) | collective-permute-done | bytes 262176 | tf_op jit(solution)/shard_map/ppermute | solution.py:512
  43.4 0.0 collective-permute-start.11
  43.4 0.0 copy-done.2
  43.5 3.6 %weight_halves.1 = (bf16[4,512,512]{2,1,0:T(8,128)(2,1)S(1)}, bf16[4,512,512]{2,1,0:T(8,128)(2,1)S(1)}, bf16[4,512,512]{2,1,0:T(8,128)(2,1)S(1)}, bf16[4,512,512]{2,1,0:T(8,128)(2,1)S(1)}) custom-call(f32[512,2048]{1,0:T(8,128)S(1)} %copy-done.2, f32[512,2048]{1,0:T(8,128)} %collective-permute-done.1.other_ref), custom_call_target="tpu_custom_call" | custom-call | flops 8049999872 | bytes 1000 | tf_op jit(solution)/shard_map/weight_halves/pallas_call | solution.py:468
  47.1 0.0 copy-start.10
  47.1 0.0 collective-permute-done.4.v1a_ref
  47.1 6.2 %collective-permute-done.5.v1b_ref = f32[256,512]{1,0:T(8,128)S(1)} collective-permute-done((f32[256,512]{1,0:T(8,128)S(1)}, f32[256,512]{1,0:T(8,128)S(1)}, u32[]{:S(2)}, u32[]{:S(2)}) %collective-permute-start.5) | collective-permute-done | bytes 524320 | tf_op jit(solution)/shard_map/ppermute | solution.py:516
  53.3 2.0 %collective-permute-done.3.k2_ref = f32[2,520,128]{2,1,0:T(8,128)S(1)} collective-permute-done((f32[2,520,128]{2,1,0:T(8,128)S(1)}, f32[2,520,128]{2,1,0:T(8,128)S(1)}, u32[]{:S(2)}, u32[]{:S(2)}) %collective-permute-start.3) | collective-permute-done | bytes 532512 | tf_op jit(solution)/shard_map/ppermute | solution.py:512
  55.3 0.1 broadcast_select_fusion.1
  55.4 0.2 collective-permute-start.6
  55.5 0.0 collective-permute-done.9.qp_ref
  55.5 3.0 %early.2 = (f32[2,512,128]{2,1,0:T(8,128)S(1)}, f32[2,512,128]{2,1,0:T(8,128)S(1)}) custom-call(s32[1]{0:T(128)} %bitcast.1.place_ref, f32[4,520,128]{2,1,0:T(8,128)S(1)} %collective-permute-done.9.qp_ref, f32[4,520,128]{2,1,0:T(8,128)S(1)} %copy-done.1, f32[512,512]{1,0:T(8,128)S(1)} %copy-done, f32[2,520,128]{2,1,0:T(8,128)S(1)} %collective-permute-done.3.k2_ref, ...), custom_call_target="tpu_custom_call" | custom-call | flops 5175000064 | bytes 1000 | tf_op jit(solution)/shard_map/early/pallas_call | solution.py:362
  58.5 4.6 %collective-permute-done.11.k2_ref = f32[2,520,128]{2,1,0:T(8,128)S(1)} collective-permute-done((f32[2,520,128]{2,1,0:T(8,128)S(1)}, f32[2,520,128]{2,1,0:T(8,128)S(1)}, u32[]{:S(2)}, u32[]{:S(2)}) %collective-permute-start.11) | collective-permute-done | bytes 532512 | tf_op jit(solution)/shard_map/ppermute | solution.py:512
  63.2 0.1 broadcast_select_fusion
  63.2 2.5 %collective-permute-start.12 = (f32[2,520,128]{2,1,0:T(8,128)S(1)}, f32[2,520,128]{2,1,0:T(8,128)S(1)}, u32[]{:S(2)}, u32[]{:S(2)}) collective-permute-start(f32[2,520,128]{2,1,0:T(8,128)S(1)} %broadcast_select_fusion), channel_id=1, source_target_pairs={{0,4},{2,6},{4,0},{6,2},{8,12},{10,14},{12,8},{14,10},{16,20},{18,... | collective-permute-start | bytes 1597448 | tf_op jit(solution)/shard_map/ppermute | solution.py:516
  65.8 3.0 %early.3 = (f32[2,512,128]{2,1,0:T(8,128)S(1)}, f32[2,512,128]{2,1,0:T(8,128)S(1)}) custom-call(s32[1]{0:T(128)} %bitcast.1.place_ref, f32[4,520,128]{2,1,0:T(8,128)S(1)} %collective-permute-done.9.qp_ref, f32[4,520,128]{2,1,0:T(8,128)S(1)} %copy-done.1, f32[512,512]{1,0:T(8,128)S(1)} %copy-done, f32[2,520,128]{2,1,0:T(8,128)S(1)} %collective-permute-done.11.k2_ref, ...), custom_call_target="tpu_custom_call" | custom-call | flops 5175000064 | bytes 1000 | tf_op jit(solution)/shard_map/early/pallas_call | solution.py:362
  68.8 0.5 collective-permute-done.6.k1_ref
  69.2 2.8 %late.3 = f32[2,520,128]{2,1,0:T(8,128)S(1)} custom-call(s32[1]{0:T(128)} %bitcast.1.place_ref, f32[4,520,128]{2,1,0:T(8,128)S(1)} %collective-permute-done.9.qp_ref, f32[2,520,128]{2,1,0:T(8,128)S(1)} %collective-permute-done.6.k1_ref, f32[256,512]{1,0:T(8,128)S(1)} %collective-permute-done.4.v1a_ref, f32[256,512]{1,0:T(8,128)S(1)} %collective-permute-done.5.v1b_ref, ...), custom_call_target="tpu_custom_call" | custom-call | flops 4600000000 | bytes 1000 | tf_op jit(solution)/shard_map/late/pallas_call | solution.py:382
  72.0 1.1 %collective-permute-start.10 = (f32[2,520,128]{2,1,0:T(8,128)S(1)}, f32[2,520,128]{2,1,0:T(8,128)S(1)}, u32[]{:S(2)}, u32[]{:S(2)}) collective-permute-start(f32[2,520,128]{2,1,0:T(8,128)S(1)} %late.3), channel_id=1, source_target_pairs={{0,2},{2,0},{4,6},{6,4},{8,10},{10,8},{12,14},{14,12},{16,18},{18,... | collective-permute-start | bytes 1597448 | tf_op jit(solution)/shard_map/ppermute | solution.py:516
  73.1 1.0 %copy-done.5 = f32[256,512]{1,0:T(8,128)S(1)} copy-done((f32[256,512]{1,0:T(8,128)S(1)}, f32[256,512]{1,0:T(8,128)}, u32[]{:S(2)}) %copy-start.5) | copy-done | bytes 524312
  74.2 2.8 %own.2 = (f32[2,512,128]{2,1,0:T(8,128)S(1)}, f32[2,512,128]{2,1,0:T(8,128)S(1)}) custom-call(s32[1]{0:T(128)} %bitcast.1.place_ref, f32[4,520,128]{2,1,0:T(8,128)S(1)} %copy-done.3, f32[2,520,128]{2,1,0:T(8,128)S(1)} %collective-permute-done.6.k1_ref, f32[256,512]{1,0:T(8,128)S(1)} %copy-done.5, f32[256,512]{1,0:T(8,128)S(1)} %collective-permute-done.5.v1b_ref, ...), custom_call_target="tpu_custom_call" | custom-call | flops 5175000064 | bytes 1000 | tf_op jit(solution)/shard_map/own/pallas_call | solution.py:403
  77.0 1.8 %collective-permute-done.12.k1_ref = f32[2,520,128]{2,1,0:T(8,128)S(1)} collective-permute-done((f32[2,520,128]{2,1,0:T(8,128)S(1)}, f32[2,520,128]{2,1,0:T(8,128)S(1)}, u32[]{:S(2)}, u32[]{:S(2)}) %collective-permute-start.12) | collective-permute-done | bytes 532512 | tf_op jit(solution)/shard_map/ppermute | solution.py:516
  78.8 1.3 %late.5 = f32[1,520,128]{2,1,0:T(8,128)S(1)} custom-call(s32[1]{0:T(128)} %bitcast.1.place_ref, f32[4,520,128]{2,1,0:T(8,128)S(1)} %collective-permute-done.9.qp_ref, f32[2,520,128]{2,1,0:T(8,128)S(1)} %collective-permute-done.12.k1_ref, f32[256,512]{1,0:T(8,128)S(1)} %copy-done.6, f32[256,512]{1,0:T(8,128)S(1)} %collective-permute-done.5.v1b_ref, ...), custom_call_target="tpu_custom_call" | custom-call | flops 2300000000 | bytes 1000 | tf_op jit(solution)/shard_map/late/pallas_call | solution.py:382
  80.1 1.3 %collective-permute-start.14 = (f32[1,520,128]{2,1,0:T(8,128)S(1)}, f32[1,520,128]{2,1,0:T(8,128)S(1)}, u32[]{:S(2)}, u32[]{:S(2)}) collective-permute-start(f32[1,520,128]{2,1,0:T(8,128)S(1)} %late.5), channel_id=1, source_target_pairs={{0,2},{2,0},{4,6},{6,4},{8,10},{10,8},{12,14},{14,12},{16,18},{18,... | collective-permute-start | bytes 798728 | tf_op jit(solution)/shard_map/ppermute | solution.py:516
  81.4 1.3 %late.4 = f32[1,520,128]{2,1,0:T(8,128)S(1)} custom-call(s32[1]{0:T(128)} %bitcast.1.place_ref, f32[4,520,128]{2,1,0:T(8,128)S(1)} %collective-permute-done.9.qp_ref, f32[2,520,128]{2,1,0:T(8,128)S(1)} %collective-permute-done.12.k1_ref, f32[256,512]{1,0:T(8,128)S(1)} %copy-done.6, f32[256,512]{1,0:T(8,128)S(1)} %collective-permute-done.5.v1b_ref, ...), custom_call_target="tpu_custom_call" | custom-call | flops 2300000000 | bytes 1000 | tf_op jit(solution)/shard_map/late/pallas_call | solution.py:382
  82.8 0.9 collective-permute-start.13
  83.6 2.8 %own.3 = (f32[2,512,128]{2,1,0:T(8,128)S(1)}, f32[2,512,128]{2,1,0:T(8,128)S(1)}) custom-call(s32[1]{0:T(128)} %bitcast.1.place_ref, f32[4,520,128]{2,1,0:T(8,128)S(1)} %copy-done.3, f32[2,520,128]{2,1,0:T(8,128)S(1)} %collective-permute-done.12.k1_ref, f32[256,512]{1,0:T(8,128)S(1)} %copy-done.6, f32[256,512]{1,0:T(8,128)S(1)} %collective-permute-done.5.v1b_ref, ...), custom_call_target="tpu_custom_call" | custom-call | flops 5175000064 | bytes 1000 | tf_op jit(solution)/shard_map/own/pallas_call | solution.py:403
  86.4 0.7 collective-permute-done.10.msg_ref
  87.1 0.5 merge.3
  87.6 0.1 collective-permute-start.15
  87.6 5.2 %collective-permute-done.14.msg_ref = f32[1,520,128]{2,1,0:T(8,128)S(1)} collective-permute-done((f32[1,520,128]{2,1,0:T(8,128)S(1)}, f32[1,520,128]{2,1,0:T(8,128)S(1)}, u32[]{:S(2)}, u32[]{:S(2)}) %collective-permute-start.14) | collective-permute-done | bytes 266272 | tf_op jit(solution)/shard_map/ppermute | solution.py:516
  92.8 0.2 merge.5
  93.0 0.0 copy-start.11
  93.0 0.1 collective-permute-start.17
  93.1 2.6 %collective-permute-done.13.msg_ref = f32[1,520,128]{2,1,0:T(8,128)S(1)} collective-permute-done((f32[1,520,128]{2,1,0:T(8,128)S(1)}, f32[1,520,128]{2,1,0:T(8,128)S(1)}, u32[]{:S(2)}, u32[]{:S(2)}) %collective-permute-start.13) | collective-permute-done | bytes 266272 | tf_op jit(solution)/shard_map/ppermute | solution.py:516
  95.7 0.2 merge.4
  95.9 0.1 collective-permute-start.16
  95.9 0.0 collective-permute-done.17.refs_5_
  95.9 1.3 %collective-permute-done.16.refs_4_ = f32[256,128]{1,0:T(8,128)S(1)} collective-permute-done((f32[256,128]{1,0:T(8,128)S(1)}, f32[256,128]{1,0:T(8,128)S(1)}, u32[]{:S(2)}, u32[]{:S(2)}) %collective-permute-start.16) | collective-permute-done | bytes 131104 | tf_op jit(solution)/shard_map/ppermute | solution.py:516
  97.3 0.0 collective-permute-done.15.refs_3_
  97.3 4.8 %project.1 = f32[256,2048]{1,0:T(8,128)} custom-call(f32[256,256]{1,0:T(8,128)S(1)} %get-tuple-element.70.refs_0_, f32[256,128]{1,0:T(8,128)S(1)} %get-tuple-element.78.refs_1_, f32[256,128]{1,0:T(8,128)S(1)} %get-tuple-element.79.refs_2_, f32[256,256]{1,0:T(8,128)S(1)} %collective-permute-done.15.refs_3_, f32[256,128]{1,0:T(8,128)S(1)} %collective-permute-done.16.refs_4_, ...), custom_call_target="tpu_custom_call" | custom-call | flops 8625000448 | bytes 1000 | tf_op jit(solution)/shard_map/project/pallas_call | solution.py:498
  (20 shorter events, 0.0 us)
Async XLA Ops:
  0.0 18.8 %collective-permute-start.1 = (f32[512,2048]{1,0:T(8,128)}, f32[512,2048]{1,0:T(8,128)}, u32[]{:S(2)}, u32[]{:S(2)}) collective-permute-start(f32[512,2048]{1,0:T(8,128)} %own_ref.1), channel_id=1, source_target_pairs={{0,1},{1,0},{2,3},{3,2},{4,5},{5,4},{6,7},{7,6},{8,9},{9,8},{10,11... | collective-permute-start | bytes 12582920 | tf_op jit(solution)/shard_map/ppermute | solution.py:516
  1.5 17.3 %copy-start = (f32[512,512]{1,0:T(8,128)S(1)}, f32[512,512]{1,0:T(8,128)}, u32[]{:S(2)}) copy-start(f32[512,512]{1,0:T(8,128)} %vo_ref.3) | copy-start | bytes 3145732
  1.5 17.2 %collective-permute-start = (f32[256,512]{1,0:T(8,128)S(1)}, f32[256,512]{1,0:T(8,128)S(1)}, u32[]{:S(2)}, u32[]{:S(2)}) collective-permute-start(f32[256,512]{1,0:T(8,128)S(1)} %slice.12), channel_id=1, source_target_pairs={{0,8},{2,10},{4,12},{6,14},{8,16},{10,18},{12,20},{14,22},{16,24},... | collective-permute-start | bytes 1572872 | tf_op jit(solution)/shard_map/ppermute | solution.py:512
  17.1 2.9 %copy-start.7 = (f32[4,128,128]{2,1,0:T(8,128)S(1)}, f32[4,128,128]{2,1,0:T(8,128)}, u32[]{:S(2)}) copy-start(f32[4,128,128]{2,1,0:T(8,128)} %get-tuple-element.51.own_ref.s_ref) | copy-start | bytes 786436
  17.1 5.9 %copy-start.1 = (f32[4,520,128]{2,1,0:T(8,128)S(1)}, f32[4,520,128]{2,1,0:T(8,128)}, u32[]{:S(2)}) copy-start(f32[4,520,128]{2,1,0:T(8,128)} %get-tuple-element.50.ko_ref) | copy-start | bytes 3194884
  20.0 15.8 %collective-permute-start.2 = (f32[256,512]{1,0:T(8,128)}, f32[256,512]{1,0:T(8,128)S(1)}, u32[]{:S(2)}, u32[]{:S(2)}) collective-permute-start(f32[256,512]{1,0:T(8,128)} %get-tuple-element.52), channel_id=1, source_target_pairs={{0,8},{2,10},{4,12},{6,14},{8,16},{10,18},{12,20},{14,22},{16,24},... | collective-permute-start | bytes 1572872 | tf_op jit(solution)/shard_map/ppermute | solution.py:512
  20.0 8.1 %collective-permute-start.7 = (f32[4,128,128]{2,1,0:T(8,128)S(1)}, f32[4,128,128]{2,1,0:T(8,128)S(1)}, u32[]{:S(2)}, u32[]{:S(2)}) collective-permute-start(f32[4,128,128]{2,1,0:T(8,128)S(1)} %copy-done.7), channel_id=1, source_target_pairs={{0,2},{2,0},{4,6},{6,4},{8,10},{10,8},{12,14},{14,12},{16,18},{18,... | collective-permute-start | bytes 786440 | tf_op jit(solution)/shard_map/ppermute | solution.py:516
  21.5 25.6 %collective-permute-start.4 = (f32[256,512]{1,0:T(8,128)}, f32[256,512]{1,0:T(8,128)S(1)}, u32[]{:S(2)}, u32[]{:S(2)}) collective-permute-start(f32[256,512]{1,0:T(8,128)} %get-tuple-element.85), channel_id=1, source_target_pairs={{0,4},{2,6},{4,0},{6,2},{8,12},{10,14},{12,8},{14,10},{16,20},{18,... | collective-permute-start | bytes 1572872 | tf_op jit(solution)/shard_map/ppermute | solution.py:516
  28.1 1.8 %copy-start.3 = (f32[4,520,128]{2,1,0:T(8,128)S(1)}, f32[4,520,128]{2,1,0:T(8,128)}, u32[]{:S(2)}) copy-start(f32[4,520,128]{2,1,0:T(8,128)} %get-tuple-element.60.qo_ref) | copy-start | bytes 3194884
  28.1 15.3 %copy-start.2 = (f32[512,2048]{1,0:T(8,128)S(1)}, f32[512,2048]{1,0:T(8,128)}, u32[]{:S(2)}) copy-start(f32[512,2048]{1,0:T(8,128)} %own_ref.1) | copy-start | bytes 12582916
  28.4 15.0 %collective-permute-start.8 = (f32[4,128,128]{2,1,0:T(8,128)S(1)}, f32[4,128,128]{2,1,0:T(8,128)S(1)}, u32[]{:S(2)}, u32[]{:S(2)}) collective-permute-start(f32[4,128,128]{2,1,0:T(8,128)S(1)} %joined_steps.1), channel_id=1, source_target_pairs={{0,4},{2,6},{4,8},{6,10},{8,12},{10,14},{12,16},{14,18},{16,20},{1... | collective-permute-start | bytes 786440 | tf_op jit(solution)/shard_map/ppermute | solution.py:512
  29.9 25.6 %collective-permute-start.9 = (f32[4,520,128]{2,1,0:T(8,128)S(1)}, f32[4,520,128]{2,1,0:T(8,128)S(1)}, u32[]{:S(2)}, u32[]{:S(2)}) collective-permute-start(f32[4,520,128]{2,1,0:T(8,128)S(1)} %copy-done.3), channel_id=1, source_target_pairs={{0,2},{2,0},{4,6},{6,4},{8,10},{10,8},{12,14},{14,12},{16,18},{18,... | collective-permute-start | bytes 3194888 | tf_op jit(solution)/shard_map/ppermute | solution.py:516
  35.9 17.5 %collective-permute-start.5 = (f32[256,512]{1,0:T(8,128)S(1)}, f32[256,512]{1,0:T(8,128)S(1)}, u32[]{:S(2)}, u32[]{:S(2)}) collective-permute-start(f32[256,512]{1,0:T(8,128)S(1)} %broadcast_select_fusion.3), channel_id=1, source_target_pairs={{0,4},{2,6},{4,0},{6,2},{8,12},{10,14},{12,8},{14,10},{16,20},{18,... | collective-permute-start | bytes 1572872 | tf_op jit(solution)/shard_map/ppermute | solution.py:516
  38.5 16.8 %collective-permute-start.3 = (f32[2,520,128]{2,1,0:T(8,128)S(1)}, f32[2,520,128]{2,1,0:T(8,128)S(1)}, u32[]{:S(2)}, u32[]{:S(2)}) collective-permute-start(f32[2,520,128]{2,1,0:T(8,128)S(1)} %get-tuple-element.55), channel_id=1, source_target_pairs={{0,8},{2,10},{4,12},{6,14},{8,16},{10,18},{12,20},{14,22},{16,24},... | collective-permute-start | bytes 1597448 | tf_op jit(solution)/shard_map/ppermute | solution.py:512
  43.4 19.7 %collective-permute-start.11 = (f32[2,520,128]{2,1,0:T(8,128)S(1)}, f32[2,520,128]{2,1,0:T(8,128)S(1)}, u32[]{:S(2)}, u32[]{:S(2)}) collective-permute-start(f32[2,520,128]{2,1,0:T(8,128)S(1)} %get-tuple-element.72), channel_id=1, source_target_pairs={{0,8},{2,10},{4,12},{6,14},{8,16},{10,18},{12,20},{14,22},{16,24},... | collective-permute-start | bytes 1597448 | tf_op jit(solution)/shard_map/ppermute | solution.py:512
  47.1 11.4 %copy-start.10 = (bf16[4,512,512]{2,1,0:T(8,128)(2,1)}, bf16[4,512,512]{2,1,0:T(8,128)(2,1)S(1)}, u32[]{:S(2)}) copy-start(bf16[4,512,512]{2,1,0:T(8,128)(2,1)S(1)} %get-tuple-element.63.refs_6_) | copy-start | bytes 6291460
  47.1 11.4 %copy-start.12 = (bf16[4,512,512]{2,1,0:T(8,128)(2,1)}, bf16[4,512,512]{2,1,0:T(8,128)(2,1)S(1)}, u32[]{:S(2)}) copy-start(bf16[4,512,512]{2,1,0:T(8,128)(2,1)S(1)} %get-tuple-element.64.refs_7_) | copy-start | bytes 6291460
  47.1 22.1 %copy-start.4 = (f32[256,512]{1,0:T(8,128)}, f32[256,512]{1,0:T(8,128)S(1)}, u32[]{:S(2)}) copy-start(f32[256,512]{1,0:T(8,128)S(1)} %collective-permute-done.4.v1a_ref) | copy-start | bytes 1572868
  55.4 13.8 %collective-permute-start.6 = (f32[2,520,128]{2,1,0:T(8,128)S(1)}, f32[2,520,128]{2,1,0:T(8,128)S(1)}, u32[]{:S(2)}, u32[]{:S(2)}) collective-permute-start(f32[2,520,128]{2,1,0:T(8,128)S(1)} %broadcast_select_fusion.1), channel_id=1, source_target_pairs={{0,4},{2,6},{4,0},{6,2},{8,12},{10,14},{12,8},{14,10},{16,20},{18,... | collective-permute-start | bytes 1597448 | tf_op jit(solution)/shard_map/ppermute | solution.py:516
  63.2 15.6 %collective-permute-start.12 = (f32[2,520,128]{2,1,0:T(8,128)S(1)}, f32[2,520,128]{2,1,0:T(8,128)S(1)}, u32[]{:S(2)}, u32[]{:S(2)}) collective-permute-start(f32[2,520,128]{2,1,0:T(8,128)S(1)} %broadcast_select_fusion), channel_id=1, source_target_pairs={{0,4},{2,6},{4,0},{6,2},{8,12},{10,14},{12,8},{14,10},{16,20},{18,... | collective-permute-start | bytes 1597448 | tf_op jit(solution)/shard_map/ppermute | solution.py:516
  69.2 3.9 %copy-start.8 = (f32[4,512,128]{2,1,0:T(8,128)S(1)}, f32[4,512,128]{2,1,0:T(8,128)}, u32[]{:S(2)}) copy-start(f32[4,512,128]{2,1,0:T(8,128)} %get-tuple-element.56.od_ref) | copy-start | bytes 3145732
  69.2 3.9 %copy-start.9 = (f32[4,512,128]{2,1,0:T(8,128)S(1)}, f32[4,512,128]{2,1,0:T(8,128)}, u32[]{:S(2)}) copy-start(f32[4,512,128]{2,1,0:T(8,128)} %get-tuple-element.57.ld_ref) | copy-start | bytes 3145732
  72.0 15.1 %collective-permute-start.10 = (f32[2,520,128]{2,1,0:T(8,128)S(1)}, f32[2,520,128]{2,1,0:T(8,128)S(1)}, u32[]{:S(2)}, u32[]{:S(2)}) collective-permute-start(f32[2,520,128]{2,1,0:T(8,128)S(1)} %late.3), channel_id=1, source_target_pairs={{0,2},{2,0},{4,6},{6,4},{8,10},{10,8},{12,14},{14,12},{16,18},{18,... | collective-permute-start | bytes 1597448 | tf_op jit(solution)/shard_map/ppermute | solution.py:516
  73.1 1.0 %copy-start.5 = (f32[256,512]{1,0:T(8,128)S(1)}, f32[256,512]{1,0:T(8,128)}, u32[]{:S(2)}) copy-start(f32[256,512]{1,0:T(8,128)} %copy-done.4) | copy-start | bytes 1572868
  74.2 4.6 %copy-start.6 = (f32[256,512]{1,0:T(8,128)S(1)}, f32[256,512]{1,0:T(8,128)}, u32[]{:S(2)}) copy-start(f32[256,512]{1,0:T(8,128)} %copy-done.4) | copy-start | bytes 1572868
  80.1 12.7 %collective-permute-start.14 = (f32[1,520,128]{2,1,0:T(8,128)S(1)}, f32[1,520,128]{2,1,0:T(8,128)S(1)}, u32[]{:S(2)}, u32[]{:S(2)}) collective-permute-start(f32[1,520,128]{2,1,0:T(8,128)S(1)} %late.5), channel_id=1, source_target_pairs={{0,2},{2,0},{4,6},{6,4},{8,10},{10,8},{12,14},{14,12},{16,18},{18,... | collective-permute-start | bytes 798728 | tf_op jit(solution)/shard_map/ppermute | solution.py:516
  82.8 12.9 %collective-permute-start.13 = (f32[1,520,128]{2,1,0:T(8,128)S(1)}, f32[1,520,128]{2,1,0:T(8,128)S(1)}, u32[]{:S(2)}, u32[]{:S(2)}) collective-permute-start(f32[1,520,128]{2,1,0:T(8,128)S(1)} %late.4), channel_id=1, source_target_pairs={{0,2},{2,0},{4,6},{6,4},{8,10},{10,8},{12,14},{14,12},{16,18},{18,... | collective-permute-start | bytes 798728 | tf_op jit(solution)/shard_map/ppermute | solution.py:516
  87.6 9.7 %collective-permute-start.15 = (f32[256,256]{1,0:T(8,128)S(1)}, f32[256,256]{1,0:T(8,128)S(1)}, u32[]{:S(2)}, u32[]{:S(2)}) collective-permute-start(f32[256,256]{1,0:T(8,128)S(1)} %get-tuple-element.80), channel_id=1, source_target_pairs={{0,1},{1,0},{2,3},{3,2},{4,5},{5,4},{6,7},{7,6},{8,9},{9,8},{10,11... | collective-permute-start | bytes 786440 | tf_op jit(solution)/shard_map/ppermute | solution.py:516
  93.0 4.3 %copy-start.11 = (bf16[4,512,512]{2,1,0:T(8,128)(2,1)S(1)}, bf16[4,512,512]{2,1,0:T(8,128)(2,1)}, u32[]{:S(2)}) copy-start(bf16[4,512,512]{2,1,0:T(8,128)(2,1)} %copy-done.10) | copy-start | bytes 6291460
  93.0 4.3 %copy-start.13 = (bf16[4,512,512]{2,1,0:T(8,128)(2,1)S(1)}, bf16[4,512,512]{2,1,0:T(8,128)(2,1)}, u32[]{:S(2)}) copy-start(bf16[4,512,512]{2,1,0:T(8,128)(2,1)} %copy-done.12) | copy-start | bytes 6291460
  93.0 2.9 %collective-permute-start.17 = (f32[256,128]{1,0:T(8,128)S(1)}, f32[256,128]{1,0:T(8,128)S(1)}, u32[]{:S(2)}, u32[]{:S(2)}) collective-permute-start(f32[256,128]{1,0:T(8,128)S(1)} %get-tuple-element.82), channel_id=1, source_target_pairs={{0,1},{1,0},{2,3},{3,2},{4,5},{5,4},{6,7},{7,6},{8,9},{9,8},{10,11... | collective-permute-start | bytes 393224 | tf_op jit(solution)/shard_map/ppermute | solution.py:516
  95.9 1.4 %collective-permute-start.16 = (f32[256,128]{1,0:T(8,128)S(1)}, f32[256,128]{1,0:T(8,128)S(1)}, u32[]{:S(2)}, u32[]{:S(2)}) collective-permute-start(f32[256,128]{1,0:T(8,128)S(1)} %get-tuple-element.81), channel_id=1, source_target_pairs={{0,1},{1,0},{2,3},{3,2},{4,5},{5,4},{6,7},{7,6},{8,9},{9,8},{10,11... | collective-permute-start | bytes 393224 | tf_op jit(solution)/shard_map/ppermute | solution.py:516
